TPU v7x, 256 devices: a whole 4x4x8 slice. The times are simulated.
256 devices in a mesh: grp: 2 (over z_hi), vocab: 32 (over y, x, core), tok: 4 (over z_lo).
Axes of the slice: x: 4, y: 4, z: 8 (z_hi: 2, z_lo: 4; z = z_hi * 4 + z_lo), core: 2. Of those that a mesh axis runs over, the one named last changes fastest.
Arguments:
- hidden: bfloat16 [2, 512, 4096], P('grp', 'tok', 'vocab'), may hold values from -24 to 24
- head_weight: bfloat16 [2, 151936, 4096], P('grp', ('vocab', 'tok')), may hold values from -0.703125 to 0.703125
- labels: int32 [512], replicated, may hold values from 0 to 151935
- loss_mask: int32 [512], replicated, may hold values 0 or 1
Outputs:
- head_input_grads: bfloat16 [512, 4096], P(('grp', 'tok'), 'vocab')
- token_loss: float32 [512], replicated
- log_norms: float32 [2, 512], replicated
All inputs are finite; a program needn't handle non-finite values.
Results may differ from a plain program's by a relative error of at most 0.0012.
The roundings to bfloat16 on the way count: a program that leaves them out, or rounds other values in their place, can miss the bound.
Values may be sent and summed in bfloat16 or wider, within the bound.
No kernel may reach another device: no remote copies, remote signals or barrier semaphores. Data moves between devices by JAX's collectives and lax.ppermute only.
A program may use at most 128 MiB of HBM per device.

v0:
```python
import jax
import jax.numpy as jnp
from jax import lax
from jax.sharding import PartitionSpec as P


def swapped(block, axis, bit):
    count = lax.axis_size(axis)
    route = []
    for low in range(count):
        high = low | 1 << bit
        if high != low and high < count:
            route += [(low, high), (high, low)]
    return lax.ppermute(block, axis, route)


def shifted(x, axis, by):
    devices = lax.axis_size(axis)
    pairs = [(i, i + by) for i in range(devices) if 0 <= i + by < devices]
    return lax.ppermute(x, axis, pairs)


def shards(hidden, head_weight, labels, loss_mask):
    weights = head_weight[0]
    vocab_dev = weights.shape[0]
    tok_dev = hidden.shape[1]
    feat_dev = hidden.shape[2]
    half_rows = tok_dev // 2
    tok_count = lax.axis_size("tok")
    voc_count = lax.axis_size("vocab")
    token_rows = lax.all_gather(hidden[0], "tok", axis=0, tiled=True)
    tokens = token_rows.shape[0]
    scores = lax.dot_general(
        weights,
        lax.all_gather(token_rows, "vocab", axis=1, tiled=True),
        (((1,), (1,)), ((), ())),
        preferred_element_type=jnp.float32,
    )
    logits = scores.astype(jnp.bfloat16)
    partner = swapped(logits, "grp", 0)
    is_teacher = lax.axis_index("grp") == 0
    own_z = lax.optimization_barrier(logits).astype(jnp.float32)
    other_z = partner.astype(jnp.float32)
    teacher_z = jnp.where(is_teacher, own_z, other_z)
    student_z = jnp.where(is_teacher, other_z, own_z)
    first_word = lax.axis_index(("vocab", "tok")) * vocab_dev
    word_ids = first_word + lax.broadcasted_iota(jnp.int32, (vocab_dev, tokens), 0)
    label_hit = word_ids == labels[None, :]
    label_part = jnp.sum(jnp.where(label_hit, student_z, 0.0), axis=0)
    teacher_peak, student_peak = lax.pmax(
        (jnp.max(teacher_z, axis=0), jnp.max(student_z, axis=0)), ("vocab", "tok")
    )
    teacher_sum, student_sum, label_logit = lax.psum(
        (
            jnp.sum(jnp.exp(teacher_z - teacher_peak), axis=0),
            jnp.sum(jnp.exp(student_z - student_peak), axis=0),
            label_part,
        ),
        ("vocab", "tok"),
    )
    teacher_norm = teacher_peak + jnp.log(teacher_sum)
    student_norm = student_peak + jnp.log(student_sum)
    teacher_logp = teacher_z - teacher_norm
    student_logp = student_z - student_norm
    teacher_prob = jnp.exp(teacher_logp)
    student_prob = jnp.exp(student_logp)
    diverge = lax.psum(
        jnp.sum(teacher_prob * (teacher_logp - student_logp), axis=0), ("vocab", "tok")
    )
    weight_mask = loss_mask.astype(jnp.float32)
    student_grad = (
        (2.0 * student_prob - teacher_prob - label_hit.astype(jnp.float32)) * weight_mask
    ).astype(jnp.bfloat16)
    partial_value = jnp.einsum(
        "kgtr,kvc->vtgrc",
        student_grad.reshape(vocab_dev, 2, tok_count, half_rows),
        weights.reshape(vocab_dev, voc_count, feat_dev),
        preferred_element_type=jnp.float32,
    )
    partial_value = partial_value.reshape(voc_count * tok_count, 2, half_rows, feat_dev)
    summed = lax.psum(partial_value, ("vocab", "tok"))
    own_block = lax.dynamic_index_in_dim(
        summed, lax.axis_index(("vocab", "tok")), 0, keepdims=False
    )
    rounded = own_block.astype(jnp.bfloat16)
    handed = shifted(rounded[0], "grp", -1)
    input_grads = jnp.where(is_teacher, handed, rounded[1])
    token_loss = weight_mask * (diverge + student_norm - label_logit)
    return (input_grads, token_loss, jnp.stack([teacher_norm, student_norm]))


def solution(mesh):
    return jax.shard_map(
        shards,
        mesh=mesh,
        in_specs=(P("grp", "tok", "vocab"), P("grp", ("vocab", "tok"), None), P(), P()),
        out_specs=(P(("grp", "tok"), "vocab"), P(), P()),
        check_vma=False,
    )
```

profile of v0, /device:TPU:2, one launch (start us, length us, event | category | flops | bytes accessed | tf_op | source)
XLA Modules:
  0.0 1656.3 jit_solution(7838321085138640431)
XLA Ops:
  7.2 0.0 all-gather.4.cloned.1.call-start
  7.2 16.5 all-gather
  23.7 0.0 all-gather.4.cloned.1.call-update
  23.7 54.9 %all-gather.4.cloned.1.call-done = bf16[1,512,4096]{2,1,0:T(8,128)(2,1)} async-done(((bf16[1,512,128]{2,1,0:T(8,128)(2,1)}), bf16[1,512,4096]{2,1,0:T(8,128)(2,1)}) %all-gather.4.cloned.1.call-update) | async-done | bytes 4194320 | tf_op jit(solution)/shard_map/all_gather | solution.py:35
  78.6 10.1 fusion.8
  88.7 5.8 collective-permute-start
  94.5 10.8 copy.16
  105.3 9.9 slice_bitcast_fusion
  115.1 32.4 %collective-permute-done = bf16[1187,512]{1,0:T(8,128)(2,1)S(1)} collective-permute-done((bf16[1187,512]{1,0:T(8,128)(2,1)S(1)}, bf16[1187,512]{1,0:T(8,128)(2,1)S(1)}, u32[]{:S(2)}, u32[]{:S(2)}) %collective-permute-start) | collective-permute-done | bytes 1215520 | tf_op jit(solution)/shard_map/ppermute | solution.py:14
  147.5 0.5 fusion.18
  148.0 316.5 %all-reduce.2 = (f32[512]{0:T(512)S(1)}, f32[512]{0:T(512)S(1)}) all-reduce(f32[512]{0:T(512)S(1)} %get-tuple-element.8, f32[512]{0:T(512)S(1)} %get-tuple-element.7), channel_id=1, replica_groups=mesh['grp'=2,'vocab'=32,'tok'=4] {'vocab','tok'}, use_global_device_ids=true, to_apply=%region_5.6 | all-reduce | flops 1024 | bytes 8192 | tf_op jit(solution)/shard_map/pmax | solution.py:50
  464.5 1.0 exponential_reduce_fusion.1
  465.5 337.3 %all-reduce.1 = (f32[512]{0:T(512)S(1)}, f32[512]{0:T(512)S(1)}) all-reduce(f32[512]{0:T(512)S(1)} %get-tuple-element.6, f32[512]{0:T(512)S(1)} %get-tuple-element.5), channel_id=1, replica_groups=mesh['grp'=2,'vocab'=32,'tok'=4] {'vocab','tok'}, use_global_device_ids=true, to_apply=%region_7.8 | all-reduce | flops 1024 | bytes 8192 | tf_op jit(solution)/shard_map/psum | solution.py:53
  802.8 3.0 multiply_reduce_fusion
  805.8 1.6 copy.9
  807.4 8.4 fusion.5
  815.8 4.1 copy.11
  819.8 818.8 %all-reduce.4 = (bf16[128,2,64,128]{3,2,1,0:T(8,128)(2,1)}, f32[512]{0:T(512)S(1)}, f32[512]{0:T(512)S(1)}) all-reduce(f32[128,2,64,128]{3,2,1,0:T(8,128)} %bitcast.34, f32[512]{0:T(512)S(1)} %get-tuple-element.4, f32[512]{0:T(512)S(1)} %get-tuple-element.3), channel_id=1, replica_groups=mesh['grp'=2,'vocab'=32,'tok'=4] {'vocab','tok'}, use_global_device_ids=true, to_apply=%region_8.9 | all-reduce | flops 2098176 | bytes 12591104 | tf_op jit(solution)/shard_map/psum | solution.py:81
  1638.6 0.8 dynamic-slice_convert_fusion
  1639.4 1.3 collective-permute-start.1
  1640.6 0.6 subtract_multiply_fusion
  1641.2 0.6 pad_maximum_fusion
  1641.8 7.1 collective-permute-done.1
  1648.9 0.6 fusion.19
  (8 shorter events, 0.0 us)
Async XLA Ops:
  7.2 71.4 %all-gather.4.cloned.1.call-start = ((), (), s32[]{:S(2)}) async-start(), calls=%async_computation | async-start | bytes 4325376 | tf_op jit(solution)/shard_map/all_gather | solution.py:35
  23.7 70.8 %copy-start = (s32[512]{0:T(512)S(1)}, s32[512]{0:T(512)}, u32[]{:S(2)}) copy-start(s32[512]{0:T(512)} %param.7) | copy-start | bytes 6148
  88.7 58.8 %collective-permute-start = (bf16[1187,512]{1,0:T(8,128)(2,1)S(1)}, bf16[1187,512]{1,0:T(8,128)(2,1)S(1)}, u32[]{:S(2)}, u32[]{:S(2)}) collective-permute-start(bf16[1187,512]{1,0:T(8,128)(2,1)S(1)} %fusion.8), channel_id=1, source_target_pairs={{0,128},{128,0},{1,129},{129,1},{2,130},{130,2},{3,131},{131,3},{4... | collective-permute-start | bytes 3646472 | tf_op jit(solution)/shard_map/ppermute | solution.py:14
  115.1 687.7 %copy-start.1 = (s32[512]{0:T(512)S(1)}, s32[512]{0:T(512)}, u32[]{:S(2)}) copy-start(s32[512]{0:T(512)} %param.6) | copy-start | bytes 6148
  1639.4 9.5 collective-permute-start.1
Sparse Core Ops, SparseCore 0:
  23.8 54.7 all-gather.3
where the time goes:
time: 1680 us; the launch traced here: 1660 us
  blocking collectives  1490 us (89%)
  waiting for transfers between devices  94.3 us (6%)
  local copies, waits for them, and re-layouts  27.1 us (2%)
  matrix products  18.4 us (1%)
    psum x1, blocking collectives, shards(): summed = lax.psum(partial_value, ('vocab', 'tok'))  819 us
    psum x1, blocking collectives, shards(): lax.psum((jnp.sum(jnp.exp(teacher_z - teacher_peak), axis=0), jnp.sum(jnp...  337 us
    pmax x1, blocking collectives, shards(): lax.pmax((jnp.max(teacher_z, axis=0), jnp.max(student_z, axis=0)), ('voca...  317 us
    all_gather x1, waiting for transfers between devices, shards(): lax.all_gather(token_rows, 'vocab', axis=1, tiled=True)  54.9 us
  transfers between devices with their start and end apart: 3, of which 3 were waited for; matrix products, arithmetic and copies ran while one was open for 1% of the time, Pallas kernels for 0%

commit v1 on v0

v1 whole, which is shorter than its diff:
```python
import functools
import jax
import jax.numpy as jnp
from jax import lax
from jax.experimental import pallas as pl
from jax.experimental.pallas import tpu as pltpu
from jax.sharding import Mesh, PartitionSpec as P

BF16 = jnp.bfloat16
F32 = jnp.float32
VMEM_LIMIT = 50 * 1024 * 1024
EXTRA = 8


def shifts(x, axis, step):
    size = lax.axis_size(axis)
    return lax.ppermute(x, axis, [(i, (i + step) % size) for i in range(size)])


def student_shifts(x, axis, step):
    size = lax.axis_size(axis)
    return lax.ppermute(
        x, ("grp", axis), [(size + i, size + (i + step) % size) for i in range(size)]
    )


def gathered(x, axis):
    return [x] + [shifts(x, axis, k) for k in range(1, lax.axis_size(axis))]


def scattered(parts, axis):
    return [parts[0]] + [student_shifts(parts[k], axis, k) for k in range(1, len(parts))]


def in_vmem():
    return pl.BlockSpec(memory_space=pltpu.VMEM)


def vmem_call(kernel, out_shape, *arrays, place=None, scratch=()):
    scalars = [] if place is None else [place]
    return pl.pallas_call(
        kernel,
        out_shape=out_shape,
        in_specs=[pl.BlockSpec(memory_space=pltpu.SMEM)] * len(scalars)
        + [in_vmem()] * len(arrays),
        out_specs=jax.tree.map(lambda _: in_vmem(), out_shape),
        scratch_shapes=list(scratch),
        compiler_params=pltpu.CompilerParams(vmem_limit_bytes=VMEM_LIMIT),
    )(*scalars, *arrays)


def order_tok_kernel(place_ref, p0, p1, p2, p3, lower, upper, held):
    me = place_ref[3]
    rows = p0.shape[0]
    for k, piece in enumerate((p0, p1, p2, p3)):
        held[lax.rem(me + 4 - k, 4)] = piece[...]
    lower[:rows] = held[0]
    lower[rows:] = held[1]
    upper[:rows] = held[2]
    upper[rows:] = held[3]


def stack_kernel(u0, u1, u2, u3, v0, v1, v2, v3, u_out, v_out):
    for k, piece in enumerate((u0, u1, u2, u3)):
        u_out[k] = piece[...]
    for k, piece in enumerate((v0, v1, v2, v3)):
        v_out[k] = piece[...]


def order_chips_kernel(place_ref, u0, u1, u2, u3, v0, v1, v2, v3, out):
    y, x = place_ref[0], place_ref[1]
    rows, wide = u0.shape[1:]
    for ky in range(4):
        for kx in range(4):
            chip = lax.rem(y + 4 - ky, 4) * 4 + lax.rem(x + 4 - kx, 4)
            out[chip, :rows] = (u0, u1, u2, u3)[ky][kx]
            out[chip, rows:] = (v0, v1, v2, v3)[kx][ky]


def join_cores_kernel(place_ref, own, sibling, lower, upper):
    core = place_ref[2]
    chips, rows, wide = own.shape
    half = rows // 2
    for chip in range(chips):
        first = jnp.where(core == 0, own[chip], sibling[chip])
        second = jnp.where(core == 0, sibling[chip], own[chip])
        at = 2 * chip * wide
        lower[:, at : at + wide] = first[:half]
        lower[:, at + wide : at + 2 * wide] = second[:half]
        upper[:, at : at + wide] = first[half:]
        upper[:, at + wide : at + 2 * wide] = second[half:]


def merge_kernel(*refs):
    parts, out = refs[:-1], refs[-1]
    peak = functools.reduce(jnp.maximum, [p[0:1] for p in parts])
    out[0:1] = peak
    out[1:2] = total([p[1:2] * jnp.exp(p[0:1] - peak) for p in parts])
    out[2:3] = total([p[2:3] for p in parts])


def total(parts):
    if len(parts) == 2:
        return parts[0] + parts[1]
    return (parts[0] + parts[2]) + (parts[1] + parts[3])


def grads_kernel(place_ref, grads, weights, extra, keep, send, turned):
    step = pl.program_id(0)
    core = place_ref[2]

    @pl.when(step == 0)
    def _():
        turned[...] = grads[...].T

    tokens = grads.shape[1]
    wide = weights.shape[1] // 2
    full = jnp.dot(turned[...], weights[...], preferred_element_type=F32)
    low = full[:, :wide]
    high = full[:, wide:]
    first = step // 4
    second = step % 4
    at = pl.ds(pl.multiple_of(second * tokens, tokens), tokens)
    keep[first, at] = jnp.where(core == 0, low, high)
    send[first, at] = jnp.where(core == 0, high, low)

    @pl.when(second == 0)
    def _():
        keep[first, 4 * tokens :] = extra[...]
        send[first, 4 * tokens :] = extra[...]


def split_grads(place, grads, weights, extra, x_first):
    words, tokens = grads.shape
    wide = weights.shape[1] // 16

    def chip(i, p):
        kx, ky = (i // 4, i % 4) if x_first else (i % 4, i // 4)
        return (0, lax.rem(p[0] + ky, 4) * 4 + lax.rem(p[1] + kx, 4))

    part = jax.ShapeDtypeStruct((4, 4 * tokens + EXTRA, wide // 2), F32)
    return pl.pallas_call(
        grads_kernel,
        out_shape=[part] * 2,
        grid_spec=pltpu.PrefetchScalarGridSpec(
            num_scalar_prefetch=1,
            grid=(16,),
            in_specs=[in_vmem(), pl.BlockSpec((words, wide), chip), in_vmem()],
            out_specs=[in_vmem()] * 2,
            scratch_shapes=[pltpu.VMEM((tokens, words), BF16)],
        ),
        compiler_params=pltpu.CompilerParams(vmem_limit_bytes=VMEM_LIMIT),
    )(place, grads, weights, extra)


def pair_sum_kernel(keep, got, *outs):
    for k, out in enumerate(outs):
        out[...] = keep[k] + got[k]


def line_sum_kernel(p0, p1, p2, p3, *outs):
    rows = outs[0].shape[0] - EXTRA
    tail = pl.ds(4 * rows, EXTRA)
    extra = total([p0[tail], p1[tail], p2[tail], p3[tail]])
    for k, out in enumerate(outs):
        at = pl.ds(k * rows, rows)
        out[:rows] = total([p0[at], p1[at], p2[at], p3[at]])
        out[rows:] = extra


def last_split_kernel(place_ref, a0, a1, a2, a3, b0, b1, b2, b3, *refs):
    outs, held = refs[:8], refs[8]
    me = place_ref[3]
    rows = a0.shape[0] - EXTRA
    held[0] = total([a0[...], a1[...], a2[...], a3[...]])
    held[1] = total([b0[...], b1[...], b2[...], b3[...]])
    part = rows // 4
    for k in range(4):
        start = pl.multiple_of(lax.rem(me + k, 4) * part, part)
        for half in range(2):
            out = outs[4 * half + k]
            out[:part] = held[half, pl.ds(start, part)]
            out[part : part + EXTRA] = held[0, rows:]
            out[part + EXTRA :] = held[1, rows:]


def shards(hidden, head_weight, labels, loss_mask):
    weights = head_weight[0]
    words, feats = weights.shape
    place = jnp.stack([lax.axis_index(a) for a in ("y", "x", "core", "tok")]).astype(jnp.int32)
    is_teacher = lax.axis_index("grp") == 0
    first_word = lax.axis_index(("y", "x", "core", "tok")) * words
    word_ids = first_word + lax.broadcasted_iota(jnp.int32, (words, 1), 0)
    mask = loss_mask.astype(F32)

    block = hidden[0]
    rows, wide = block.shape
    half = 2 * rows
    array = jax.ShapeDtypeStruct
    lower, upper = vmem_call(
        order_tok_kernel,
        [array((half, wide), BF16)] * 2,
        *gathered(block, "tok"),
        place=place,
        scratch=[pltpu.VMEM((4, rows, wide), BF16)],
    )
    u, v = vmem_call(
        stack_kernel,
        [array((4, half, wide), BF16)] * 2,
        *gathered(lower, "x"),
        *gathered(upper, "y"),
    )
    own = vmem_call(
        order_chips_kernel,
        array((16, 2 * half, wide), BF16),
        *gathered(u, "y"),
        *gathered(v, "x"),
        place=place,
    )
    inputs = vmem_call(
        join_cores_kernel,
        [array((half, feats), BF16)] * 2,
        own,
        shifts(own, "core", 1),
        place=place,
    )

    own_z, sent = [], []
    for c in range(2):
        z = lax.dot_general(
            weights, inputs[c], (((1,), (1,)), ((), ())), preferred_element_type=F32
        ).astype(BF16)
        own_z.append(lax.optimization_barrier(z))
        sent.append(lax.ppermute(own_z[c], "grp", [(0, 1)]))

    hits = [word_ids == labels[c * half : (c + 1) * half][None, :] for c in range(2)]
    stats = []
    for c in range(2):
        z = own_z[c].astype(F32)
        peak = jnp.max(z, axis=0)
        stats.append(
            jnp.stack(
                [
                    peak,
                    jnp.sum(jnp.exp(z - peak), axis=0),
                    jnp.sum(jnp.where(hits[c], z, 0.0), axis=0),
                ]
            )
        )
    stats = jnp.concatenate(stats, axis=1)
    for axis in ("core", "x", "y", "tok"):
        stats = vmem_call(merge_kernel, array(stats.shape, F32), *gathered(stats, axis))
    own_norm = stats[0] + jnp.log(stats[1])
    told = jnp.stack([own_norm, stats[2]])
    heard = lax.ppermute(told, "grp", [(0, 1), (1, 0)])
    teacher_norm = jnp.where(is_teacher, own_norm, heard[0])
    student_norm = jnp.where(is_teacher, heard[0], own_norm)
    label_logit = jnp.where(is_teacher, heard[1], stats[2])

    ends = []
    for c in range(2):
        span = slice(c * half, (c + 1) * half)
        teacher_logp = sent[c].astype(F32) - teacher_norm[span]
        student_logp = own_z[c].astype(F32) - student_norm[span]
        teacher_prob = jnp.exp(teacher_logp)
        student_prob = jnp.exp(student_logp)
        diverge = jnp.sum(teacher_prob * (teacher_logp - student_logp), axis=0)
        grads = (
            (2.0 * student_prob - teacher_prob - hits[c].astype(F32)) * mask[span]
        ).astype(BF16)
        extra = jnp.zeros((EXTRA, wide), F32).at[:2].set(diverge.reshape(2, wide))
        keep, send = split_grads(place, grads, weights, extra, c == 0)
        axes = ("x", "y") if c == 0 else ("y", "x")
        parts = vmem_call(
            pair_sum_kernel,
            [array(keep.shape[1:], F32)] * 4,
            keep,
            student_shifts(send, "core", 1),
        )
        parts = vmem_call(
            line_sum_kernel,
            [array((half + EXTRA, wide), F32)] * 4,
            *scattered(parts, axes[0]),
        )
        ends += scattered(parts, axes[1])

    part = half // 4
    last = vmem_call(
        last_split_kernel,
        [array((part + 2 * EXTRA, wide), F32)] * 8,
        *ends,
        place=place,
        scratch=[pltpu.VMEM((2, half + EXTRA, wide), F32)],
    )
    for_teacher, for_student = last[:4], last[4:]
    got_student = scattered(for_student, "tok")
    got_teacher = [
        lax.ppermute(
            for_teacher[k], ("grp", "tok"), [(4 + i, (i + k) % 4) for i in range(4)]
        )
        for k in range(4)
    ]
    mine = total([jnp.where(is_teacher, t, s) for t, s in zip(got_teacher, got_student)])
    input_grads = mine[:part].astype(BF16)
    diverged = jnp.concatenate([mine[part : part + 2], mine[part + EXTRA : part + EXTRA + 2]])
    token_loss = mask * (diverged.reshape(-1) + student_norm - label_logit)
    return (input_grads, token_loss, jnp.stack([teacher_norm, student_norm]))


def solution(mesh):
    fine = Mesh(mesh.devices.reshape(2, 4, 4, 2, 4), ("grp", "y", "x", "core", "tok"))
    vocab = ("y", "x", "core")
    return jax.shard_map(
        shards,
        mesh=fine,
        in_specs=(
            P("grp", "tok", vocab),
            P("grp", vocab + ("tok",), None),
            P(),
            P(),
        ),
        out_specs=(P(("grp", "tok"), vocab), P(), P()),
        check_vma=False,
    )
```

time: 1680 us -> 271 us (0.16); the launches traced: 1660 us -> 268 us
  blocking collectives: 1490 us -> 0 us
  starting transfers between devices: 7.14 us -> 65.5 us
  Pallas kernels: 0 us -> 41.5 us
  waiting for transfers between devices: 94.3 us -> 135 us
  local copies, waits for them, and re-layouts: 27.1 us -> 8.19 us
    psum x2 -> x0, blocking collectives: 1160 us -> none  [the longest x1 819 us: shards(): summed = lax.psum(partial_value, ('vocab', 'tok'))]
    pmax x1 -> x0, blocking collectives: 317 us -> none  [shards(): lax.pmax((jnp.max(teacher_z, axis=0), jnp.max(student_z, axis=0)), ('voca...]
    ppermute x2 -> x50, waiting for transfers between devices: 39.4 us -> 135 us  [the longest x4 86.4 us: shards(): lax.ppermute(for_teacher[k], ('grp', 'tok'), [(4 + i, (i + k) % 4) for i...]
    ppermute x2 -> x50, starting transfers between devices: 7.1 us -> 65.5 us  [the longest x26 39.1 us: shifts(): return lax.ppermute(x, axis, [(i, (i + step) % size) for i in range(size)])]
    all_gather x1 -> x0, waiting for transfers between devices: 54.9 us -> none  [shards(): lax.all_gather(token_rows, 'vocab', axis=1, tiled=True)]
    pallas_call x0 -> x15, Pallas kernels: none -> 41.5 us  [the longest x2 28.7 us: split_grads(): pl.pallas_call(grads_kernel, out_shape=[part] * 2, grid_spec=pltpu.Prefet...]
  transfers between devices with their start and end apart: 3 -> 50, of which waited for: 3 -> 25; matrix products, arithmetic and copies ran while one was open for 1% -> 0% of each run, Pallas kernels for 0% -> 7%
where the time goes in v1:
time: 271 us; the launch traced here: 268 us
  waiting for transfers between devices  135 us (50%)
  starting transfers between devices  65.5 us (24%)
  Pallas kernels  41.5 us (15%)
  matrix products  12.6 us (5%)
  local copies, waits for them, and re-layouts  8.19 us (3%)
  other arithmetic  4.19 us (2%)
    ppermute x4, waiting for transfers between devices, shards(): lax.ppermute(for_teacher[k], ('grp', 'tok'), [(4 + i, (i + k) % 4) for i...  86.4 us
    ppermute x26, starting transfers between devices, shifts(): return lax.ppermute(x, axis, [(i, (i + step) % size) for i in range(size)])  39.1 us
    ppermute x26, waiting for transfers between devices, shifts(): return lax.ppermute(x, axis, [(i, (i + step) % size) for i in range(size)])  28.9 us
    pallas_call x2, Pallas kernels, split_grads(): pl.pallas_call(grads_kernel, out_shape=[part] * 2, grid_spec=pltpu.Prefet...  28.7 us
    ppermute x2, waiting for transfers between devices, shards(): sent.append(lax.ppermute(own_z[c], 'grp', [(0, 1)]))  19.4 us
    pallas_call x13, Pallas kernels, vmem_call(): pl.pallas_call(kernel, out_shape=out_shape, in_specs=[pl.BlockSpec(memory...  12.8 us
    dot_general x2, matrix products, shards(): lax.dot_general(weights, inputs[c], (((1,), (1,)), ((), ())), preferred_e...  12.6 us
    ppermute x17, starting transfers between devices, student_shifts(): lax.ppermute(x, ('grp', axis), [(size + i, size + (i + step) % size) for...  11.7 us
  transfers between devices with their start and end apart: 50, of which 25 were waited for; matrix products, arithmetic and copies ran while one was open for 0% of the time, Pallas kernels for 7%

profile of v1, /device:TPU:2, one launch (start us, length us, event | category | flops | bytes accessed | tf_op | source)
XLA Modules:
  0.0 268.0 jit_solution(14398044132066920361)
XLA Ops:
  2.6 3.3 %collective-permute-start.1 = (bf16[128,128]{1,0:T(8,128)(2,1)}, bf16[128,128]{1,0:T(8,128)(2,1)S(1)}, u32[]{:S(2)}, u32[]{:S(2)}) collective-permute-start(bf16[128,128]{1,0:T(8,128)(2,1)} %bitcast.39), channel_id=1, source_target_pairs={{0,2},{1,3},{2,0},{3,1},{4,6},{5,7},{6,4},{7,5},{8,10},{9,11},{10,... | collective-permute-start | bytes 98312 | tf_op jit(solution)/shard_map/ppermute | solution.py:17
  14.0 2.2 collective-permute-start.5
  17.8 2.9 %collective-permute-start.7 = (bf16[256,128]{1,0:T(8,128)(2,1)S(1)}, bf16[256,128]{1,0:T(8,128)(2,1)S(1)}, u32[]{:S(2)}, u32[]{:S(2)}) collective-permute-start(bf16[256,128]{1,0:T(8,128)(2,1)S(1)} %get-tuple-element.62.v0), channel_id=1, source_target_pairs={{0,64},{32,96},{64,0},{96,32},{1,65},{33,97},{65,1},{97,33},{2,66}... | collective-permute-start | bytes 196616 | tf_op jit(solution)/shard_map/ppermute | solution.py:17
  28.1 3.5 %collective-permute-start.13 = (bf16[4,256,128]{2,1,0:T(8,128)(2,1)S(1)}, bf16[4,256,128]{2,1,0:T(8,128)(2,1)S(1)}, u32[]{:S(2)}, u32[]{:S(2)}) collective-permute-start(bf16[4,256,128]{2,1,0:T(8,128)(2,1)S(1)} %get-tuple-element.64.v0), channel_id=1, source_target_pairs={{0,16},{8,24},{16,0},{24,8},{1,17},{9,25},{17,1},{25,9},{2,18},{10... | collective-permute-start | bytes 786440 | tf_op jit(solution)/shard_map/ppermute | solution.py:17
  36.4 2.6 collective-permute-done.14.v3
  42.9 4.3 %collective-permute-done.15.sibling = bf16[16,512,128]{2,1,0:T(8,128)(2,1)S(1)} collective-permute-done((bf16[16,512,128]{2,1,0:T(8,128)(2,1)}, bf16[16,512,128]{2,1,0:T(8,128)(2,1)S(1)}, u32[]{:S(2)}, u32[]{:S(2)}) %collective-permute-start.15) | collective-permute-done | bytes 2097184 | tf_op jit(solution)/shard_map/ppermute | solution.py:17
  48.6 4.3 %shard_map.70 = (bf16[256,4096]{1,0:T(8,128)(2,1)S(1)}, bf16[256,4096]{1,0:T(8,128)(2,1)}) custom-call(s32[4]{0:T(128)S(1)} %pad_add_fusion.place_ref, bf16[16,512,128]{2,1,0:T(8,128)(2,1)} %shard_map.69.own, bf16[16,512,128]{2,1,0:T(8,128)(2,1)} %copy-done.5), custom_call_target="tpu_custom_call" | custom-call | tf_op jit(solution)/shard_map/pallas_call | solution.py:41
  53.0 6.4 %fusion = bf16[1187,256]{1,0:T(8,128)(2,1)S(1)} fusion(bf16[256,4096]{1,0:T(8,128)(2,1)S(1)} %get-tuple-element.65, bf16[1,1187,4096]{2,1,0:T(8,128)(2,1)} %param.9), kind=kOutput, calls=%fused_computation.2 | convolution fusion | flops 2489623296 | bytes 12428800 | tf_op jit(solution)/shard_map/dot_general | solution.py:230
  59.6 6.2 %fusion.1 = bf16[1187,256]{1,0:T(8,128)(2,1)S(1)} fusion(bf16[256,4096]{1,0:T(8,128)(2,1)S(1)} %copy-done.8, bf16[1,1187,4096]{2,1,0:T(8,128)(2,1)} %param.9), kind=kOutput, calls=%fused_computation.3 | convolution fusion | flops 2489623296 | bytes 12428800 | tf_op jit(solution)/shard_map/dot_general | solution.py:230
  68.3 3.2 %collective-permute-start.18 = (f32[3,512]{1,0:T(4,128)S(1)}, f32[3,512]{1,0:T(4,128)S(1)}, u32[]{:S(2)}, u32[]{:S(2)}) collective-permute-start(f32[3,512]{1,0:T(4,128)S(1)} %shard_map.71.refs_0_), channel_id=1, source_target_pairs={{0,16},{8,24},{16,0},{24,8},{1,17},{9,25},{17,1},{25,9},{2,18},{10... | collective-permute-start | bytes 18440 | tf_op jit(solution)/shard_map/ppermute | solution.py:17
  75.3 3.3 %collective-permute-start.21 = (f32[3,512]{1,0:T(4,128)S(1)}, f32[3,512]{1,0:T(4,128)S(1)}, u32[]{:S(2)}, u32[]{:S(2)}) collective-permute-start(f32[3,512]{1,0:T(4,128)S(1)} %shard_map.72.refs_0_), channel_id=1, source_target_pairs={{0,64},{32,96},{64,0},{96,32},{1,65},{33,97},{65,1},{97,33},{2,66}... | collective-permute-start | bytes 18440 | tf_op jit(solution)/shard_map/ppermute | solution.py:17
  82.6 5.5 %collective-permute-start.24 = (f32[3,512]{1,0:T(4,128)S(1)}, f32[3,512]{1,0:T(4,128)S(1)}, u32[]{:S(2)}, u32[]{:S(2)}) collective-permute-start(f32[3,512]{1,0:T(4,128)S(1)} %shard_map.73.refs_0_), channel_id=1, source_target_pairs={{0,2},{1,3},{2,0},{3,1},{4,6},{5,7},{6,4},{7,5},{8,10},{9,11},{10,... | collective-permute-start | bytes 18440 | tf_op jit(solution)/shard_map/ppermute | solution.py:17
  91.7 2.9 %collective-permute-start.26 = (f32[2,512]{1,0:T(2,128)S(1)}, f32[2,512]{1,0:T(2,128)S(1)}, u32[]{:S(2)}, u32[]{:S(2)}) collective-permute-start(f32[2,512]{1,0:T(2,128)S(1)} %pad_maximum_fusion), channel_id=1, source_target_pairs={{0,128},{128,0},{1,129},{129,1},{2,130},{130,2},{3,131},{131,3},{4... | collective-permute-start | bytes 12296 | tf_op jit(solution)/shard_map/ppermute | solution.py:255
  94.7 5.0 %collective-permute-start.27 = (bf16[1187,256]{1,0:T(8,128)(2,1)S(1)}, bf16[1187,256]{1,0:T(8,128)(2,1)S(1)}, u32[]{:S(2)}, u32[]{:S(2)}) collective-permute-start(bf16[1187,256]{1,0:T(8,128)(2,1)S(1)} %fusion), channel_id=1, source_target_pairs={{0,128},{1,129},{2,130},{3,131},{4,132},{5,133},{6,134},{7,135},{8... | collective-permute-start | bytes 1823240 | tf_op jit(solution)/shard_map/ppermute | solution.py:234
  101.3 12.6 %collective-permute-done.27 = bf16[1187,256]{1,0:T(8,128)(2,1)S(1)} collective-permute-done((bf16[1187,256]{1,0:T(8,128)(2,1)S(1)}, bf16[1187,256]{1,0:T(8,128)(2,1)S(1)}, u32[]{:S(2)}, u32[]{:S(2)}) %collective-permute-start.27) | collective-permute-done | bytes 607776 | tf_op jit(solution)/shard_map/ppermute | solution.py:234
  113.9 6.9 %collective-permute-done.35 = bf16[1187,256]{1,0:T(8,128)(2,1)S(1)} collective-permute-done((bf16[1187,256]{1,0:T(8,128)(2,1)S(1)}, bf16[1187,256]{1,0:T(8,128)(2,1)S(1)}, u32[]{:S(2)}, u32[]{:S(2)}) %collective-permute-start.35) | collective-permute-done | bytes 607776 | tf_op jit(solution)/shard_map/ppermute | solution.py:234
  122.6 14.4 %shard_map.78 = (f32[4,1032,128]{2,1,0:T(8,128)S(1)}, f32[4,1032,128]{2,1,0:T(8,128)}) custom-call(s32[4]{0:T(128)S(1)} %pad_add_fusion.place_ref, bf16[1187,256]{1,0:T(8,128)(2,1)S(1)} %get-tuple-element.100.grads, bf16[1187,4096]{1,0:T(8,128)(2,1)} %bitcast.42, f32[8,128]{1,0:T(8,128)S(1)} %scatter.9.extra), custom_call_target="tpu_custom_call" | custom-call | tf_op jit(solution)/shard_map/pallas_call | solution.py:142
  139.1 14.3 %shard_map.75 = (f32[4,1032,128]{2,1,0:T(8,128)S(1)}, f32[4,1032,128]{2,1,0:T(8,128)}) custom-call(s32[4]{0:T(128)S(1)} %pad_add_fusion.place_ref, bf16[1187,256]{1,0:T(8,128)(2,1)S(1)} %get-tuple-element.120.grads, bf16[1187,4096]{1,0:T(8,128)(2,1)} %bitcast.43, f32[8,128]{1,0:T(8,128)S(1)} %scatter.6.extra), custom_call_target="tpu_custom_call" | custom-call | tf_op jit(solution)/shard_map/pallas_call | solution.py:142
  157.0 2.4 shard_map.79
  162.9 2.4 shard_map.76
  177.8 54.8 %collective-permute-done.43 = f32[80,128]{1,0:T(8,128)S(1)} collective-permute-done((f32[80,128]{1,0:T(8,128)S(1)}, f32[80,128]{1,0:T(8,128)S(1)}, u32[]{:S(2)}, u32[]{:S(2)}) %collective-permute-start.43) | collective-permute-done | bytes 40992 | tf_op jit(solution)/shard_map/ppermute | solution.py:298
  233.9 24.9 %collective-permute-done.44 = f32[80,128]{1,0:T(8,128)S(1)} collective-permute-done((f32[80,128]{1,0:T(8,128)S(1)}, f32[80,128]{1,0:T(8,128)S(1)}, u32[]{:S(2)}, u32[]{:S(2)}) %collective-permute-start.44) | collective-permute-done | bytes 40992 | tf_op jit(solution)/shard_map/ppermute | solution.py:298
  260.1 2.6 collective-permute-done.46
  262.7 4.0 %collective-permute-done.48 = f32[80,128]{1,0:T(8,128)S(1)} collective-permute-done((f32[80,128]{1,0:T(8,128)S(1)}, f32[80,128]{1,0:T(8,128)S(1)}, u32[]{:S(2)}, u32[]{:S(2)}) %collective-permute-start.48) | collective-permute-done | bytes 40992 | tf_op jit(solution)/shard_map/ppermute | solution.py:298
  (135 shorter events, 71.8 us)
Async XLA Ops:
  0.6 7.0 %collective-permute-start = (bf16[128,128]{1,0:T(8,128)(2,1)}, bf16[128,128]{1,0:T(8,128)(2,1)S(1)}, u32[]{:S(2)}, u32[]{:S(2)}) collective-permute-start(bf16[128,128]{1,0:T(8,128)(2,1)} %bitcast.38), channel_id=1, source_target_pairs={{0,1},{1,2},{2,3},{3,0},{4,5},{5,6},{6,7},{7,4},{8,9},{9,10},{10,1... | collective-permute-start | bytes 98312 | tf_op jit(solution)/shard_map/ppermute | solution.py:17
  11.4 9.3 %collective-permute-start.3 = (bf16[256,128]{1,0:T(8,128)(2,1)S(1)}, bf16[256,128]{1,0:T(8,128)(2,1)S(1)}, u32[]{:S(2)}, u32[]{:S(2)}) collective-permute-start(bf16[256,128]{1,0:T(8,128)(2,1)S(1)} %get-tuple-element.61.u0), channel_id=1, source_target_pairs={{0,8},{8,16},{16,24},{24,0},{1,9},{9,17},{17,25},{25,1},{2,10},{10... | collective-permute-start | bytes 196616 | tf_op jit(solution)/shard_map/ppermute | solution.py:17
  12.9 9.1 %collective-permute-start.4 = (bf16[256,128]{1,0:T(8,128)(2,1)S(1)}, bf16[256,128]{1,0:T(8,128)(2,1)S(1)}, u32[]{:S(2)}, u32[]{:S(2)}) collective-permute-start(bf16[256,128]{1,0:T(8,128)(2,1)S(1)} %get-tuple-element.61.u0), channel_id=1, source_target_pairs={{0,16},{8,24},{16,0},{24,8},{1,17},{9,25},{17,1},{25,9},{2,18},{10... | collective-permute-start | bytes 196616 | tf_op jit(solution)/shard_map/ppermute | solution.py:17
  14.0 8.0 %collective-permute-start.5 = (bf16[256,128]{1,0:T(8,128)(2,1)S(1)}, bf16[256,128]{1,0:T(8,128)(2,1)S(1)}, u32[]{:S(2)}, u32[]{:S(2)}) collective-permute-start(bf16[256,128]{1,0:T(8,128)(2,1)S(1)} %get-tuple-element.61.u0), channel_id=1, source_target_pairs={{0,24},{8,0},{16,8},{24,16},{1,25},{9,1},{17,9},{25,17},{2,26},{10... | collective-permute-start | bytes 196616 | tf_op jit(solution)/shard_map/ppermute | solution.py:17
  25.0 8.3 %collective-permute-start.10 = (bf16[4,256,128]{2,1,0:T(8,128)(2,1)S(1)}, bf16[4,256,128]{2,1,0:T(8,128)(2,1)S(1)}, u32[]{:S(2)}, u32[]{:S(2)}) collective-permute-start(bf16[4,256,128]{2,1,0:T(8,128)(2,1)S(1)} %get-tuple-element.63.u0), channel_id=1, source_target_pairs={{0,64},{32,96},{64,0},{96,32},{1,65},{33,97},{65,1},{97,33},{2,66}... | collective-permute-start | bytes 786440 | tf_op jit(solution)/shard_map/ppermute | solution.py:17
  26.7 9.7 %collective-permute-start.11 = (bf16[4,256,128]{2,1,0:T(8,128)(2,1)S(1)}, bf16[4,256,128]{2,1,0:T(8,128)(2,1)S(1)}, u32[]{:S(2)}, u32[]{:S(2)}) collective-permute-start(bf16[4,256,128]{2,1,0:T(8,128)(2,1)S(1)} %get-tuple-element.63.u0), channel_id=1, source_target_pairs={{0,96},{32,0},{64,32},{96,64},{1,97},{33,1},{65,33},{97,65},{2,98}... | collective-permute-start | bytes 786440 | tf_op jit(solution)/shard_map/ppermute | solution.py:17
  28.1 8.3 %collective-permute-start.12 = (bf16[4,256,128]{2,1,0:T(8,128)(2,1)S(1)}, bf16[4,256,128]{2,1,0:T(8,128)(2,1)S(1)}, u32[]{:S(2)}, u32[]{:S(2)}) collective-permute-start(bf16[4,256,128]{2,1,0:T(8,128)(2,1)S(1)} %get-tuple-element.64.v0), channel_id=1, source_target_pairs={{0,8},{8,16},{16,24},{24,0},{1,9},{9,17},{17,25},{25,1},{2,10},{10... | collective-permute-start | bytes 786440 | tf_op jit(solution)/shard_map/ppermute | solution.py:17
  28.1 8.3 %collective-permute-start.13 = (bf16[4,256,128]{2,1,0:T(8,128)(2,1)S(1)}, bf16[4,256,128]{2,1,0:T(8,128)(2,1)S(1)}, u32[]{:S(2)}, u32[]{:S(2)}) collective-permute-start(bf16[4,256,128]{2,1,0:T(8,128)(2,1)S(1)} %get-tuple-element.64.v0), channel_id=1, source_target_pairs={{0,16},{8,24},{16,0},{24,8},{1,17},{9,25},{17,1},{25,9},{2,18},{10... | collective-permute-start | bytes 786440 | tf_op jit(solution)/shard_map/ppermute | solution.py:17
  31.6 7.4 %collective-permute-start.14 = (bf16[4,256,128]{2,1,0:T(8,128)(2,1)S(1)}, bf16[4,256,128]{2,1,0:T(8,128)(2,1)S(1)}, u32[]{:S(2)}, u32[]{:S(2)}) collective-permute-start(bf16[4,256,128]{2,1,0:T(8,128)(2,1)S(1)} %get-tuple-element.64.v0), channel_id=1, source_target_pairs={{0,24},{8,0},{16,8},{24,16},{1,25},{9,1},{17,9},{25,17},{2,26},{10... | collective-permute-start | bytes 786440 | tf_op jit(solution)/shard_map/ppermute | solution.py:17
  33.3 7.6 %collective-permute-start.9 = (bf16[4,256,128]{2,1,0:T(8,128)(2,1)S(1)}, bf16[4,256,128]{2,1,0:T(8,128)(2,1)S(1)}, u32[]{:S(2)}, u32[]{:S(2)}) collective-permute-start(bf16[4,256,128]{2,1,0:T(8,128)(2,1)S(1)} %get-tuple-element.63.u0), channel_id=1, source_target_pairs={{0,32},{32,64},{64,96},{96,0},{1,33},{33,65},{65,97},{97,1},{2,34}... | collective-permute-start | bytes 786440 | tf_op jit(solution)/shard_map/ppermute | solution.py:17
  82.6 7.1 %collective-permute-start.24 = (f32[3,512]{1,0:T(4,128)S(1)}, f32[3,512]{1,0:T(4,128)S(1)}, u32[]{:S(2)}, u32[]{:S(2)}) collective-permute-start(f32[3,512]{1,0:T(4,128)S(1)} %shard_map.73.refs_0_), channel_id=1, source_target_pairs={{0,2},{1,3},{2,0},{3,1},{4,6},{5,7},{6,4},{7,5},{8,10},{9,11},{10,... | collective-permute-start | bytes 18440 | tf_op jit(solution)/shard_map/ppermute | solution.py:17
  91.7 9.5 %collective-permute-start.26 = (f32[2,512]{1,0:T(2,128)S(1)}, f32[2,512]{1,0:T(2,128)S(1)}, u32[]{:S(2)}, u32[]{:S(2)}) collective-permute-start(f32[2,512]{1,0:T(2,128)S(1)} %pad_maximum_fusion), channel_id=1, source_target_pairs={{0,128},{128,0},{1,129},{129,1},{2,130},{130,2},{3,131},{131,3},{4... | collective-permute-start | bytes 12296 | tf_op jit(solution)/shard_map/ppermute | solution.py:255
  94.7 19.2 %collective-permute-start.27 = (bf16[1187,256]{1,0:T(8,128)(2,1)S(1)}, bf16[1187,256]{1,0:T(8,128)(2,1)S(1)}, u32[]{:S(2)}, u32[]{:S(2)}) collective-permute-start(bf16[1187,256]{1,0:T(8,128)(2,1)S(1)} %fusion), channel_id=1, source_target_pairs={{0,128},{1,129},{2,130},{3,131},{4,132},{5,133},{6,134},{7,135},{8... | collective-permute-start | bytes 1823240 | tf_op jit(solution)/shard_map/ppermute | solution.py:234
  99.7 21.1 %collective-permute-start.35 = (bf16[1187,256]{1,0:T(8,128)(2,1)S(1)}, bf16[1187,256]{1,0:T(8,128)(2,1)S(1)}, u32[]{:S(2)}, u32[]{:S(2)}) collective-permute-start(bf16[1187,256]{1,0:T(8,128)(2,1)S(1)} %fusion.1), channel_id=1, source_target_pairs={{0,128},{1,129},{2,130},{3,131},{4,132},{5,133},{6,134},{7,135},{8... | collective-permute-start | bytes 1823240 | tf_op jit(solution)/shard_map/ppermute | solution.py:234
  138.3 17.3 %collective-permute-start.36 = (f32[4,1032,128]{2,1,0:T(8,128)}, f32[4,1032,128]{2,1,0:T(8,128)S(1)}, u32[]{:S(2)}, u32[]{:S(2)}) collective-permute-start(f32[4,1032,128]{2,1,0:T(8,128)} %get-tuple-element.78), channel_id=1, source_target_pairs={{128,132},{132,128},{129,133},{133,129},{130,134},{134,130},{131,1... | collective-permute-start | bytes 6340616 | tf_op jit(solution)/shard_map/ppermute | solution.py:22
  159.4 7.3 %collective-permute-start.37 = (f32[1032,128]{1,0:T(8,128)S(1)}, f32[1032,128]{1,0:T(8,128)S(1)}, u32[]{:S(2)}, u32[]{:S(2)}) collective-permute-start(f32[1032,128]{1,0:T(8,128)S(1)} %get-tuple-element.80), channel_id=1, source_target_pairs={{128,160},{160,192},{192,224},{224,128},{129,161},{161,193},{193,2... | collective-permute-start | bytes 1585160 | tf_op jit(solution)/shard_map/ppermute | solution.py:22
  160.1 7.3 %collective-permute-start.38 = (f32[1032,128]{1,0:T(8,128)S(1)}, f32[1032,128]{1,0:T(8,128)S(1)}, u32[]{:S(2)}, u32[]{:S(2)}) collective-permute-start(f32[1032,128]{1,0:T(8,128)S(1)} %get-tuple-element.81), channel_id=1, source_target_pairs={{128,192},{160,224},{192,128},{224,160},{129,193},{161,225},{193,1... | collective-permute-start | bytes 1585160 | tf_op jit(solution)/shard_map/ppermute | solution.py:22
  172.6 60.0 %collective-permute-start.43 = (f32[80,128]{1,0:T(8,128)S(1)}, f32[80,128]{1,0:T(8,128)S(1)}, u32[]{:S(2)}, u32[]{:S(2)}) collective-permute-start(f32[80,128]{1,0:T(8,128)S(1)} %get-tuple-element.87), channel_id=1, source_target_pairs={{128,0},{129,1},{130,2},{131,3},{132,4},{133,5},{134,6},{135,7},{1... | collective-permute-start | bytes 122888 | tf_op jit(solution)/shard_map/ppermute | solution.py:298
  173.9 85.0 %collective-permute-start.44 = (f32[80,128]{1,0:T(8,128)S(1)}, f32[80,128]{1,0:T(8,128)S(1)}, u32[]{:S(2)}, u32[]{:S(2)}) collective-permute-start(f32[80,128]{1,0:T(8,128)S(1)} %get-tuple-element.89), channel_id=1, source_target_pairs={{128,2},{129,3},{130,0},{131,1},{132,6},{133,7},{134,4},{135,5},{1... | collective-permute-start | bytes 122888 | tf_op jit(solution)/shard_map/ppermute | solution.py:298
  175.2 84.9 %collective-permute-start.45 = (f32[80,128]{1,0:T(8,128)S(1)}, f32[80,128]{1,0:T(8,128)S(1)}, u32[]{:S(2)}, u32[]{:S(2)}) collective-permute-start(f32[80,128]{1,0:T(8,128)S(1)} %get-tuple-element.90), channel_id=1, source_target_pairs={{128,130},{129,131},{130,128},{131,129},{132,134},{133,135},{134,1... | collective-permute-start | bytes 122888 | tf_op jit(solution)/shard_map/ppermute | solution.py:22
  175.8 86.9 %collective-permute-start.46 = (f32[80,128]{1,0:T(8,128)S(1)}, f32[80,128]{1,0:T(8,128)S(1)}, u32[]{:S(2)}, u32[]{:S(2)}) collective-permute-start(f32[80,128]{1,0:T(8,128)S(1)} %get-tuple-element.91), channel_id=1, source_target_pairs={{128,1},{129,2},{130,3},{131,0},{132,5},{133,6},{134,7},{135,4},{1... | collective-permute-start | bytes 122888 | tf_op jit(solution)/shard_map/ppermute | solution.py:298
  177.1 85.6 %collective-permute-start.47 = (f32[80,128]{1,0:T(8,128)S(1)}, f32[80,128]{1,0:T(8,128)S(1)}, u32[]{:S(2)}, u32[]{:S(2)}) collective-permute-start(f32[80,128]{1,0:T(8,128)S(1)} %get-tuple-element.92), channel_id=1, source_target_pairs={{128,129},{129,130},{130,131},{131,128},{132,133},{133,134},{134,1... | collective-permute-start | bytes 122888 | tf_op jit(solution)/shard_map/ppermute | solution.py:22
  232.6 34.1 %collective-permute-start.48 = (f32[80,128]{1,0:T(8,128)S(1)}, f32[80,128]{1,0:T(8,128)S(1)}, u32[]{:S(2)}, u32[]{:S(2)}) collective-permute-start(f32[80,128]{1,0:T(8,128)S(1)} %get-tuple-element.93), channel_id=1, source_target_pairs={{128,3},{129,0},{130,1},{131,2},{132,7},{133,4},{134,5},{135,6},{1... | collective-permute-start | bytes 122888 | tf_op jit(solution)/shard_map/ppermute | solution.py:298
  258.8 7.9 %collective-permute-start.49 = (f32[80,128]{1,0:T(8,128)S(1)}, f32[80,128]{1,0:T(8,128)S(1)}, u32[]{:S(2)}, u32[]{:S(2)}) collective-permute-start(f32[80,128]{1,0:T(8,128)S(1)} %get-tuple-element.94), channel_id=1, source_target_pairs={{128,131},{129,128},{130,129},{131,130},{132,135},{133,132},{134,1... | collective-permute-start | bytes 122888 | tf_op jit(solution)/shard_map/ppermute | solution.py:22
  (35 other events, 157.5 us)

commit v2 on v0

v2 whole, which is shorter than its diff:
```python
import functools
import jax
import jax.numpy as jnp
from jax import lax
from jax.experimental import pallas as pl
from jax.experimental.pallas import tpu as pltpu
from jax.sharding import Mesh, PartitionSpec as P

BF16 = jnp.bfloat16
F32 = jnp.float32
VMEM_LIMIT = 50 * 1024 * 1024
EXTRA = 8
STRIPS = 4
CHIPS = ("y", "x")
PLANES = ("grp", "tok")


def in_vmem():
    return pl.BlockSpec(memory_space=pltpu.VMEM)


def in_smem():
    return pl.BlockSpec(memory_space=pltpu.SMEM)


def vmem_call(kernel, out_shape, *arrays, place=None, weights=None, scratch=()):
    scalars = [] if place is None else [place]
    remote = [] if weights is None else [weights]
    return pl.pallas_call(
        kernel,
        out_shape=out_shape,
        in_specs=[in_smem()] * len(scalars)
        + [pl.BlockSpec(memory_space=pl.ANY)] * len(remote)
        + [in_vmem()] * len(arrays),
        out_specs=jax.tree.map(lambda _: in_vmem(), out_shape),
        scratch_shapes=list(scratch),
        compiler_params=pltpu.CompilerParams(vmem_limit_bytes=VMEM_LIMIT),
    )(*scalars, *remote, *arrays)


def swapped(x, axis):
    return lax.ppermute(x, axis, [(0, 1), (1, 0)])


def swapped_in_student(x):
    return lax.ppermute(x, ("grp", "core"), [(2, 3), (3, 2)])


def exchanged(x, axes):
    return lax.all_to_all(x, axes, 0, 0)


def order_tok_kernel(place_ref, p0, p1, p2, p3, lower, upper, held):
    me = place_ref[1]
    rows = p0.shape[0]
    for k, piece in enumerate((p0, p1, p2, p3)):
        held[lax.rem(me + 4 - k, 4)] = piece[...]
    for chip in range(lower.shape[0]):
        lower[chip, :rows] = held[0]
        lower[chip, rows:] = held[1]
        upper[chip, :rows] = held[2]
        upper[chip, rows:] = held[3]


def strips_of(weights, held, sems):
    depth = held.shape[2]
    copies = [
        pltpu.make_async_copy(weights.at[:, pl.ds(i * depth, depth)], held.at[i], sems.at[i])
        for i in range(STRIPS)
    ]
    for copy in copies:
        copy.start()
    return copies


def scores_kernel(place_ref, weights, own, sibling, out, joined, held, acc, sems):
    core = place_ref[0]
    chips, _, wide = own.shape
    depth = held.shape[2]
    words = out.shape[0]
    copies = strips_of(weights, held, sems)

    def join(first, second):
        for chip in range(chips):
            at = 2 * chip * wide
            joined[:, at : at + wide] = first[chip]
            joined[:, at + wide : at + 2 * wide] = second[chip]

    @pl.when(core == 0)
    def _():
        join(own, sibling)

    @pl.when(core != 0)
    def _():
        join(sibling, own)

    tall = 608
    for i in range(STRIPS):
        copies[i].wait()
        for start in range(0, words, tall):
            at = slice(start, min(start + tall, words))
            part = lax.dot_general(
                held[i, at],
                joined[:, i * depth : (i + 1) * depth],
                (((1,), (1,)), ((), ())),
                preferred_element_type=F32,
            )
            if i > 0:
                part = acc[at] + part
            if i < STRIPS - 1:
                acc[at] = part
            else:
                out[at] = part.astype(BF16)


def scores(place, weights, own):
    words, feats = weights.shape
    tokens = own.shape[1]
    return vmem_call(
        scores_kernel,
        jax.ShapeDtypeStruct((words, tokens), BF16),
        own,
        swapped(own, "core"),
        place=place,
        weights=weights,
        scratch=[
            pltpu.VMEM((tokens, feats), BF16),
            pltpu.VMEM((STRIPS, words, feats // STRIPS), BF16),
            pltpu.VMEM((words, tokens), F32),
            pltpu.SemaphoreType.DMA((STRIPS,)),
        ],
    )


def total(parts):
    parts = list(parts)
    while len(parts) > 1:
        parts = [a + b for a, b in zip(parts[::2], parts[1::2])]
    return parts[0]


def merge(parts):
    peak = functools.reduce(jnp.maximum, [p[0:1] for p in parts])
    mass = total([p[1:2] * jnp.exp(p[0:1] - peak) for p in parts])
    return peak, mass, total([p[2:3] for p in parts])


def pair_kernel(mine, other, out):
    merged = merge([mine[...], other[...]])
    for copy in range(out.shape[0]):
        for row in range(3):
            out[copy, row : row + 1] = merged[row]


def chips_kernel(parts, out):
    merged = merge([parts[i] for i in range(parts.shape[0])])
    for copy in range(out.shape[0]):
        for row in range(3):
            out[copy, row : row + 1] = merged[row]


def planes_kernel(parts, out):
    for group in range(2):
        peak, mass, label = merge([parts[4 * group + i] for i in range(4)])
        out[group : group + 1] = peak + jnp.log(mass)
    out[2:3] = label


def grads_kernel(place_ref, weights, grads, extra, keep, send, turned, held, sems):
    core = place_ref[0]
    tokens = grads.shape[1]
    chips, _, wide = keep.shape
    copies = strips_of(weights, held, sems)
    turned[...] = grads[...].T
    per_strip = chips // STRIPS
    for chip in range(chips):
        strip, at = chip // per_strip, (chip % per_strip) * 2 * wide
        if at == 0:
            copies[strip].wait()
        full = jnp.dot(
            turned[...], held[strip, :, at : at + 2 * wide], preferred_element_type=F32
        )
        low = full[:, :wide]
        high = full[:, wide:]
        keep[chip, :tokens] = jnp.where(core == 0, low, high)
        send[chip, :tokens] = jnp.where(core == 0, high, low)
        keep[chip, tokens:] = extra[...]
        send[chip, tokens:] = extra[...]


def split_grads(place, weights, grads, extra):
    words, tokens = grads.shape
    feats = weights.shape[1]
    wide = extra.shape[1]
    part = jax.ShapeDtypeStruct((feats // (2 * wide), tokens + EXTRA, wide), F32)
    return vmem_call(
        grads_kernel,
        [part] * 2,
        grads,
        extra,
        place=place,
        weights=weights,
        scratch=[
            pltpu.VMEM((tokens, words), BF16),
            pltpu.VMEM((STRIPS, words, feats // STRIPS), BF16),
            pltpu.SemaphoreType.DMA((STRIPS,)),
        ],
    )


def pair_sum_kernel(keep, got, out):
    out[...] = keep[...] + got[...]


def last_split_kernel(lower, upper, out):
    rows = lower.shape[1] - EXTRA
    part = rows // 4
    chips = lower.shape[0]
    tail = [total([half[i, rows:] for i in range(chips)]) for half in (lower, upper)]
    for plane in range(8):
        half = lower if plane < 4 else upper
        at = slice((plane % 4) * part, (plane % 4 + 1) * part)
        out[plane, :part] = total([half[i, at] for i in range(chips)])
        out[plane, part : part + EXTRA] = tail[0]
        out[plane, part + EXTRA :] = tail[1]


def shards(hidden, head_weight, labels, loss_mask):
    weights = head_weight[0]
    words, feats = weights.shape
    place = jnp.stack([lax.axis_index(a) for a in ("core", "tok")]).astype(jnp.int32)
    first_word = lax.axis_index(("y", "x", "core", "tok")) * words
    word_ids = first_word + lax.broadcasted_iota(jnp.int32, (words, 1), 0)
    mask = loss_mask.astype(F32)

    block = hidden[0]
    rows, wide = block.shape
    half = 2 * rows
    array = jax.ShapeDtypeStruct
    turns = [
        lax.ppermute(block, "tok", [(i, (i + k) % 4) for i in range(4)]) for k in range(1, 4)
    ]
    halves = vmem_call(
        order_tok_kernel,
        [array((16, half, wide), BF16)] * 2,
        block,
        *turns,
        place=place,
        scratch=[pltpu.VMEM((4, rows, wide), BF16)],
    )

    own_z, sent = [], []
    for c in range(2):
        x = halves[c]
        if c == 1:
            x, own_z[0] = lax.optimization_barrier((x, own_z[0]))
        own_z.append(scores(place, weights, exchanged(x, CHIPS)))
        sent.append(lax.ppermute(own_z[c], "grp", [(0, 1)]))

    hits = [word_ids == labels[c * half : (c + 1) * half][None, :] for c in range(2)]
    stats = []
    for c in range(2):
        z = own_z[c].astype(F32)
        peak = jnp.max(z, axis=0)
        stats.append(
            jnp.stack(
                [
                    peak,
                    jnp.sum(jnp.exp(z - peak), axis=0),
                    jnp.sum(jnp.where(hits[c], z, 0.0), axis=0),
                ]
            )
        )
    stats = jnp.concatenate(stats, axis=1)
    stats = vmem_call(
        pair_kernel, array((16,) + stats.shape, F32), stats, swapped(stats, "core")
    )
    stats = vmem_call(
        chips_kernel, array((8,) + stats.shape[1:], F32), exchanged(stats, CHIPS)
    )
    norms = vmem_call(planes_kernel, array(stats.shape[1:], F32), exchanged(stats, PLANES))
    teacher_norm, student_norm, label_logit = norms

    parts = []
    for c in range(2):
        span = slice(c * half, (c + 1) * half)
        teacher_logp = sent[c].astype(F32) - teacher_norm[span]
        student_logp = own_z[c].astype(F32) - student_norm[span]
        teacher_prob = jnp.exp(teacher_logp)
        student_prob = jnp.exp(student_logp)
        diverge = jnp.sum(teacher_prob * (teacher_logp - student_logp), axis=0)
        grads = (
            (2.0 * student_prob - teacher_prob - hits[c].astype(F32)) * mask[span]
        ).astype(BF16)
        extra = jnp.zeros((EXTRA, wide), F32).at[:2].set(diverge.reshape(2, wide))
        parts.append(split_grads(place, weights, grads, extra))
    summed = []
    for keep, send in parts:
        paired = vmem_call(
            pair_sum_kernel, array(keep.shape, F32), keep, swapped_in_student(send)
        )
        summed.append(exchanged(paired, CHIPS))

    part = half // 4
    last = vmem_call(
        last_split_kernel, array((8, part + 2 * EXTRA, wide), F32), *summed
    )
    mine = total(list(exchanged(last, PLANES))[4:])
    input_grads = mine[:part].astype(BF16)
    diverged = jnp.concatenate([mine[part : part + 2], mine[part + EXTRA : part + EXTRA + 2]])
    token_loss = mask * (diverged.reshape(-1) + student_norm - label_logit)
    return (input_grads, token_loss, jnp.stack([teacher_norm, student_norm]))


def solution(mesh):
    fine = Mesh(mesh.devices.reshape(2, 4, 4, 2, 4), ("grp", "y", "x", "core", "tok"))
    vocab = ("y", "x", "core")
    return jax.shard_map(
        shards,
        mesh=fine,
        in_specs=(
            P("grp", "tok", vocab),
            P("grp", vocab + ("tok",), None),
            P(),
            P(),
        ),
        out_specs=(P(("grp", "tok"), vocab), P(), P()),
        check_vma=False,
    )
```

time: 1680 us -> 259 us (0.15); the launches traced: 1660 us -> 258 us
  blocking collectives: 1490 us -> 78 us
  starting transfers between devices: 7.14 us -> 57.1 us
  Pallas kernels: 0 us -> 37 us
  waiting for transfers between devices: 94.3 us -> 73.2 us
  local copies, waits for them, and re-layouts: 27.1 us -> 7.5 us
  matrix products: 18.4 us -> 0 us
    psum x2 -> x0, blocking collectives: 1160 us -> none  [the longest x1 819 us: shards(): summed = lax.psum(partial_value, ('vocab', 'tok'))]
    pmax x1 -> x0, blocking collectives: 317 us -> none  [shards(): lax.pmax((jnp.max(teacher_z, axis=0), jnp.max(student_z, axis=0)), ('voca...]
    all_to_all x0 -> x3, blocking collectives: none -> 78 us  [exchanged(): return lax.all_to_all(x, axes, 0, 0)]
    all_gather x1 -> x0, waiting for transfers between devices: 54.9 us -> none  [shards(): lax.all_gather(token_rows, 'vocab', axis=1, tiled=True)]
    all_to_all x0 -> x4, waiting for transfers between devices: none -> 50.8 us  [exchanged(): return lax.all_to_all(x, axes, 0, 0)]
    all_to_all x0 -> x4, starting transfers between devices: none -> 38.8 us  [exchanged(): return lax.all_to_all(x, axes, 0, 0)]
    pallas_call x0 -> x11, Pallas kernels: none -> 37 us  [vmem_call(): pl.pallas_call(kernel, out_shape=out_shape, in_specs=[in_smem()] * len(sc...]
    dot_general x2 -> x0, matrix products: 18.4 us -> none  [the longest x1 10.1 us: shards(): lax.dot_general(weights, lax.all_gather(token_rows, 'vocab', axis=1, tile...]
  transfers between devices with their start and end apart: 3 -> 14, of which waited for: 3 -> 10; matrix products, arithmetic and copies ran while one was open for 1% -> 1% of each run, Pallas kernels for 0% -> 8%
where the time goes in v2:
time: 259 us; the launch traced here: 258 us
  blocking collectives  78 us (30%)
  waiting for transfers between devices  73.2 us (28%)
  starting transfers between devices  57.1 us (22%)
  Pallas kernels  37 us (14%)
  local copies, waits for them, and re-layouts  7.5 us (3%)
  other arithmetic  4.23 us (2%)
    all_to_all x3, blocking collectives, exchanged(): return lax.all_to_all(x, axes, 0, 0)  78 us
    all_to_all x4, waiting for transfers between devices, exchanged(): return lax.all_to_all(x, axes, 0, 0)  50.8 us
    all_to_all x4, starting transfers between devices, exchanged(): return lax.all_to_all(x, axes, 0, 0)  38.8 us
    pallas_call x11, Pallas kernels, vmem_call(): pl.pallas_call(kernel, out_shape=out_shape, in_specs=[in_smem()] * len(sc...  37 us
    ppermute x2, waiting for transfers between devices, shards(): sent.append(lax.ppermute(own_z[c], 'grp', [(0, 1)]))  13.6 us
    ppermute x2, starting transfers between devices, shards(): sent.append(lax.ppermute(own_z[c], 'grp', [(0, 1)]))  11 us
    unnamed x14, local copies, waits for them, and re-layouts  6.25 us
    ppermute x3, starting transfers between devices, shards(): lax.ppermute(block, 'tok', [(i, (i + k) % 4) for i in range(4)])  5.37 us
  transfers between devices with their start and end apart: 14, of which 10 were waited for; matrix products, arithmetic and copies ran while one was open for 1% of the time, Pallas kernels for 8%

profile of v2, /device:TPU:2, one launch (start us, length us, event | category | flops | bytes accessed | tf_op | source)
XLA Modules:
  0.0 257.9 jit_solution(12720953868545677511)
XLA Ops:
  0.6 4.7 %collective-permute-start.2 = (bf16[128,128]{1,0:T(8,128)(2,1)}, bf16[128,128]{1,0:T(8,128)(2,1)S(1)}, u32[]{:S(2)}, u32[]{:S(2)}) collective-permute-start(bf16[128,128]{1,0:T(8,128)(2,1)} %bitcast.32), channel_id=1, source_target_pairs={{0,3},{1,0},{2,1},{3,2},{4,7},{5,4},{6,5},{7,6},{8,11},{9,8},{10,9... | collective-permute-start | bytes 98312 | tf_op jit(solution)/shard_map/ppermute | solution.py:241
  7.2 3.1 %collective-permute-done.1.p2 = bf16[128,128]{1,0:T(8,128)(2,1)S(1)} collective-permute-done((bf16[128,128]{1,0:T(8,128)(2,1)}, bf16[128,128]{1,0:T(8,128)(2,1)S(1)}, u32[]{:S(2)}, u32[]{:S(2)}) %collective-permute-start.1) | collective-permute-done | bytes 32800 | tf_op jit(solution)/shard_map/ppermute | solution.py:241
  12.8 22.0 %all_to_all.35.own = bf16[16,256,128]{2,1,0:T(8,128)(2,1)S(1)} all-to-all(bf16[16,256,128]{2,1,0:T(8,128)(2,1)S(1)} %get-tuple-element.36), channel_id=1, replica_groups=mesh['grp'=2,'y'=4,'x'=4,'core'=2,'tok'=4] {'y','x'}, dimensions={0} | all-to-all | bytes 2097152 | tf_op jit(solution)/shard_map/all_to_all | solution.py:50
  34.9 2.7 %collective-permute-done.3.sibling = bf16[16,256,128]{2,1,0:T(8,128)(2,1)S(1)} collective-permute-done((bf16[16,256,128]{2,1,0:T(8,128)(2,1)S(1)}, bf16[16,256,128]{2,1,0:T(8,128)(2,1)S(1)}, u32[]{:S(2)}, u32[]{:S(2)}) %collective-permute-start.3) | collective-permute-done | bytes 1048608 | tf_op jit(solution)/shard_map/ppermute | solution.py:42
  37.6 5.6 %shard_map.68 = bf16[1187,256]{1,0:T(8,128)(2,1)S(1)} custom-call(s32[2]{0:T(128)S(1)} %pad_add_fusion.place_ref, bf16[1187,4096]{1,0:T(8,128)(2,1)} %bitcast.36, bf16[16,256,128]{2,1,0:T(8,128)(2,1)S(1)} %all_to_all.35.own, bf16[16,256,128]{2,1,0:T(8,128)(2,1)S(1)} %collective-permute-done.3.sibling), custom_call_target="tpu_custom_call" | custom-call | tf_op jit(solution)/shard_map/pallas_call | solution.py:29
  43.2 20.3 %all_to_all.36.own = bf16[16,256,128]{2,1,0:T(8,128)(2,1)S(1)} all-to-all(bf16[16,256,128]{2,1,0:T(8,128)(2,1)S(1)} %get-tuple-element.38), channel_id=1, replica_groups=mesh['grp'=2,'y'=4,'x'=4,'core'=2,'tok'=4] {'y','x'}, dimensions={0} | all-to-all | bytes 2097152 | tf_op jit(solution)/shard_map/all_to_all | solution.py:50
  63.5 7.4 %collective-permute-start.6 = (bf16[1187,256]{1,0:T(8,128)(2,1)S(1)}, bf16[1187,256]{1,0:T(8,128)(2,1)}, u32[]{:S(2)}, u32[]{:S(2)}) collective-permute-start(bf16[1187,256]{1,0:T(8,128)(2,1)S(1)} %shard_map.68), channel_id=1, source_target_pairs={{0,128},{1,129},{2,130},{3,131},{4,132},{5,133},{6,134},{7,135},{8... | collective-permute-start | bytes 1823240 | tf_op jit(solution)/shard_map/ppermute | solution.py:258
  71.1 5.6 %shard_map.69 = bf16[1187,256]{1,0:T(8,128)(2,1)S(1)} custom-call(s32[2]{0:T(128)S(1)} %pad_add_fusion.place_ref, bf16[1187,4096]{1,0:T(8,128)(2,1)} %bitcast.37, bf16[16,256,128]{2,1,0:T(8,128)(2,1)S(1)} %all_to_all.36.own, bf16[16,256,128]{2,1,0:T(8,128)(2,1)S(1)} %collective-permute-done.4.sibling), custom_call_target="tpu_custom_call" | custom-call | tf_op jit(solution)/shard_map/pallas_call | solution.py:29
  79.5 4.8 %all-to-all-start.2 = ((f32[16,3,512]{2,1,0:T(4,128)}), f32[16,3,512]{2,1,0:T(4,128)S(1)}, u32[]{:S(2)}, u32[]{:S(2)}) async-start(f32[16,3,512]{2,1,0:T(4,128)} %shard_map.70), calls=%async_computation.2 | async-start | bytes 262144 | tf_op jit(solution)/shard_map/all_to_all | solution.py:50
  84.3 6.7 %all-to-all-done.2.parts = f32[16,3,512]{2,1,0:T(4,128)S(1)} async-done(((f32[16,3,512]{2,1,0:T(4,128)}), f32[16,3,512]{2,1,0:T(4,128)S(1)}, u32[]{:S(2)}, u32[]{:S(2)}) %all-to-all-start.2) | async-done | bytes 98336 | tf_op jit(solution)/shard_map/all_to_all | solution.py:50
  91.7 3.5 %all-to-all-start.3 = ((f32[8,3,512]{2,1,0:T(4,128)}), f32[8,3,512]{2,1,0:T(4,128)S(1)}, u32[]{:S(2)}, u32[]{:S(2)}) async-start(f32[8,3,512]{2,1,0:T(4,128)} %shard_map.71), calls=%async_computation.3 | async-start | bytes 131072 | tf_op jit(solution)/shard_map/all_to_all | solution.py:50
  95.2 8.1 %all-to-all-done.3.parts = f32[8,3,512]{2,1,0:T(4,128)S(1)} async-done(((f32[8,3,512]{2,1,0:T(4,128)}), f32[8,3,512]{2,1,0:T(4,128)S(1)}, u32[]{:S(2)}, u32[]{:S(2)}) %all-to-all-start.3) | async-done | bytes 49184 | tf_op jit(solution)/shard_map/all_to_all | solution.py:50
  105.2 7.0 %shard_map.73 = (f32[16,264,128]{2,1,0:T(8,128)S(1)}, f32[16,264,128]{2,1,0:T(8,128)}) custom-call(s32[2]{0:T(128)S(1)} %pad_add_fusion.place_ref, bf16[1187,4096]{1,0:T(8,128)(2,1)} %bitcast.38, bf16[1187,256]{1,0:T(8,128)(2,1)S(1)} %get-tuple-element.50.grads, f32[8,128]{1,0:T(8,128)S(1)} %scatter.6.extra), custom_call_target="tpu_custom_call" | custom-call | tf_op jit(solution)/shard_map/pallas_call | solution.py:29
  114.4 3.6 %collective-permute-start.8 = (bf16[1187,256]{1,0:T(8,128)(2,1)S(1)}, bf16[1187,256]{1,0:T(8,128)(2,1)S(1)}, u32[]{:S(2)}, u32[]{:S(2)}) collective-permute-start(bf16[1187,256]{1,0:T(8,128)(2,1)S(1)} %shard_map.69), channel_id=1, source_target_pairs={{0,128},{1,129},{2,130},{3,131},{4,132},{5,133},{6,134},{7,135},{8... | collective-permute-start | bytes 1823240 | tf_op jit(solution)/shard_map/ppermute | solution.py:258
  117.9 13.6 %collective-permute-done.8 = bf16[1187,256]{1,0:T(8,128)(2,1)S(1)} collective-permute-done((bf16[1187,256]{1,0:T(8,128)(2,1)S(1)}, bf16[1187,256]{1,0:T(8,128)(2,1)S(1)}, u32[]{:S(2)}, u32[]{:S(2)}) %collective-permute-start.8) | collective-permute-done | bytes 607776 | tf_op jit(solution)/shard_map/ppermute | solution.py:258
  132.3 7.1 %shard_map.75 = (f32[16,264,128]{2,1,0:T(8,128)S(1)}, f32[16,264,128]{2,1,0:T(8,128)}) custom-call(s32[2]{0:T(128)S(1)} %pad_add_fusion.place_ref, bf16[1187,4096]{1,0:T(8,128)(2,1)} %bitcast.39, bf16[1187,256]{1,0:T(8,128)(2,1)S(1)} %get-tuple-element.48.grads, f32[8,128]{1,0:T(8,128)S(1)} %scatter.9.extra), custom_call_target="tpu_custom_call" | custom-call | tf_op jit(solution)/shard_map/pallas_call | solution.py:29
  143.0 3.8 %shard_map.74 = f32[16,264,128]{2,1,0:T(8,128)} custom-call(f32[16,264,128]{2,1,0:T(8,128)} %copy-done, f32[16,264,128]{2,1,0:T(8,128)} %copy-done.3), custom_call_target="tpu_custom_call" | custom-call | tf_op jit(solution)/shard_map/pallas_call | solution.py:29
  146.8 5.6 %all-to-all-start.4 = ((f32[16,264,128]{2,1,0:T(8,128)}), f32[16,264,128]{2,1,0:T(8,128)}, u32[]{:S(2)}, u32[]{:S(2)}) async-start(f32[16,264,128]{2,1,0:T(8,128)} %shard_map.74), calls=%async_computation.4 | async-start | bytes 4325376 | tf_op jit(solution)/shard_map/all_to_all | solution.py:50
  153.9 2.5 shard_map.76
  156.3 24.4 %all-to-all-done.4.lower = f32[16,264,128]{2,1,0:T(8,128)} async-done(((f32[16,264,128]{2,1,0:T(8,128)}), f32[16,264,128]{2,1,0:T(8,128)}, u32[]{:S(2)}, u32[]{:S(2)}) %all-to-all-start.4) | async-done | bytes 2162720 | tf_op jit(solution)/shard_map/all_to_all | solution.py:50
  180.8 35.6 %all_to_all.37.upper = f32[16,264,128]{2,1,0:T(8,128)} all-to-all(f32[16,264,128]{2,1,0:T(8,128)S(1)} %shard_map.76), channel_id=1, replica_groups=mesh['grp'=2,'y'=4,'x'=4,'core'=2,'tok'=4] {'y','x'}, dimensions={0} | all-to-all | bytes 4325376 | tf_op jit(solution)/shard_map/all_to_all | solution.py:50
  216.4 3.2 %shard_map.77 = f32[8,80,128]{2,1,0:T(8,128)} custom-call(f32[16,264,128]{2,1,0:T(8,128)} %all-to-all-done.4.lower, f32[16,264,128]{2,1,0:T(8,128)} %all_to_all.37.upper), custom_call_target="tpu_custom_call" | custom-call | tf_op jit(solution)/shard_map/pallas_call | solution.py:29
  219.6 24.9 %all-to-all-start.6 = ((f32[8,80,128]{2,1,0:T(8,128)}), f32[8,80,128]{2,1,0:T(8,128)S(1)}, u32[]{:S(2)}, u32[]{:S(2)}) async-start(f32[8,80,128]{2,1,0:T(8,128)} %shard_map.77), calls=%async_computation.6 | async-start | bytes 655360 | tf_op jit(solution)/shard_map/all_to_all | solution.py:50
  245.1 11.6 %all-to-all-done.6 = f32[8,80,128]{2,1,0:T(8,128)S(1)} async-done(((f32[8,80,128]{2,1,0:T(8,128)}), f32[8,80,128]{2,1,0:T(8,128)S(1)}, u32[]{:S(2)}, u32[]{:S(2)}) %all-to-all-start.6) | async-done | bytes 327712 | tf_op jit(solution)/shard_map/all_to_all | solution.py:50
  (54 shorter events, 19.5 us)
Async XLA Ops:
  0.6 6.6 %collective-permute-start.2 = (bf16[128,128]{1,0:T(8,128)(2,1)}, bf16[128,128]{1,0:T(8,128)(2,1)S(1)}, u32[]{:S(2)}, u32[]{:S(2)}) collective-permute-start(bf16[128,128]{1,0:T(8,128)(2,1)} %bitcast.32), channel_id=1, source_target_pairs={{0,3},{1,0},{2,1},{3,2},{4,7},{5,4},{6,5},{7,6},{8,11},{9,8},{10,9... | collective-permute-start | bytes 98312 | tf_op jit(solution)/shard_map/ppermute | solution.py:241
  5.3 5.0 %collective-permute-start.1 = (bf16[128,128]{1,0:T(8,128)(2,1)}, bf16[128,128]{1,0:T(8,128)(2,1)S(1)}, u32[]{:S(2)}, u32[]{:S(2)}) collective-permute-start(bf16[128,128]{1,0:T(8,128)(2,1)} %bitcast.33), channel_id=1, source_target_pairs={{0,2},{1,3},{2,0},{3,1},{4,6},{5,7},{6,4},{7,5},{8,10},{9,11},{10,... | collective-permute-start | bytes 98312 | tf_op jit(solution)/shard_map/ppermute | solution.py:241
  5.3 5.9 %collective-permute-start = (bf16[128,128]{1,0:T(8,128)(2,1)}, bf16[128,128]{1,0:T(8,128)(2,1)S(1)}, u32[]{:S(2)}, u32[]{:S(2)}) collective-permute-start(bf16[128,128]{1,0:T(8,128)(2,1)} %bitcast.34), channel_id=1, source_target_pairs={{0,1},{1,2},{2,3},{3,0},{4,5},{5,6},{6,7},{7,4},{8,9},{9,10},{10,1... | collective-permute-start | bytes 98312 | tf_op jit(solution)/shard_map/ppermute | solution.py:241
  11.3 0.8 copy-start.2
  34.9 2.7 %collective-permute-start.3 = (bf16[16,256,128]{2,1,0:T(8,128)(2,1)S(1)}, bf16[16,256,128]{2,1,0:T(8,128)(2,1)S(1)}, u32[]{:S(2)}, u32[]{:S(2)}) collective-permute-start(bf16[16,256,128]{2,1,0:T(8,128)(2,1)S(1)} %all_to_all.35.own), channel_id=1, source_target_pairs={{0,4},{4,0},{1,5},{5,1},{2,6},{6,2},{3,7},{7,3},{8,12},{12,8},{9,1... | collective-permute-start | bytes 3145736 | tf_op jit(solution)/shard_map/ppermute | solution.py:42
  43.1 20.3 %copy-start.6 = (s32[512]{0:T(512)S(1)}, s32[512]{0:T(512)}, u32[]{:S(2)}) copy-start(s32[512]{0:T(512)} %param.10) | copy-start | bytes 6148
  63.5 7.6 %collective-permute-start.4 = (bf16[16,256,128]{2,1,0:T(8,128)(2,1)S(1)}, bf16[16,256,128]{2,1,0:T(8,128)(2,1)S(1)}, u32[]{:S(2)}, u32[]{:S(2)}) collective-permute-start(bf16[16,256,128]{2,1,0:T(8,128)(2,1)S(1)} %all_to_all.36.own), channel_id=1, source_target_pairs={{0,4},{4,0},{1,5},{5,1},{2,6},{6,2},{3,7},{7,3},{8,12},{12,8},{9,1... | collective-permute-start | bytes 3145736 | tf_op jit(solution)/shard_map/ppermute | solution.py:42
  63.5 39.9 %collective-permute-start.6 = (bf16[1187,256]{1,0:T(8,128)(2,1)S(1)}, bf16[1187,256]{1,0:T(8,128)(2,1)}, u32[]{:S(2)}, u32[]{:S(2)}) collective-permute-start(bf16[1187,256]{1,0:T(8,128)(2,1)S(1)} %shard_map.68), channel_id=1, source_target_pairs={{0,128},{1,129},{2,130},{3,131},{4,132},{5,133},{6,134},{7,135},{8... | collective-permute-start | bytes 1823240 | tf_op jit(solution)/shard_map/ppermute | solution.py:258
  76.7 7.6 %copy-start.5 = (s32[512]{0:T(512)S(1)}, s32[512]{0:T(512)}, u32[]{:S(2)}) copy-start(s32[512]{0:T(512)} %param.11) | copy-start | bytes 6148
  77.6 1.3 collective-permute-start.5
  79.5 11.5 %all-to-all-start.2 = ((f32[16,3,512]{2,1,0:T(4,128)}), f32[16,3,512]{2,1,0:T(4,128)S(1)}, u32[]{:S(2)}, u32[]{:S(2)}) async-start(f32[16,3,512]{2,1,0:T(4,128)} %shard_map.70), calls=%async_computation.2 | async-start | bytes 262144 | tf_op jit(solution)/shard_map/all_to_all | solution.py:50
  91.7 11.7 %all-to-all-start.3 = ((f32[8,3,512]{2,1,0:T(4,128)}), f32[8,3,512]{2,1,0:T(4,128)S(1)}, u32[]{:S(2)}, u32[]{:S(2)}) async-start(f32[8,3,512]{2,1,0:T(4,128)} %shard_map.71), calls=%async_computation.3 | async-start | bytes 131072 | tf_op jit(solution)/shard_map/all_to_all | solution.py:50
  112.2 1.3 copy-start
  113.6 28.0 %collective-permute-start.7 = (f32[16,264,128]{2,1,0:T(8,128)}, f32[16,264,128]{2,1,0:T(8,128)S(1)}, u32[]{:S(2)}, u32[]{:S(2)}) collective-permute-start(f32[16,264,128]{2,1,0:T(8,128)} %get-tuple-element.40), channel_id=1, source_target_pairs={{128,132},{132,128},{129,133},{133,129},{130,134},{134,130},{131,1... | collective-permute-start | bytes 6488072 | tf_op jit(solution)/shard_map/ppermute | solution.py:46
  114.4 17.2 %collective-permute-start.8 = (bf16[1187,256]{1,0:T(8,128)(2,1)S(1)}, bf16[1187,256]{1,0:T(8,128)(2,1)S(1)}, u32[]{:S(2)}, u32[]{:S(2)}) collective-permute-start(bf16[1187,256]{1,0:T(8,128)(2,1)S(1)} %shard_map.69), channel_id=1, source_target_pairs={{0,128},{1,129},{2,130},{3,131},{4,132},{5,133},{6,134},{7,135},{8... | collective-permute-start | bytes 1823240 | tf_op jit(solution)/shard_map/ppermute | solution.py:258
  139.4 1.4 copy-start.1
  140.7 11.7 %collective-permute-start.9 = (f32[16,264,128]{2,1,0:T(8,128)}, f32[16,264,128]{2,1,0:T(8,128)S(1)}, u32[]{:S(2)}, u32[]{:S(2)}) collective-permute-start(f32[16,264,128]{2,1,0:T(8,128)} %get-tuple-element.42), channel_id=1, source_target_pairs={{128,132},{132,128},{129,133},{133,129},{130,134},{134,130},{131,1... | collective-permute-start | bytes 6488072 | tf_op jit(solution)/shard_map/ppermute | solution.py:46
  141.6 1.4 copy-start.3
  146.8 34.0 %all-to-all-start.4 = ((f32[16,264,128]{2,1,0:T(8,128)}), f32[16,264,128]{2,1,0:T(8,128)}, u32[]{:S(2)}, u32[]{:S(2)}) async-start(f32[16,264,128]{2,1,0:T(8,128)} %shard_map.74), calls=%async_computation.4 | async-start | bytes 4325376 | tf_op jit(solution)/shard_map/all_to_all | solution.py:50
  152.4 1.4 copy-start.4
  219.6 37.1 %all-to-all-start.6 = ((f32[8,80,128]{2,1,0:T(8,128)}), f32[8,80,128]{2,1,0:T(8,128)S(1)}, u32[]{:S(2)}, u32[]{:S(2)}) async-start(f32[8,80,128]{2,1,0:T(8,128)} %shard_map.77), calls=%async_computation.6 | async-start | bytes 655360 | tf_op jit(solution)/shard_map/all_to_all | solution.py:50

commit v3 on v2

--- a/solution.py
+++ b/solution.py
@@ -8,7 +8,7 @@
 
 BF16 = jnp.bfloat16
 F32 = jnp.float32
-VMEM_LIMIT = 50 * 1024 * 1024
+MIB = 1024 * 1024
 EXTRA = 8
 STRIPS = 4
 CHIPS = ("y", "x")
@@ -23,7 +23,7 @@
     return pl.BlockSpec(memory_space=pltpu.SMEM)
 
 
-def vmem_call(kernel, out_shape, *arrays, place=None, weights=None, scratch=()):
+def vmem_call(kernel, out_shape, *arrays, place=None, weights=None, scratch=(), mib=12):
     scalars = [] if place is None else [place]
     remote = [] if weights is None else [weights]
     return pl.pallas_call(
@@ -34,7 +34,7 @@
         + [in_vmem()] * len(arrays),
         out_specs=jax.tree.map(lambda _: in_vmem(), out_shape),
         scratch_shapes=list(scratch),
-        compiler_params=pltpu.CompilerParams(vmem_limit_bytes=VMEM_LIMIT),
+        compiler_params=pltpu.CompilerParams(vmem_limit_bytes=mib * MIB),
     )(*scalars, *remote, *arrays)
 
 
@@ -129,6 +129,7 @@
             pltpu.VMEM((words, tokens), F32),
             pltpu.SemaphoreType.DMA((STRIPS,)),
         ],
+        mib=22,
     )
 
 
@@ -205,6 +206,7 @@
             pltpu.VMEM((STRIPS, words, feats // STRIPS), BF16),
             pltpu.SemaphoreType.DMA((STRIPS,)),
         ],
+        mib=22,
     )
 
 
@@ -254,7 +256,10 @@
         x = halves[c]
         if c == 1:
             x, own_z[0] = lax.optimization_barrier((x, own_z[0]))
-        own_z.append(scores(place, weights, exchanged(x, CHIPS)))
+        x = exchanged(x, CHIPS)
+        if c == 1:
+            x, sent[0] = lax.optimization_barrier((x, sent[0]))
+        own_z.append(scores(place, weights, x))
         sent.append(lax.ppermute(own_z[c], "grp", [(0, 1)]))
 
     hits = [word_ids == labels[c * half : (c + 1) * half][None, :] for c in range(2)]
@@ -279,6 +284,7 @@
         chips_kernel, array((8,) + stats.shape[1:], F32), exchanged(stats, CHIPS)
     )
     norms = vmem_call(planes_kernel, array(stats.shape[1:], F32), exchanged(stats, PLANES))
+    norms, sent[0], sent[1] = lax.optimization_barrier((norms, sent[0], sent[1]))
     teacher_norm, student_norm, label_logit = norms
 
     parts = []

time: 259 us -> 248 us (0.958)
  blocking collectives: 78 us -> 54.6 us
  local copies, waits for them, and re-layouts: 7.5 us -> 20 us
  starting transfers between devices: 57.1 us -> 66.8 us
  Pallas kernels: 37 us -> 31.3 us
    all_to_all x3 -> x2, blocking collectives: 78 us -> 54.6 us  [exchanged(): return lax.all_to_all(x, axes, 0, 0)]
    unnamed x14 -> x24, local copies, waits for them, and re-layouts: 6.25 us -> 18.7 us
    pallas_call x11, Pallas kernels: 37 us -> 31.3 us  [vmem_call(): pl.pallas_call(kernel, out_shape=out_shape, in_specs=[in_smem()] * len(sc...]
    all_to_all x4 -> x5, starting transfers between devices: 38.8 us -> 44.4 us  [exchanged(): return lax.all_to_all(x, axes, 0, 0)]
    ppermute x2, starting transfers between devices: 11 us -> 15.2 us  [shards(): sent.append(lax.ppermute(own_z[c], 'grp', [(0, 1)]))]
    all_to_all x4 -> x5, waiting for transfers between devices: 50.8 us -> 46.9 us  [exchanged(): return lax.all_to_all(x, axes, 0, 0)]
  transfers between devices with their start and end apart: 14 -> 15, of which waited for: 10 -> 11; matrix products, arithmetic and copies ran while one was open for 1% -> 1% of each run, Pallas kernels for 8% -> 4%
where the time goes in v3:
time: 248 us; the launch traced here: 247 us
  waiting for transfers between devices  70.7 us (29%)
  starting transfers between devices  66.8 us (27%)
  blocking collectives  54.6 us (22%)
  Pallas kernels  31.3 us (13%)
  local copies, waits for them, and re-layouts  20 us (8%)
  other arithmetic  3.16 us (1%)
    all_to_all x2, blocking collectives, exchanged(): return lax.all_to_all(x, axes, 0, 0)  54.6 us
    all_to_all x5, waiting for transfers between devices, exchanged(): return lax.all_to_all(x, axes, 0, 0)  46.9 us
    all_to_all x5, starting transfers between devices, exchanged(): return lax.all_to_all(x, axes, 0, 0)  44.4 us
    pallas_call x11, Pallas kernels, vmem_call(): pl.pallas_call(kernel, out_shape=out_shape, in_specs=[in_smem()] * len(sc...  31.3 us
    unnamed x24, local copies, waits for them, and re-layouts  18.7 us
    ppermute x2, starting transfers between devices, shards(): sent.append(lax.ppermute(own_z[c], 'grp', [(0, 1)]))  15.2 us
    ppermute x2, waiting for transfers between devices, shards(): sent.append(lax.ppermute(own_z[c], 'grp', [(0, 1)]))  13 us
    ppermute x3, waiting for transfers between devices, swapped(): return lax.ppermute(x, axis, [(0, 1), (1, 0)])  5.64 us
  transfers between devices with their start and end apart: 15, of which 11 were waited for; matrix products, arithmetic and copies ran while one was open for 1% of the time, Pallas kernels for 4%

profile of v3, /device:TPU:2, one launch (start us, length us, event | category | flops | bytes accessed | tf_op | source)
XLA Modules:
  0.0 247.4 jit_solution(7838720470011149708)
XLA Ops:
  0.6 4.7 %collective-permute-start.2 = (bf16[128,128]{1,0:T(8,128)(2,1)}, bf16[128,128]{1,0:T(8,128)(2,1)S(1)}, u32[]{:S(2)}, u32[]{:S(2)}) collective-permute-start(bf16[128,128]{1,0:T(8,128)(2,1)} %bitcast.36), channel_id=1, source_target_pairs={{0,3},{1,0},{2,1},{3,2},{4,7},{5,4},{6,5},{7,6},{8,11},{9,8},{10,9... | collective-permute-start | bytes 98312 | tf_op jit(solution)/shard_map/ppermute | solution.py:243
  7.2 3.1 %collective-permute-done.1.p2 = bf16[128,128]{1,0:T(8,128)(2,1)S(1)} collective-permute-done((bf16[128,128]{1,0:T(8,128)(2,1)}, bf16[128,128]{1,0:T(8,128)(2,1)S(1)}, u32[]{:S(2)}, u32[]{:S(2)}) %collective-permute-start.1) | collective-permute-done | bytes 32800 | tf_op jit(solution)/shard_map/ppermute | solution.py:243
  13.8 22.0 %all_to_all.35.own = bf16[16,256,128]{2,1,0:T(8,128)(2,1)S(1)} all-to-all(bf16[16,256,128]{2,1,0:T(8,128)(2,1)S(1)} %get-tuple-element.41), channel_id=1, replica_groups=mesh['grp'=2,'y'=4,'x'=4,'core'=2,'tok'=4] {'y','x'}, dimensions={0} | all-to-all | bytes 2097152 | tf_op jit(solution)/shard_map/all_to_all | solution.py:50
  35.9 2.7 %collective-permute-done.3.sibling = bf16[16,256,128]{2,1,0:T(8,128)(2,1)S(1)} collective-permute-done((bf16[16,256,128]{2,1,0:T(8,128)(2,1)S(1)}, bf16[16,256,128]{2,1,0:T(8,128)(2,1)S(1)}, u32[]{:S(2)}, u32[]{:S(2)}) %collective-permute-start.3) | collective-permute-done | bytes 1048608 | tf_op jit(solution)/shard_map/ppermute | solution.py:42
  38.5 3.8 %copy-done = bf16[1,1187,4096]{2,1,0:T(8,128)(2,1)S(1)} copy-done((bf16[1,1187,4096]{2,1,0:T(8,128)(2,1)S(1)}, bf16[1,1187,4096]{2,1,0:T(8,128)(2,1)}, u32[]{:S(2)}) %copy-start) | copy-done | bytes 9723928
  42.3 5.8 %shard_map.68 = bf16[1187,256]{1,0:T(8,128)(2,1)S(1)} custom-call(s32[2]{0:T(128)S(1)} %pad_add_fusion.place_ref, bf16[1187,4096]{1,0:T(8,128)(2,1)S(1)} %bitcast.32, bf16[16,256,128]{2,1,0:T(8,128)(2,1)S(1)} %all_to_all.35.own, bf16[16,256,128]{2,1,0:T(8,128)(2,1)S(1)} %collective-permute-done.3.sibling), custom_call_target="tpu_custom_call" | custom-call | tf_op jit(solution)/shard_map/pallas_call | solution.py:29
  48.1 4.9 %all-to-all-start.1 = ((bf16[16,256,128]{2,1,0:T(8,128)(2,1)}), bf16[16,256,128]{2,1,0:T(8,128)(2,1)S(1)}, u32[]{:S(2)}, u32[]{:S(2)}) async-start(bf16[16,256,128]{2,1,0:T(8,128)(2,1)} %get-tuple-element.43), calls=%async_computation.1 | async-start | bytes 2097152 | tf_op jit(solution)/shard_map/all_to_all | solution.py:50
  52.9 6.6 %collective-permute-start.4 = (bf16[1187,256]{1,0:T(8,128)(2,1)S(1)}, bf16[1187,256]{1,0:T(8,128)(2,1)S(1)}, u32[]{:S(2)}, u32[]{:S(2)}) collective-permute-start(bf16[1187,256]{1,0:T(8,128)(2,1)S(1)} %shard_map.68), channel_id=1, source_target_pairs={{0,128},{1,129},{2,130},{3,131},{4,132},{5,133},{6,134},{7,135},{8... | collective-permute-start | bytes 1823240 | tf_op jit(solution)/shard_map/ppermute | solution.py:263
  59.6 13.0 %collective-permute-done.4 = bf16[1187,256]{1,0:T(8,128)(2,1)S(1)} collective-permute-done((bf16[1187,256]{1,0:T(8,128)(2,1)S(1)}, bf16[1187,256]{1,0:T(8,128)(2,1)S(1)}, u32[]{:S(2)}, u32[]{:S(2)}) %collective-permute-start.4) | collective-permute-done | bytes 607776 | tf_op jit(solution)/shard_map/ppermute | solution.py:263
  75.2 3.8 %copy-done.1 = bf16[1,1187,4096]{2,1,0:T(8,128)(2,1)S(1)} copy-done((bf16[1,1187,4096]{2,1,0:T(8,128)(2,1)S(1)}, bf16[1,1187,4096]{2,1,0:T(8,128)(2,1)}, u32[]{:S(2)}) %copy-start.1) | copy-done | bytes 9723928
  79.0 5.8 %shard_map.69 = bf16[1187,256]{1,0:T(8,128)(2,1)S(1)} custom-call(s32[2]{0:T(128)S(1)} %pad_add_fusion.place_ref, bf16[1187,4096]{1,0:T(8,128)(2,1)S(1)} %bitcast.33, bf16[16,256,128]{2,1,0:T(8,128)(2,1)S(1)} %all-to-all-done.1.own, bf16[16,256,128]{2,1,0:T(8,128)(2,1)S(1)} %collective-permute-done.5.sibling), custom_call_target="tpu_custom_call" | custom-call | tf_op jit(solution)/shard_map/pallas_call | solution.py:29
  84.9 8.6 %collective-permute-start.7 = (bf16[1187,256]{1,0:T(8,128)(2,1)S(1)}, bf16[1187,256]{1,0:T(8,128)(2,1)S(1)}, u32[]{:S(2)}, u32[]{:S(2)}) collective-permute-start(bf16[1187,256]{1,0:T(8,128)(2,1)S(1)} %shard_map.69), channel_id=1, source_target_pairs={{0,128},{1,129},{2,130},{3,131},{4,132},{5,133},{6,134},{7,135},{8... | collective-permute-start | bytes 1823240 | tf_op jit(solution)/shard_map/ppermute | solution.py:263
  96.3 7.3 %all-to-all-start.2 = ((f32[16,3,512]{2,1,0:T(4,128)}), f32[16,3,512]{2,1,0:T(4,128)S(1)}, u32[]{:S(2)}, u32[]{:S(2)}) async-start(f32[16,3,512]{2,1,0:T(4,128)} %shard_map.70), calls=%async_computation.2 | async-start | bytes 262144 | tf_op jit(solution)/shard_map/all_to_all | solution.py:50
  103.6 6.6 %all-to-all-done.2.parts = f32[16,3,512]{2,1,0:T(4,128)S(1)} async-done(((f32[16,3,512]{2,1,0:T(4,128)}), f32[16,3,512]{2,1,0:T(4,128)S(1)}, u32[]{:S(2)}, u32[]{:S(2)}) %all-to-all-start.2) | async-done | bytes 98336 | tf_op jit(solution)/shard_map/all_to_all | solution.py:50
  110.9 15.4 %all-to-all-start.3 = ((f32[8,3,512]{2,1,0:T(4,128)}), f32[8,3,512]{2,1,0:T(4,128)S(1)}, u32[]{:S(2)}, u32[]{:S(2)}) async-start(f32[8,3,512]{2,1,0:T(4,128)} %shard_map.71), calls=%async_computation.3 | async-start | bytes 131072 | tf_op jit(solution)/shard_map/all_to_all | solution.py:50
  126.4 8.4 %all-to-all-done.3.parts = f32[8,3,512]{2,1,0:T(4,128)S(1)} async-done(((f32[8,3,512]{2,1,0:T(4,128)}), f32[8,3,512]{2,1,0:T(4,128)S(1)}, u32[]{:S(2)}, u32[]{:S(2)}) %all-to-all-start.3) | async-done | bytes 49184 | tf_op jit(solution)/shard_map/all_to_all | solution.py:50
  135.5 3.8 %copy-done.2 = bf16[1,1187,4096]{2,1,0:T(8,128)(2,1)S(1)} copy-done((bf16[1,1187,4096]{2,1,0:T(8,128)(2,1)S(1)}, bf16[1,1187,4096]{2,1,0:T(8,128)(2,1)}, u32[]{:S(2)}) %copy-start.2) | copy-done | bytes 9723928
  139.3 5.5 %shard_map.73 = (f32[16,264,128]{2,1,0:T(8,128)S(1)}, f32[16,264,128]{2,1,0:T(8,128)S(1)}) custom-call(s32[2]{0:T(128)S(1)} %pad_add_fusion.place_ref, bf16[1187,4096]{1,0:T(8,128)(2,1)S(1)} %bitcast.34, bf16[1187,256]{1,0:T(8,128)(2,1)S(1)} %get-tuple-element.60.grads, f32[8,128]{1,0:T(8,128)S(1)} %scatter.6.extra), custom_call_target="tpu_custom_call" | custom-call | tf_op jit(solution)/shard_map/pallas_call | solution.py:29
  146.3 6.9 %shard_map.75 = (f32[16,264,128]{2,1,0:T(8,128)S(1)}, f32[16,264,128]{2,1,0:T(8,128)}) custom-call(s32[2]{0:T(128)S(1)} %pad_add_fusion.place_ref, bf16[1187,4096]{1,0:T(8,128)(2,1)S(1)} %bitcast.35, bf16[1187,256]{1,0:T(8,128)(2,1)S(1)} %get-tuple-element.58.grads, f32[8,128]{1,0:T(8,128)S(1)} %scatter.9.extra), custom_call_target="tpu_custom_call" | custom-call | tf_op jit(solution)/shard_map/pallas_call | solution.py:29
  156.9 5.6 %all-to-all-start.4 = ((f32[16,264,128]{2,1,0:T(8,128)}), f32[16,264,128]{2,1,0:T(8,128)}, u32[]{:S(2)}, u32[]{:S(2)}) async-start(f32[16,264,128]{2,1,0:T(8,128)} %shard_map.74), calls=%async_computation.4 | async-start | bytes 4325376 | tf_op jit(solution)/shard_map/all_to_all | solution.py:50
  167.4 21.2 %all-to-all-done.4.lower = f32[16,264,128]{2,1,0:T(8,128)} async-done(((f32[16,264,128]{2,1,0:T(8,128)}), f32[16,264,128]{2,1,0:T(8,128)}, u32[]{:S(2)}, u32[]{:S(2)}) %all-to-all-start.4) | async-done | bytes 2162720 | tf_op jit(solution)/shard_map/all_to_all | solution.py:50
  188.6 32.6 %all_to_all.36.upper = f32[16,264,128]{2,1,0:T(8,128)S(1)} all-to-all(f32[16,264,128]{2,1,0:T(8,128)S(1)} %shard_map.76), channel_id=1, replica_groups=mesh['grp'=2,'y'=4,'x'=4,'core'=2,'tok'=4] {'y','x'}, dimensions={0} | all-to-all | bytes 4325376 | tf_op jit(solution)/shard_map/all_to_all | solution.py:50
  223.7 11.2 %all-to-all-start.6 = ((f32[8,80,128]{2,1,0:T(8,128)}), f32[8,80,128]{2,1,0:T(8,128)S(1)}, u32[]{:S(2)}, u32[]{:S(2)}) async-start(f32[8,80,128]{2,1,0:T(8,128)} %shard_map.77), calls=%async_computation.6 | async-start | bytes 655360 | tf_op jit(solution)/shard_map/all_to_all | solution.py:50
  235.5 10.7 %all-to-all-done.6 = f32[8,80,128]{2,1,0:T(8,128)S(1)} async-done(((f32[8,80,128]{2,1,0:T(8,128)}), f32[8,80,128]{2,1,0:T(8,128)S(1)}, u32[]{:S(2)}, u32[]{:S(2)}) %all-to-all-start.6) | async-done | bytes 327712 | tf_op jit(solution)/shard_map/all_to_all | solution.py:50
  (65 shorter events, 26.9 us)
Async XLA Ops:
  0.6 6.6 %collective-permute-start.2 = (bf16[128,128]{1,0:T(8,128)(2,1)}, bf16[128,128]{1,0:T(8,128)(2,1)S(1)}, u32[]{:S(2)}, u32[]{:S(2)}) collective-permute-start(bf16[128,128]{1,0:T(8,128)(2,1)} %bitcast.36), channel_id=1, source_target_pairs={{0,3},{1,0},{2,1},{3,2},{4,7},{5,4},{6,5},{7,6},{8,11},{9,8},{10,9... | collective-permute-start | bytes 98312 | tf_op jit(solution)/shard_map/ppermute | solution.py:243
  5.3 5.0 %collective-permute-start.1 = (bf16[128,128]{1,0:T(8,128)(2,1)}, bf16[128,128]{1,0:T(8,128)(2,1)S(1)}, u32[]{:S(2)}, u32[]{:S(2)}) collective-permute-start(bf16[128,128]{1,0:T(8,128)(2,1)} %bitcast.37), channel_id=1, source_target_pairs={{0,2},{1,3},{2,0},{3,1},{4,6},{5,7},{6,4},{7,5},{8,10},{9,11},{10,... | collective-permute-start | bytes 98312 | tf_op jit(solution)/shard_map/ppermute | solution.py:243
  5.3 5.9 %collective-permute-start = (bf16[128,128]{1,0:T(8,128)(2,1)}, bf16[128,128]{1,0:T(8,128)(2,1)S(1)}, u32[]{:S(2)}, u32[]{:S(2)}) collective-permute-start(bf16[128,128]{1,0:T(8,128)(2,1)} %bitcast.38), channel_id=1, source_target_pairs={{0,1},{1,2},{2,3},{3,0},{4,5},{5,6},{6,7},{7,4},{8,9},{9,10},{10,1... | collective-permute-start | bytes 98312 | tf_op jit(solution)/shard_map/ppermute | solution.py:243
  35.8 2.7 %collective-permute-start.3 = (bf16[16,256,128]{2,1,0:T(8,128)(2,1)S(1)}, bf16[16,256,128]{2,1,0:T(8,128)(2,1)S(1)}, u32[]{:S(2)}, u32[]{:S(2)}) collective-permute-start(bf16[16,256,128]{2,1,0:T(8,128)(2,1)S(1)} %all_to_all.35.own), channel_id=1, source_target_pairs={{0,4},{4,0},{1,5},{5,1},{2,6},{6,2},{3,7},{7,3},{8,12},{12,8},{9,1... | collective-permute-start | bytes 3145736 | tf_op jit(solution)/shard_map/ppermute | solution.py:42
  38.5 3.8 %copy-start = (bf16[1,1187,4096]{2,1,0:T(8,128)(2,1)S(1)}, bf16[1,1187,4096]{2,1,0:T(8,128)(2,1)}, u32[]{:S(2)}) copy-start(bf16[1,1187,4096]{2,1,0:T(8,128)(2,1)} %param.9) | copy-start | bytes 29171716
  48.0 24.5 %copy-start.11 = (s32[512]{0:T(512)S(1)}, s32[512]{0:T(512)}, u32[]{:S(2)}) copy-start(s32[512]{0:T(512)} %param.10) | copy-start | bytes 6148
  48.1 24.5 %all-to-all-start.1 = ((bf16[16,256,128]{2,1,0:T(8,128)(2,1)}), bf16[16,256,128]{2,1,0:T(8,128)(2,1)S(1)}, u32[]{:S(2)}, u32[]{:S(2)}) async-start(bf16[16,256,128]{2,1,0:T(8,128)(2,1)} %get-tuple-element.43), calls=%async_computation.1 | async-start | bytes 2097152 | tf_op jit(solution)/shard_map/all_to_all | solution.py:50
  52.9 19.6 %collective-permute-start.4 = (bf16[1187,256]{1,0:T(8,128)(2,1)S(1)}, bf16[1187,256]{1,0:T(8,128)(2,1)S(1)}, u32[]{:S(2)}, u32[]{:S(2)}) collective-permute-start(bf16[1187,256]{1,0:T(8,128)(2,1)S(1)} %shard_map.68), channel_id=1, source_target_pairs={{0,128},{1,129},{2,130},{3,131},{4,132},{5,133},{6,134},{7,135},{8... | collective-permute-start | bytes 1823240 | tf_op jit(solution)/shard_map/ppermute | solution.py:263
  72.6 2.7 %collective-permute-start.5 = (bf16[16,256,128]{2,1,0:T(8,128)(2,1)S(1)}, bf16[16,256,128]{2,1,0:T(8,128)(2,1)S(1)}, u32[]{:S(2)}, u32[]{:S(2)}) collective-permute-start(bf16[16,256,128]{2,1,0:T(8,128)(2,1)S(1)} %all-to-all-done.1.own), channel_id=1, source_target_pairs={{0,4},{4,0},{1,5},{5,1},{2,6},{6,2},{3,7},{7,3},{8,12},{12,8},{9,1... | collective-permute-start | bytes 3145736 | tf_op jit(solution)/shard_map/ppermute | solution.py:42
  75.2 3.8 %copy-start.1 = (bf16[1,1187,4096]{2,1,0:T(8,128)(2,1)S(1)}, bf16[1,1187,4096]{2,1,0:T(8,128)(2,1)}, u32[]{:S(2)}) copy-start(bf16[1,1187,4096]{2,1,0:T(8,128)(2,1)} %param.9) | copy-start | bytes 29171716
  84.8 18.9 %copy-start.10 = (s32[512]{0:T(512)S(1)}, s32[512]{0:T(512)}, u32[]{:S(2)}) copy-start(s32[512]{0:T(512)} %param.11) | copy-start | bytes 6148
  84.8 50.0 %copy-start.9 = (bf16[1187,256]{1,0:T(8,128)(2,1)S(1)}, bf16[1187,256]{1,0:T(8,128)(2,1)}, u32[]{:S(2)}) copy-start(bf16[1187,256]{1,0:T(8,128)(2,1)} %copy-done.8) | copy-start | bytes 1823236
  84.9 49.8 %collective-permute-start.7 = (bf16[1187,256]{1,0:T(8,128)(2,1)S(1)}, bf16[1187,256]{1,0:T(8,128)(2,1)S(1)}, u32[]{:S(2)}, u32[]{:S(2)}) collective-permute-start(bf16[1187,256]{1,0:T(8,128)(2,1)S(1)} %shard_map.69), channel_id=1, source_target_pairs={{0,128},{1,129},{2,130},{3,131},{4,132},{5,133},{6,134},{7,135},{8... | collective-permute-start | bytes 1823240 | tf_op jit(solution)/shard_map/ppermute | solution.py:263
  94.2 1.4 collective-permute-start.6
  96.3 13.9 %all-to-all-start.2 = ((f32[16,3,512]{2,1,0:T(4,128)}), f32[16,3,512]{2,1,0:T(4,128)S(1)}, u32[]{:S(2)}, u32[]{:S(2)}) async-start(f32[16,3,512]{2,1,0:T(4,128)} %shard_map.70), calls=%async_computation.2 | async-start | bytes 262144 | tf_op jit(solution)/shard_map/all_to_all | solution.py:50
  110.9 23.8 %all-to-all-start.3 = ((f32[8,3,512]{2,1,0:T(4,128)}), f32[8,3,512]{2,1,0:T(4,128)S(1)}, u32[]{:S(2)}, u32[]{:S(2)}) async-start(f32[8,3,512]{2,1,0:T(4,128)} %shard_map.71), calls=%async_computation.3 | async-start | bytes 131072 | tf_op jit(solution)/shard_map/all_to_all | solution.py:50
  135.5 3.8 %copy-start.2 = (bf16[1,1187,4096]{2,1,0:T(8,128)(2,1)S(1)}, bf16[1,1187,4096]{2,1,0:T(8,128)(2,1)}, u32[]{:S(2)}) copy-start(bf16[1,1187,4096]{2,1,0:T(8,128)(2,1)} %param.9) | copy-start | bytes 29171716
  144.8 10.6 %collective-permute-start.8 = (f32[16,264,128]{2,1,0:T(8,128)S(1)}, f32[16,264,128]{2,1,0:T(8,128)S(1)}, u32[]{:S(2)}, u32[]{:S(2)}) collective-permute-start(f32[16,264,128]{2,1,0:T(8,128)S(1)} %get-tuple-element.49), channel_id=1, source_target_pairs={{128,132},{132,128},{129,133},{133,129},{130,134},{134,130},{131,1... | collective-permute-start | bytes 6488072 | tf_op jit(solution)/shard_map/ppermute | solution.py:46
  154.6 8.0 %collective-permute-start.9 = (f32[16,264,128]{2,1,0:T(8,128)}, f32[16,264,128]{2,1,0:T(8,128)S(1)}, u32[]{:S(2)}, u32[]{:S(2)}) collective-permute-start(f32[16,264,128]{2,1,0:T(8,128)} %get-tuple-element.52), channel_id=1, source_target_pairs={{128,132},{132,128},{129,133},{133,129},{130,134},{134,130},{131,1... | collective-permute-start | bytes 6488072 | tf_op jit(solution)/shard_map/ppermute | solution.py:46
  156.9 31.7 %all-to-all-start.4 = ((f32[16,264,128]{2,1,0:T(8,128)}), f32[16,264,128]{2,1,0:T(8,128)}, u32[]{:S(2)}, u32[]{:S(2)}) async-start(f32[16,264,128]{2,1,0:T(8,128)} %shard_map.74), calls=%async_computation.4 | async-start | bytes 4325376 | tf_op jit(solution)/shard_map/all_to_all | solution.py:50
  162.6 1.4 copy-start.5
  164.0 1.6 copy-start.4
  165.6 1.6 copy-start.6
  223.7 22.5 %all-to-all-start.6 = ((f32[8,80,128]{2,1,0:T(8,128)}), f32[8,80,128]{2,1,0:T(8,128)S(1)}, u32[]{:S(2)}, u32[]{:S(2)}) async-start(f32[8,80,128]{2,1,0:T(8,128)} %shard_map.77), calls=%async_computation.6 | async-start | bytes 655360 | tf_op jit(solution)/shard_map/all_to_all | solution.py:50
  (3 other events, 3.0 us)

commit v4 on v3

--- a/solution.py
+++ b/solution.py
@@ -30,7 +30,7 @@
         kernel,
         out_shape=out_shape,
         in_specs=[in_smem()] * len(scalars)
-        + [pl.BlockSpec(memory_space=pl.ANY)] * len(remote)
+        + [pl.BlockSpec(memory_space=pltpu.HBM)] * len(remote)
         + [in_vmem()] * len(arrays),
         out_specs=jax.tree.map(lambda _: in_vmem(), out_shape),
         scratch_shapes=list(scratch),
@@ -228,7 +228,7 @@
 
 
 def shards(hidden, head_weight, labels, loss_mask):
-    weights = head_weight[0]
+    weights = pltpu.with_memory_space_constraint(head_weight[0], pltpu.HBM)
     words, feats = weights.shape
     place = jnp.stack([lax.axis_index(a) for a in ("core", "tok")]).astype(jnp.int32)
     first_word = lax.axis_index(("y", "x", "core", "tok")) * words
@@ -257,8 +257,6 @@
         if c == 1:
             x, own_z[0] = lax.optimization_barrier((x, own_z[0]))
         x = exchanged(x, CHIPS)
-        if c == 1:
-            x, sent[0] = lax.optimization_barrier((x, sent[0]))
         own_z.append(scores(place, weights, x))
         sent.append(lax.ppermute(own_z[c], "grp", [(0, 1)]))
 
@@ -280,6 +278,7 @@
     stats = vmem_call(
         pair_kernel, array((16,) + stats.shape, F32), stats, swapped(stats, "core")
     )
+    stats, sent[0] = lax.optimization_barrier((stats, sent[0]))
     stats = vmem_call(
         chips_kernel, array((8,) + stats.shape[1:], F32), exchanged(stats, CHIPS)
     )

time: 248 us -> 249 us (level)
  blocking collectives: 54.6 us -> 74.9 us
  waiting for transfers between devices: 70.7 us -> 58.6 us
  local copies, waits for them, and re-layouts: 20 us -> 7.99 us
  starting transfers between devices: 66.8 us -> 70.8 us
    all_to_all x2 -> x3, blocking collectives: 54.6 us -> 74.9 us  [exchanged(): return lax.all_to_all(x, axes, 0, 0)]
    unnamed x24 -> x14, local copies, waits for them, and re-layouts: 18.7 us -> 6.75 us
    all_to_all x5 -> x4, starting transfers between devices: 44.4 us -> 54.7 us  [exchanged(): return lax.all_to_all(x, axes, 0, 0)]
    ppermute x2, waiting for transfers between devices: 13 us -> 2.93 us  [shards(): sent.append(lax.ppermute(own_z[c], 'grp', [(0, 1)]))]
    ppermute x2, starting transfers between devices: 15.2 us -> 9.07 us  [shards(): sent.append(lax.ppermute(own_z[c], 'grp', [(0, 1)]))]
    all_to_all x5 -> x4, waiting for transfers between devices: 46.9 us -> 46.6 us  [exchanged(): return lax.all_to_all(x, axes, 0, 0)]
  transfers between devices with their start and end apart: 15 -> 14, of which waited for: 11 -> 10; matrix products, arithmetic and copies ran while one was open for 1% -> 1% of each run, Pallas kernels for 4% -> 6%
where the time goes in v4:
time: 249 us; the launch traced here: 248 us
  blocking collectives  74.9 us (30%)
  starting transfers between devices  70.8 us (28%)
  waiting for transfers between devices  58.6 us (24%)
  Pallas kernels  30.4 us (12%)
  local copies, waits for them, and re-layouts  7.99 us (3%)
  other arithmetic  4.23 us (2%)
    all_to_all x3, blocking collectives, exchanged(): return lax.all_to_all(x, axes, 0, 0)  74.9 us
    all_to_all x4, starting transfers between devices, exchanged(): return lax.all_to_all(x, axes, 0, 0)  54.7 us
    all_to_all x4, waiting for transfers between devices, exchanged(): return lax.all_to_all(x, axes, 0, 0)  46.6 us
    pallas_call x11, Pallas kernels, vmem_call(): pl.pallas_call(kernel, out_shape=out_shape, in_specs=[in_smem()] * len(sc...  30.4 us
    ppermute x2, starting transfers between devices, shards(): sent.append(lax.ppermute(own_z[c], 'grp', [(0, 1)]))  9.07 us
    unnamed x14, local copies, waits for them, and re-layouts  6.75 us
    ppermute x3, starting transfers between devices, shards(): lax.ppermute(block, 'tok', [(i, (i + k) % 4) for i in range(4)])  5.37 us
    ppermute x3, waiting for transfers between devices, shards(): lax.ppermute(block, 'tok', [(i, (i + k) % 4) for i in range(4)])  5.18 us
  transfers between devices with their start and end apart: 14, of which 10 were waited for; matrix products, arithmetic and copies ran while one was open for 1% of the time, Pallas kernels for 6%

profile of v4, /device:TPU:2, one launch (start us, length us, event | category | flops | bytes accessed | tf_op | source)
XLA Modules:
  0.0 247.7 jit_solution(14870806387530216802)
XLA Ops:
  0.6 4.7 %collective-permute-start.2 = (bf16[128,128]{1,0:T(8,128)(2,1)}, bf16[128,128]{1,0:T(8,128)(2,1)S(1)}, u32[]{:S(2)}, u32[]{:S(2)}) collective-permute-start(bf16[128,128]{1,0:T(8,128)(2,1)} %bitcast.32), channel_id=1, source_target_pairs={{0,3},{1,0},{2,1},{3,2},{4,7},{5,4},{6,5},{7,6},{8,11},{9,8},{10,9... | collective-permute-start | bytes 98312 | tf_op jit(solution)/shard_map/ppermute | solution.py:243
  7.2 3.1 %collective-permute-done.1.p2 = bf16[128,128]{1,0:T(8,128)(2,1)S(1)} collective-permute-done((bf16[128,128]{1,0:T(8,128)(2,1)}, bf16[128,128]{1,0:T(8,128)(2,1)S(1)}, u32[]{:S(2)}, u32[]{:S(2)}) %collective-permute-start.1) | collective-permute-done | bytes 32800 | tf_op jit(solution)/shard_map/ppermute | solution.py:243
  12.8 22.0 %all_to_all.35.own = bf16[16,256,128]{2,1,0:T(8,128)(2,1)S(1)} all-to-all(bf16[16,256,128]{2,1,0:T(8,128)(2,1)S(1)} %get-tuple-element.41), channel_id=1, replica_groups=mesh['grp'=2,'y'=4,'x'=4,'core'=2,'tok'=4] {'y','x'}, dimensions={0} | all-to-all | bytes 2097152 | tf_op jit(solution)/shard_map/all_to_all | solution.py:50
  34.9 2.7 %collective-permute-done.3.sibling = bf16[16,256,128]{2,1,0:T(8,128)(2,1)S(1)} collective-permute-done((bf16[16,256,128]{2,1,0:T(8,128)(2,1)S(1)}, bf16[16,256,128]{2,1,0:T(8,128)(2,1)S(1)}, u32[]{:S(2)}, u32[]{:S(2)}) %collective-permute-start.3) | collective-permute-done | bytes 1048608 | tf_op jit(solution)/shard_map/ppermute | solution.py:42
  37.6 5.6 %shard_map.68 = bf16[1187,256]{1,0:T(8,128)(2,1)S(1)} custom-call(s32[2]{0:T(128)S(1)} %pad_add_fusion.place_ref, bf16[1187,4096]{1,0:T(8,128)(2,1)} %bitcast.36, bf16[16,256,128]{2,1,0:T(8,128)(2,1)S(1)} %all_to_all.35.own, bf16[16,256,128]{2,1,0:T(8,128)(2,1)S(1)} %collective-permute-done.3.sibling), custom_call_target="tpu_custom_call" | custom-call | tf_op jit(solution)/shard_map/pallas_call | solution.py:29
  43.2 20.3 %all_to_all.36.own = bf16[16,256,128]{2,1,0:T(8,128)(2,1)S(1)} all-to-all(bf16[16,256,128]{2,1,0:T(8,128)(2,1)S(1)} %get-tuple-element.43), channel_id=1, replica_groups=mesh['grp'=2,'y'=4,'x'=4,'core'=2,'tok'=4] {'y','x'}, dimensions={0} | all-to-all | bytes 2097152 | tf_op jit(solution)/shard_map/all_to_all | solution.py:50
  63.5 7.4 %collective-permute-start.6 = (bf16[1187,256]{1,0:T(8,128)(2,1)S(1)}, bf16[1187,256]{1,0:T(8,128)(2,1)}, u32[]{:S(2)}, u32[]{:S(2)}) collective-permute-start(bf16[1187,256]{1,0:T(8,128)(2,1)S(1)} %shard_map.68), channel_id=1, source_target_pairs={{0,128},{1,129},{2,130},{3,131},{4,132},{5,133},{6,134},{7,135},{8... | collective-permute-start | bytes 1823240 | tf_op jit(solution)/shard_map/ppermute | solution.py:261
  71.1 5.6 %shard_map.69 = bf16[1187,256]{1,0:T(8,128)(2,1)S(1)} custom-call(s32[2]{0:T(128)S(1)} %pad_add_fusion.place_ref, bf16[1187,4096]{1,0:T(8,128)(2,1)} %bitcast.37, bf16[16,256,128]{2,1,0:T(8,128)(2,1)S(1)} %all_to_all.36.own, bf16[16,256,128]{2,1,0:T(8,128)(2,1)S(1)} %collective-permute-done.4.sibling), custom_call_target="tpu_custom_call" | custom-call | tf_op jit(solution)/shard_map/pallas_call | solution.py:29
  76.9 1.7 collective-permute-start.7
  81.2 2.9 %collective-permute-done.6 = bf16[1187,256]{1,0:T(8,128)(2,1)} collective-permute-done((bf16[1187,256]{1,0:T(8,128)(2,1)S(1)}, bf16[1187,256]{1,0:T(8,128)(2,1)}, u32[]{:S(2)}, u32[]{:S(2)}) %collective-permute-start.6) | collective-permute-done | bytes 607776 | tf_op jit(solution)/shard_map/ppermute | solution.py:261
  84.1 4.8 %all-to-all-start.2 = ((f32[16,3,512]{2,1,0:T(4,128)}), f32[16,3,512]{2,1,0:T(4,128)S(1)}, u32[]{:S(2)}, u32[]{:S(2)}) async-start(f32[16,3,512]{2,1,0:T(4,128)} %shard_map.70), calls=%async_computation.2 | async-start | bytes 262144 | tf_op jit(solution)/shard_map/all_to_all | solution.py:50
  88.9 6.7 %all-to-all-done.2.parts = f32[16,3,512]{2,1,0:T(4,128)S(1)} async-done(((f32[16,3,512]{2,1,0:T(4,128)}), f32[16,3,512]{2,1,0:T(4,128)S(1)}, u32[]{:S(2)}, u32[]{:S(2)}) %all-to-all-start.2) | async-done | bytes 98336 | tf_op jit(solution)/shard_map/all_to_all | solution.py:50
  96.3 32.7 %all-to-all-start.3 = ((f32[8,3,512]{2,1,0:T(4,128)}), f32[8,3,512]{2,1,0:T(4,128)S(1)}, u32[]{:S(2)}, u32[]{:S(2)}) async-start(f32[8,3,512]{2,1,0:T(4,128)} %shard_map.71), calls=%async_computation.3 | async-start | bytes 131072 | tf_op jit(solution)/shard_map/all_to_all | solution.py:50
  129.0 8.4 %all-to-all-done.3.parts = f32[8,3,512]{2,1,0:T(4,128)S(1)} async-done(((f32[8,3,512]{2,1,0:T(4,128)}), f32[8,3,512]{2,1,0:T(4,128)S(1)}, u32[]{:S(2)}, u32[]{:S(2)}) %all-to-all-start.3) | async-done | bytes 49184 | tf_op jit(solution)/shard_map/all_to_all | solution.py:50
  137.5 1.8 fusion.17
  139.3 5.7 %shard_map.73 = (f32[16,264,128]{2,1,0:T(8,128)S(1)}, f32[16,264,128]{2,1,0:T(8,128)S(1)}) custom-call(s32[2]{0:T(128)S(1)} %pad_add_fusion.place_ref, bf16[1187,4096]{1,0:T(8,128)(2,1)} %bitcast.38, bf16[1187,256]{1,0:T(8,128)(2,1)S(1)} %get-tuple-element.60.grads, f32[8,128]{1,0:T(8,128)S(1)} %scatter.6.extra), custom_call_target="tpu_custom_call" | custom-call | tf_op jit(solution)/shard_map/pallas_call | solution.py:29
  146.5 7.1 %shard_map.75 = (f32[16,264,128]{2,1,0:T(8,128)S(1)}, f32[16,264,128]{2,1,0:T(8,128)}) custom-call(s32[2]{0:T(128)S(1)} %pad_add_fusion.place_ref, bf16[1187,4096]{1,0:T(8,128)(2,1)} %bitcast.39, bf16[1187,256]{1,0:T(8,128)(2,1)S(1)} %get-tuple-element.58.grads, f32[8,128]{1,0:T(8,128)S(1)} %scatter.9.extra), custom_call_target="tpu_custom_call" | custom-call | tf_op jit(solution)/shard_map/pallas_call | solution.py:29
  157.3 5.6 %all-to-all-start.4 = ((f32[16,264,128]{2,1,0:T(8,128)}), f32[16,264,128]{2,1,0:T(8,128)}, u32[]{:S(2)}, u32[]{:S(2)}) async-start(f32[16,264,128]{2,1,0:T(8,128)} %shard_map.74), calls=%async_computation.4 | async-start | bytes 4325376 | tf_op jit(solution)/shard_map/all_to_all | solution.py:50
  164.3 1.6 copy-done.1
  167.8 20.9 %all-to-all-done.4.lower = f32[16,264,128]{2,1,0:T(8,128)} async-done(((f32[16,264,128]{2,1,0:T(8,128)}), f32[16,264,128]{2,1,0:T(8,128)}, u32[]{:S(2)}, u32[]{:S(2)}) %all-to-all-start.4) | async-done | bytes 2162720 | tf_op jit(solution)/shard_map/all_to_all | solution.py:50
  188.6 32.5 %all_to_all.37.upper = f32[16,264,128]{2,1,0:T(8,128)S(1)} all-to-all(f32[16,264,128]{2,1,0:T(8,128)S(1)} %shard_map.76), channel_id=1, replica_groups=mesh['grp'=2,'y'=4,'x'=4,'core'=2,'tok'=4] {'y','x'}, dimensions={0} | all-to-all | bytes 4325376 | tf_op jit(solution)/shard_map/all_to_all | solution.py:50
  221.2 2.5 %shard_map.77 = f32[8,80,128]{2,1,0:T(8,128)} custom-call(f32[16,264,128]{2,1,0:T(8,128)} %all-to-all-done.4.lower, f32[16,264,128]{2,1,0:T(8,128)S(1)} %all_to_all.37.upper), custom_call_target="tpu_custom_call" | custom-call | tf_op jit(solution)/shard_map/pallas_call | solution.py:29
  223.7 11.6 %all-to-all-start.6 = ((f32[8,80,128]{2,1,0:T(8,128)}), f32[8,80,128]{2,1,0:T(8,128)S(1)}, u32[]{:S(2)}, u32[]{:S(2)}) async-start(f32[8,80,128]{2,1,0:T(8,128)} %shard_map.77), calls=%async_computation.6 | async-start | bytes 655360 | tf_op jit(solution)/shard_map/all_to_all | solution.py:50
  235.8 10.7 %all-to-all-done.6 = f32[8,80,128]{2,1,0:T(8,128)S(1)} async-done(((f32[8,80,128]{2,1,0:T(8,128)}), f32[8,80,128]{2,1,0:T(8,128)S(1)}, u32[]{:S(2)}, u32[]{:S(2)}) %all-to-all-start.6) | async-done | bytes 327712 | tf_op jit(solution)/shard_map/all_to_all | solution.py:50
  (54 shorter events, 18.4 us)
Async XLA Ops:
  0.6 6.6 %collective-permute-start.2 = (bf16[128,128]{1,0:T(8,128)(2,1)}, bf16[128,128]{1,0:T(8,128)(2,1)S(1)}, u32[]{:S(2)}, u32[]{:S(2)}) collective-permute-start(bf16[128,128]{1,0:T(8,128)(2,1)} %bitcast.32), channel_id=1, source_target_pairs={{0,3},{1,0},{2,1},{3,2},{4,7},{5,4},{6,5},{7,6},{8,11},{9,8},{10,9... | collective-permute-start | bytes 98312 | tf_op jit(solution)/shard_map/ppermute | solution.py:243
  5.3 5.0 %collective-permute-start.1 = (bf16[128,128]{1,0:T(8,128)(2,1)}, bf16[128,128]{1,0:T(8,128)(2,1)S(1)}, u32[]{:S(2)}, u32[]{:S(2)}) collective-permute-start(bf16[128,128]{1,0:T(8,128)(2,1)} %bitcast.33), channel_id=1, source_target_pairs={{0,2},{1,3},{2,0},{3,1},{4,6},{5,7},{6,4},{7,5},{8,10},{9,11},{10,... | collective-permute-start | bytes 98312 | tf_op jit(solution)/shard_map/ppermute | solution.py:243
  5.3 5.9 %collective-permute-start = (bf16[128,128]{1,0:T(8,128)(2,1)}, bf16[128,128]{1,0:T(8,128)(2,1)S(1)}, u32[]{:S(2)}, u32[]{:S(2)}) collective-permute-start(bf16[128,128]{1,0:T(8,128)(2,1)} %bitcast.34), channel_id=1, source_target_pairs={{0,1},{1,2},{2,3},{3,0},{4,5},{5,6},{6,7},{7,4},{8,9},{9,10},{10,1... | collective-permute-start | bytes 98312 | tf_op jit(solution)/shard_map/ppermute | solution.py:243
  11.3 0.8 copy-start.4
  34.9 2.7 %collective-permute-start.3 = (bf16[16,256,128]{2,1,0:T(8,128)(2,1)S(1)}, bf16[16,256,128]{2,1,0:T(8,128)(2,1)S(1)}, u32[]{:S(2)}, u32[]{:S(2)}) collective-permute-start(bf16[16,256,128]{2,1,0:T(8,128)(2,1)S(1)} %all_to_all.35.own), channel_id=1, source_target_pairs={{0,4},{4,0},{1,5},{5,1},{2,6},{6,2},{3,7},{7,3},{8,12},{12,8},{9,1... | collective-permute-start | bytes 3145736 | tf_op jit(solution)/shard_map/ppermute | solution.py:42
  43.1 27.7 %copy-start.6 = (s32[512]{0:T(512)S(1)}, s32[512]{0:T(512)}, u32[]{:S(2)}) copy-start(s32[512]{0:T(512)} %param.10) | copy-start | bytes 6148
  63.5 7.6 %collective-permute-start.4 = (bf16[16,256,128]{2,1,0:T(8,128)(2,1)S(1)}, bf16[16,256,128]{2,1,0:T(8,128)(2,1)S(1)}, u32[]{:S(2)}, u32[]{:S(2)}) collective-permute-start(bf16[16,256,128]{2,1,0:T(8,128)(2,1)S(1)} %all_to_all.36.own), channel_id=1, source_target_pairs={{0,4},{4,0},{1,5},{5,1},{2,6},{6,2},{3,7},{7,3},{8,12},{12,8},{9,1... | collective-permute-start | bytes 3145736 | tf_op jit(solution)/shard_map/ppermute | solution.py:42
  63.5 20.6 %collective-permute-start.6 = (bf16[1187,256]{1,0:T(8,128)(2,1)S(1)}, bf16[1187,256]{1,0:T(8,128)(2,1)}, u32[]{:S(2)}, u32[]{:S(2)}) collective-permute-start(bf16[1187,256]{1,0:T(8,128)(2,1)S(1)} %shard_map.68), channel_id=1, source_target_pairs={{0,128},{1,129},{2,130},{3,131},{4,132},{5,133},{6,134},{7,135},{8... | collective-permute-start | bytes 1823240 | tf_op jit(solution)/shard_map/ppermute | solution.py:261
  76.7 12.2 %copy-start.5 = (s32[512]{0:T(512)S(1)}, s32[512]{0:T(512)}, u32[]{:S(2)}) copy-start(s32[512]{0:T(512)} %param.11) | copy-start | bytes 6148
  76.9 60.6 %collective-permute-start.7 = (bf16[1187,256]{1,0:T(8,128)(2,1)S(1)}, bf16[1187,256]{1,0:T(8,128)(2,1)S(1)}, u32[]{:S(2)}, u32[]{:S(2)}) collective-permute-start(bf16[1187,256]{1,0:T(8,128)(2,1)S(1)} %shard_map.69), channel_id=1, source_target_pairs={{0,128},{1,129},{2,130},{3,131},{4,132},{5,133},{6,134},{7,135},{8... | collective-permute-start | bytes 1823240 | tf_op jit(solution)/shard_map/ppermute | solution.py:261
  79.3 1.3 collective-permute-start.5
  84.1 11.5 %all-to-all-start.2 = ((f32[16,3,512]{2,1,0:T(4,128)}), f32[16,3,512]{2,1,0:T(4,128)S(1)}, u32[]{:S(2)}, u32[]{:S(2)}) async-start(f32[16,3,512]{2,1,0:T(4,128)} %shard_map.70), calls=%async_computation.2 | async-start | bytes 262144 | tf_op jit(solution)/shard_map/all_to_all | solution.py:50
  96.3 41.1 %all-to-all-start.3 = ((f32[8,3,512]{2,1,0:T(4,128)}), f32[8,3,512]{2,1,0:T(4,128)S(1)}, u32[]{:S(2)}, u32[]{:S(2)}) async-start(f32[8,3,512]{2,1,0:T(4,128)} %shard_map.71), calls=%async_computation.3 | async-start | bytes 131072 | tf_op jit(solution)/shard_map/all_to_all | solution.py:50
  144.9 10.8 %collective-permute-start.8 = (f32[16,264,128]{2,1,0:T(8,128)S(1)}, f32[16,264,128]{2,1,0:T(8,128)S(1)}, u32[]{:S(2)}, u32[]{:S(2)}) collective-permute-start(f32[16,264,128]{2,1,0:T(8,128)S(1)} %get-tuple-element.49), channel_id=1, source_target_pairs={{128,132},{132,128},{129,133},{133,129},{130,134},{134,130},{131,1... | collective-permute-start | bytes 6488072 | tf_op jit(solution)/shard_map/ppermute | solution.py:46
  153.6 1.4 copy-start
  154.9 8.0 %collective-permute-start.9 = (f32[16,264,128]{2,1,0:T(8,128)}, f32[16,264,128]{2,1,0:T(8,128)S(1)}, u32[]{:S(2)}, u32[]{:S(2)}) collective-permute-start(f32[16,264,128]{2,1,0:T(8,128)} %get-tuple-element.52), channel_id=1, source_target_pairs={{128,132},{132,128},{129,133},{133,129},{130,134},{134,130},{131,1... | collective-permute-start | bytes 6488072 | tf_op jit(solution)/shard_map/ppermute | solution.py:46
  157.3 31.4 %all-to-all-start.4 = ((f32[16,264,128]{2,1,0:T(8,128)}), f32[16,264,128]{2,1,0:T(8,128)}, u32[]{:S(2)}, u32[]{:S(2)}) async-start(f32[16,264,128]{2,1,0:T(8,128)} %shard_map.74), calls=%async_computation.4 | async-start | bytes 4325376 | tf_op jit(solution)/shard_map/all_to_all | solution.py:50
  162.9 1.4 copy-start.2
  164.3 1.6 copy-start.1
  165.9 1.6 copy-start.3
  223.7 22.8 %all-to-all-start.6 = ((f32[8,80,128]{2,1,0:T(8,128)}), f32[8,80,128]{2,1,0:T(8,128)S(1)}, u32[]{:S(2)}, u32[]{:S(2)}) async-start(f32[8,80,128]{2,1,0:T(8,128)} %shard_map.77), calls=%async_computation.6 | async-start | bytes 655360 | tf_op jit(solution)/shard_map/all_to_all | solution.py:50

commit v5 on v4

--- a/solution.py
+++ b/solution.py
@@ -50,16 +50,14 @@
     return lax.all_to_all(x, axes, 0, 0)
 
 
-def order_tok_kernel(place_ref, p0, p1, p2, p3, lower, upper, held):
+def order_tok_kernel(place_ref, p0, p1, p2, p3, out, held):
     me = place_ref[1]
     rows = p0.shape[0]
     for k, piece in enumerate((p0, p1, p2, p3)):
         held[lax.rem(me + 4 - k, 4)] = piece[...]
-    for chip in range(lower.shape[0]):
-        lower[chip, :rows] = held[0]
-        lower[chip, rows:] = held[1]
-        upper[chip, :rows] = held[2]
-        upper[chip, rows:] = held[3]
+    for chip in range(out.shape[0]):
+        for j in range(4):
+            out[chip, j * rows : (j + 1) * rows] = held[j]
 
 
 def strips_of(weights, held, sems):
@@ -73,9 +71,11 @@
     return copies
 
 
-def scores_kernel(place_ref, weights, own, sibling, out, joined, held, acc, sems):
+def scores_kernel(half, place_ref, weights, own, sibling, out, joined, held, acc, sems):
     core = place_ref[0]
     chips, _, wide = own.shape
+    tokens = out.shape[1]
+    rows = slice(half * tokens, (half + 1) * tokens)
     depth = held.shape[2]
     words = out.shape[0]
     copies = strips_of(weights, held, sems)
@@ -83,8 +83,8 @@
     def join(first, second):
         for chip in range(chips):
             at = 2 * chip * wide
-            joined[:, at : at + wide] = first[chip]
-            joined[:, at + wide : at + 2 * wide] = second[chip]
+            joined[:, at : at + wide] = first[chip, rows]
+            joined[:, at + wide : at + 2 * wide] = second[chip, rows]
 
     @pl.when(core == 0)
     def _():
@@ -113,14 +113,14 @@
                 out[at] = part.astype(BF16)
 
 
-def scores(place, weights, own):
+def scores(place, weights, own, sibling, half):
     words, feats = weights.shape
-    tokens = own.shape[1]
+    tokens = own.shape[1] // 2
     return vmem_call(
-        scores_kernel,
+        functools.partial(scores_kernel, half),
         jax.ShapeDtypeStruct((words, tokens), BF16),
         own,
-        swapped(own, "core"),
+        sibling,
         place=place,
         weights=weights,
         scratch=[
@@ -210,27 +210,55 @@
     )
 
 
-def pair_sum_kernel(keep, got, out):
-    out[...] = keep[...] + got[...]
-
-
-def last_split_kernel(lower, upper, out):
-    rows = lower.shape[1] - EXTRA
+def line_total(parts):
+    return (parts[0] + parts[2]) + (parts[1] + parts[3])
+
+
+def pair_sum_kernel(x_first, place_ref, keep, got, *outs):
+    y, x = place_ref[2], place_ref[3]
+    rows = keep.shape[1] - EXTRA
+    for first, out in enumerate(outs):
+        for second in range(4):
+            kx, ky = (first, second) if x_first else (second, first)
+            chip = lax.rem(y + ky, 4) * 4 + lax.rem(x + kx, 4)
+            at = slice(second * rows, (second + 1) * rows)
+            out[at] = keep[chip, :rows] + got[chip, :rows]
+        out[4 * rows :] = keep[0, rows:] + got[0, rows:]
+
+
+def line_sum_kernel(p0, p1, p2, p3, *outs):
+    parts = (p0, p1, p2, p3)
+    rows = outs[0].shape[0] - EXTRA
+    extra = line_total([p[4 * rows :] for p in parts])
+    for k, out in enumerate(outs):
+        at = slice(k * rows, (k + 1) * rows)
+        out[:rows] = line_total([p[at] for p in parts])
+        out[rows:] = extra
+
+
+def last_split_kernel(a0, a1, a2, a3, b0, b1, b2, b3, out):
+    halves = ((a0, a1, a2, a3), (b0, b1, b2, b3))
+    rows = a0.shape[0] - EXTRA
     part = rows // 4
-    chips = lower.shape[0]
-    tail = [total([half[i, rows:] for i in range(chips)]) for half in (lower, upper)]
+    tails = [line_total([p[rows:] for p in half]) for half in halves]
     for plane in range(8):
-        half = lower if plane < 4 else upper
         at = slice((plane % 4) * part, (plane % 4 + 1) * part)
-        out[plane, :part] = total([half[i, at] for i in range(chips)])
-        out[plane, part : part + EXTRA] = tail[0]
-        out[plane, part + EXTRA :] = tail[1]
+        out[plane, :part] = line_total([p[at] for p in halves[plane // 4]])
+        out[plane, part : part + EXTRA] = tails[0]
+        out[plane, part + EXTRA :] = tails[1]
+
+
+def scattered(parts, axis):
+    def moved(part, step):
+        return lax.ppermute(part, axis, [(i, (i + step) % 4) for i in range(4)])
+
+    return [parts[0]] + [moved(parts[k], k) for k in range(1, 4)]
 
 
 def shards(hidden, head_weight, labels, loss_mask):
     weights = pltpu.with_memory_space_constraint(head_weight[0], pltpu.HBM)
     words, feats = weights.shape
-    place = jnp.stack([lax.axis_index(a) for a in ("core", "tok")]).astype(jnp.int32)
+    place = jnp.stack([lax.axis_index(a) for a in ("core", "tok", "y", "x")]).astype(jnp.int32)
     first_word = lax.axis_index(("y", "x", "core", "tok")) * words
     word_ids = first_word + lax.broadcasted_iota(jnp.int32, (words, 1), 0)
     mask = loss_mask.astype(F32)
@@ -242,23 +270,22 @@
     turns = [
         lax.ppermute(block, "tok", [(i, (i + k) % 4) for i in range(4)]) for k in range(1, 4)
     ]
-    halves = vmem_call(
+    own = vmem_call(
         order_tok_kernel,
-        [array((16, half, wide), BF16)] * 2,
+        array((16, 2 * half, wide), BF16),
         block,
         *turns,
         place=place,
         scratch=[pltpu.VMEM((4, rows, wide), BF16)],
     )
-
+    own = exchanged(own, CHIPS)
+    sibling = swapped(own, "core")
     own_z, sent = [], []
     for c in range(2):
-        x = halves[c]
-        if c == 1:
-            x, own_z[0] = lax.optimization_barrier((x, own_z[0]))
-        x = exchanged(x, CHIPS)
-        own_z.append(scores(place, weights, x))
+        own_z.append(scores(place, weights, own, sibling, c))
         sent.append(lax.ppermute(own_z[c], "grp", [(0, 1)]))
+        if c == 0:
+            sibling, own_z[0] = lax.optimization_barrier((sibling, own_z[0]))
 
     hits = [word_ids == labels[c * half : (c + 1) * half][None, :] for c in range(2)]
     stats = []
@@ -278,7 +305,6 @@
     stats = vmem_call(
         pair_kernel, array((16,) + stats.shape, F32), stats, swapped(stats, "core")
     )
-    stats, sent[0] = lax.optimization_barrier((stats, sent[0]))
     stats = vmem_call(
         chips_kernel, array((8,) + stats.shape[1:], F32), exchanged(stats, CHIPS)
     )
@@ -299,16 +325,28 @@
         ).astype(BF16)
         extra = jnp.zeros((EXTRA, wide), F32).at[:2].set(diverge.reshape(2, wide))
         parts.append(split_grads(place, weights, grads, extra))
-    summed = []
-    for keep, send in parts:
-        paired = vmem_call(
-            pair_sum_kernel, array(keep.shape, F32), keep, swapped_in_student(send)
+    orders = (("x", "y"), ("y", "x"))
+    array_of = lambda rows: [array((rows + EXTRA, wide), F32)] * 4
+    pieces = [
+        vmem_call(
+            functools.partial(pair_sum_kernel, c == 0),
+            array_of(4 * half),
+            keep,
+            swapped_in_student(send),
+            place=place,
         )
-        summed.append(exchanged(paired, CHIPS))
+        for c, (keep, send) in enumerate(parts)
+    ]
+    pieces = [scattered(pieces[c], orders[c][0]) for c in range(2)]
+    pieces = [vmem_call(line_sum_kernel, array_of(half), *pieces[c]) for c in range(2)]
+    pieces = [scattered(pieces[c], orders[c][1]) for c in range(2)]
 
     part = half // 4
     last = vmem_call(
-        last_split_kernel, array((8, part + 2 * EXTRA, wide), F32), *summed
+        last_split_kernel,
+        array((8, part + 2 * EXTRA, wide), F32),
+        *pieces[0],
+        *pieces[1],
     )
     mine = total(list(exchanged(last, PLANES))[4:])
     input_grads = mine[:part].astype(BF16)

time: 249 us -> 208 us (0.84)
  blocking collectives: 74.9 us -> 34.2 us
  waiting for transfers between devices: 58.6 us -> 79.8 us
  starting transfers between devices: 70.8 us -> 56.4 us
  local copies, waits for them, and re-layouts: 7.99 us -> 2.01 us
    all_to_all x3 -> x1, blocking collectives: 74.9 us -> 34.2 us  [exchanged(): return lax.all_to_all(x, axes, 0, 0)]
    all_to_all x4 -> x3, starting transfers between devices: 54.7 us -> 21.8 us  [exchanged(): return lax.all_to_all(x, axes, 0, 0)]
    ppermute x0 -> x12, waiting for transfers between devices: none -> 21 us  [moved(): return lax.ppermute(part, axis, [(i, (i + step) % 4) for i in range(4)])]
    ppermute x0 -> x12, starting transfers between devices: none -> 19.2 us  [moved(): return lax.ppermute(part, axis, [(i, (i + step) % 4) for i in range(4)])]
    unnamed x14 -> x6, local copies, waits for them, and re-layouts: 6.75 us -> 0.77 us
    ppermute x2, waiting for transfers between devices: 2.93 us -> 0.01 us  [shards(): sent.append(lax.ppermute(own_z[c], 'grp', [(0, 1)]))]
    ppermute x3 -> x2, waiting for transfers between devices: 3.82 us -> 5.43 us  [swapped(): return lax.ppermute(x, axis, [(0, 1), (1, 0)])]
    all_to_all x4 -> x3, waiting for transfers between devices: 46.6 us -> 48.2 us  [exchanged(): return lax.all_to_all(x, axes, 0, 0)]
  transfers between devices with their start and end apart: 14 -> 24, of which waited for: 10 -> 16; matrix products, arithmetic and copies ran while one was open for 1% -> 1% of each run, Pallas kernels for 6% -> 8%
where the time goes in v5:
time: 208 us; the launch traced here: 207 us
  waiting for transfers between devices  79.8 us (38%)
  starting transfers between devices  56.4 us (27%)
  blocking collectives  34.2 us (16%)
  Pallas kernels  29.5 us (14%)
  other arithmetic  4.24 us (2%)
    all_to_all x3, waiting for transfers between devices, exchanged(): return lax.all_to_all(x, axes, 0, 0)  48.2 us
    all_to_all x1, blocking collectives, exchanged(): return lax.all_to_all(x, axes, 0, 0)  34.2 us
    pallas_call x13, Pallas kernels, vmem_call(): pl.pallas_call(kernel, out_shape=out_shape, in_specs=[in_smem()] * len(sc...  29.5 us
    all_to_all x3, starting transfers between devices, exchanged(): return lax.all_to_all(x, axes, 0, 0)  21.8 us
    ppermute x12, waiting for transfers between devices, moved(): return lax.ppermute(part, axis, [(i, (i + step) % 4) for i in range(4)])  21 us
    ppermute x12, starting transfers between devices, moved(): return lax.ppermute(part, axis, [(i, (i + step) % 4) for i in range(4)])  19.2 us
    ppermute x2, starting transfers between devices, shards(): sent.append(lax.ppermute(own_z[c], 'grp', [(0, 1)]))  8.3 us
    ppermute x2, waiting for transfers between devices, swapped(): return lax.ppermute(x, axis, [(0, 1), (1, 0)])  5.43 us
  transfers between devices with their start and end apart: 24, of which 16 were waited for; matrix products, arithmetic and copies ran while one was open for 1% of the time, Pallas kernels for 8%

profile of v5, /device:TPU:2, one launch (start us, length us, event | category | flops | bytes accessed | tf_op | source)
XLA Modules:
  0.0 207.0 jit_solution(10303119247944065129)
XLA Ops:
  0.6 4.7 %collective-permute-start.2 = (bf16[128,128]{1,0:T(8,128)(2,1)}, bf16[128,128]{1,0:T(8,128)(2,1)S(1)}, u32[]{:S(2)}, u32[]{:S(2)}) collective-permute-start(bf16[128,128]{1,0:T(8,128)(2,1)} %bitcast.34), channel_id=1, source_target_pairs={{0,3},{1,0},{2,1},{3,2},{4,7},{5,4},{6,5},{7,6},{8,11},{9,8},{10,9... | collective-permute-start | bytes 98312 | tf_op jit(solution)/shard_map/ppermute | solution.py:271
  7.2 3.1 %collective-permute-done.1.p2 = bf16[128,128]{1,0:T(8,128)(2,1)S(1)} collective-permute-done((bf16[128,128]{1,0:T(8,128)(2,1)}, bf16[128,128]{1,0:T(8,128)(2,1)S(1)}, u32[]{:S(2)}, u32[]{:S(2)}) %collective-permute-start.1) | collective-permute-done | bytes 32800 | tf_op jit(solution)/shard_map/ppermute | solution.py:271
  12.9 34.2 %all_to_all.20.own = bf16[16,512,128]{2,1,0:T(8,128)(2,1)S(1)} all-to-all(bf16[16,512,128]{2,1,0:T(8,128)(2,1)S(1)} %shard_map.67), channel_id=1, replica_groups=mesh['grp'=2,'y'=4,'x'=4,'core'=2,'tok'=4] {'y','x'}, dimensions={0} | all-to-all | bytes 4194304 | tf_op jit(solution)/shard_map/all_to_all | solution.py:50
  47.1 4.3 %collective-permute-done.3.sibling = bf16[16,512,128]{2,1,0:T(8,128)(2,1)} collective-permute-done((bf16[16,512,128]{2,1,0:T(8,128)(2,1)S(1)}, bf16[16,512,128]{2,1,0:T(8,128)(2,1)}, u32[]{:S(2)}, u32[]{:S(2)}) %collective-permute-start.3) | collective-permute-done | bytes 2097184 | tf_op jit(solution)/shard_map/ppermute | solution.py:42
  51.3 6.7 %shard_map.68 = bf16[1187,256]{1,0:T(8,128)(2,1)S(1)} custom-call(s32[4]{0:T(128)S(1)} %pad_add_fusion.place_ref, bf16[1187,4096]{1,0:T(8,128)(2,1)} %bitcast.38, bf16[16,512,128]{2,1,0:T(8,128)(2,1)S(1)} %all_to_all.20.own, bf16[16,512,128]{2,1,0:T(8,128)(2,1)} %collective-permute-done.3.sibling), custom_call_target="tpu_custom_call" | custom-call | tf_op jit(solution)/shard_map/pallas_call | solution.py:29
  58.0 7.0 %collective-permute-start.5 = (bf16[1187,256]{1,0:T(8,128)(2,1)S(1)}, bf16[1187,256]{1,0:T(8,128)(2,1)}, u32[]{:S(2)}, u32[]{:S(2)}) collective-permute-start(bf16[1187,256]{1,0:T(8,128)(2,1)S(1)} %shard_map.68), channel_id=1, source_target_pairs={{0,128},{1,129},{2,130},{3,131},{4,132},{5,133},{6,134},{7,135},{8... | collective-permute-start | bytes 1823240 | tf_op jit(solution)/shard_map/ppermute | solution.py:286
  65.0 6.6 %shard_map.69 = bf16[1187,256]{1,0:T(8,128)(2,1)S(1)} custom-call(s32[4]{0:T(128)S(1)} %pad_add_fusion.place_ref, bf16[1187,4096]{1,0:T(8,128)(2,1)} %bitcast.39, bf16[16,512,128]{2,1,0:T(8,128)(2,1)S(1)} %all_to_all.20.own, bf16[16,512,128]{2,1,0:T(8,128)(2,1)} %collective-permute-done.3.sibling), custom_call_target="tpu_custom_call" | custom-call | tf_op jit(solution)/shard_map/pallas_call | solution.py:29
  76.0 4.4 %all-to-all-start.1 = ((f32[16,3,512]{2,1,0:T(4,128)}), f32[16,3,512]{2,1,0:T(4,128)S(1)}, u32[]{:S(2)}, u32[]{:S(2)}) async-start(f32[16,3,512]{2,1,0:T(4,128)} %shard_map.70), calls=%async_computation.1 | async-start | bytes 262144 | tf_op jit(solution)/shard_map/all_to_all | solution.py:50
  80.4 6.7 %all-to-all-done.1.parts = f32[16,3,512]{2,1,0:T(4,128)S(1)} async-done(((f32[16,3,512]{2,1,0:T(4,128)}), f32[16,3,512]{2,1,0:T(4,128)S(1)}, u32[]{:S(2)}, u32[]{:S(2)}) %all-to-all-start.1) | async-done | bytes 98336 | tf_op jit(solution)/shard_map/all_to_all | solution.py:50
  87.8 3.5 %all-to-all-start.2 = ((f32[8,3,512]{2,1,0:T(4,128)}), f32[8,3,512]{2,1,0:T(4,128)S(1)}, u32[]{:S(2)}, u32[]{:S(2)}) async-start(f32[8,3,512]{2,1,0:T(4,128)} %shard_map.71), calls=%async_computation.2 | async-start | bytes 131072 | tf_op jit(solution)/shard_map/all_to_all | solution.py:50
  91.4 30.9 %all-to-all-done.2.parts = f32[8,3,512]{2,1,0:T(4,128)S(1)} async-done(((f32[8,3,512]{2,1,0:T(4,128)}), f32[8,3,512]{2,1,0:T(4,128)S(1)}, u32[]{:S(2)}, u32[]{:S(2)}) %all-to-all-start.2) | async-done | bytes 49184 | tf_op jit(solution)/shard_map/all_to_all | solution.py:50
  122.4 1.8 fusion.17
  124.2 5.7 %shard_map.73 = (f32[16,264,128]{2,1,0:T(8,128)S(1)}, f32[16,264,128]{2,1,0:T(8,128)S(1)}) custom-call(s32[4]{0:T(128)S(1)} %pad_add_fusion.place_ref, bf16[1187,4096]{1,0:T(8,128)(2,1)} %bitcast.40, bf16[1187,256]{1,0:T(8,128)(2,1)S(1)} %get-tuple-element.84.grads, f32[8,128]{1,0:T(8,128)S(1)} %scatter.6.extra), custom_call_target="tpu_custom_call" | custom-call | tf_op jit(solution)/shard_map/pallas_call | solution.py:29
  131.4 5.7 %shard_map.76 = (f32[16,264,128]{2,1,0:T(8,128)S(1)}, f32[16,264,128]{2,1,0:T(8,128)S(1)}) custom-call(s32[4]{0:T(128)S(1)} %pad_add_fusion.place_ref, bf16[1187,4096]{1,0:T(8,128)(2,1)} %bitcast.41, bf16[1187,256]{1,0:T(8,128)(2,1)S(1)} %get-tuple-element.82.grads, f32[8,128]{1,0:T(8,128)S(1)} %scatter.9.extra), custom_call_target="tpu_custom_call" | custom-call | tf_op jit(solution)/shard_map/pallas_call | solution.py:29
  139.2 3.0 %collective-permute-start.9 = (f32[1032,128]{1,0:T(8,128)S(1)}, f32[1032,128]{1,0:T(8,128)S(1)}, u32[]{:S(2)}, u32[]{:S(2)}) collective-permute-start(f32[1032,128]{1,0:T(8,128)S(1)} %get-tuple-element.60), channel_id=1, source_target_pairs={{0,16},{8,24},{16,0},{24,8},{1,17},{9,25},{17,1},{25,9},{2,18},{10... | collective-permute-start | bytes 1585160 | tf_op jit(solution)/shard_map/ppermute | solution.py:253
  143.6 2.2 %collective-permute-start.16 = (f32[1032,128]{1,0:T(8,128)S(1)}, f32[1032,128]{1,0:T(8,128)S(1)}, u32[]{:S(2)}, u32[]{:S(2)}) collective-permute-start(f32[1032,128]{1,0:T(8,128)S(1)} %get-tuple-element.71), channel_id=1, source_target_pairs={{0,64},{32,96},{64,0},{96,32},{1,65},{33,97},{65,1},{97,33},{2,66}... | collective-permute-start | bytes 1585160 | tf_op jit(solution)/shard_map/ppermute | solution.py:253
  145.8 7.0 %collective-permute-done.8.p1 = f32[1032,128]{1,0:T(8,128)S(1)} collective-permute-done((f32[1032,128]{1,0:T(8,128)S(1)}, f32[1032,128]{1,0:T(8,128)S(1)}, u32[]{:S(2)}, u32[]{:S(2)}) %collective-permute-start.8) | collective-permute-done | bytes 528416 | tf_op jit(solution)/shard_map/ppermute | solution.py:253
  154.6 5.5 %collective-permute-done.10.p3 = f32[1032,128]{1,0:T(8,128)S(1)} collective-permute-done((f32[1032,128]{1,0:T(8,128)S(1)}, f32[1032,128]{1,0:T(8,128)S(1)}, u32[]{:S(2)}, u32[]{:S(2)}) %collective-permute-start.10) | collective-permute-done | bytes 528416 | tf_op jit(solution)/shard_map/ppermute | solution.py:253
  165.8 3.5 %collective-permute-start.18 = (f32[264,128]{1,0:T(8,128)S(1)}, f32[264,128]{1,0:T(8,128)S(1)}, u32[]{:S(2)}, u32[]{:S(2)}) collective-permute-start(f32[264,128]{1,0:T(8,128)S(1)} %get-tuple-element.74), channel_id=1, source_target_pairs={{0,8},{8,16},{16,24},{24,0},{1,9},{9,17},{17,25},{25,1},{2,10},{10... | collective-permute-start | bytes 405512 | tf_op jit(solution)/shard_map/ppermute | solution.py:253
  169.2 5.7 %collective-permute-start.19 = (f32[264,128]{1,0:T(8,128)S(1)}, f32[264,128]{1,0:T(8,128)S(1)}, u32[]{:S(2)}, u32[]{:S(2)}) collective-permute-start(f32[264,128]{1,0:T(8,128)S(1)} %get-tuple-element.75), channel_id=1, source_target_pairs={{0,16},{8,24},{16,0},{24,8},{1,17},{9,25},{17,1},{25,9},{2,18},{10... | collective-permute-start | bytes 405512 | tf_op jit(solution)/shard_map/ppermute | solution.py:253
  175.9 2.1 collective-permute-done.19.b2
  177.9 2.0 collective-permute-done.20.b3
  180.8 13.9 %all-to-all-start.3 = ((f32[8,80,128]{2,1,0:T(8,128)}), f32[8,80,128]{2,1,0:T(8,128)S(1)}, u32[]{:S(2)}, u32[]{:S(2)}) async-start(f32[8,80,128]{2,1,0:T(8,128)} %shard_map.79), calls=%async_computation.3 | async-start | bytes 655360 | tf_op jit(solution)/shard_map/all_to_all | solution.py:50
  195.2 10.6 %all-to-all-done.3 = f32[8,80,128]{2,1,0:T(8,128)S(1)} async-done(((f32[8,80,128]{2,1,0:T(8,128)}), f32[8,80,128]{2,1,0:T(8,128)S(1)}, u32[]{:S(2)}, u32[]{:S(2)}) %all-to-all-start.3) | async-done | bytes 327712 | tf_op jit(solution)/shard_map/all_to_all | solution.py:50
  (66 shorter events, 25.5 us)
Async XLA Ops:
  0.6 6.6 %collective-permute-start.2 = (bf16[128,128]{1,0:T(8,128)(2,1)}, bf16[128,128]{1,0:T(8,128)(2,1)S(1)}, u32[]{:S(2)}, u32[]{:S(2)}) collective-permute-start(bf16[128,128]{1,0:T(8,128)(2,1)} %bitcast.34), channel_id=1, source_target_pairs={{0,3},{1,0},{2,1},{3,2},{4,7},{5,4},{6,5},{7,6},{8,11},{9,8},{10,9... | collective-permute-start | bytes 98312 | tf_op jit(solution)/shard_map/ppermute | solution.py:271
  5.3 5.0 %collective-permute-start.1 = (bf16[128,128]{1,0:T(8,128)(2,1)}, bf16[128,128]{1,0:T(8,128)(2,1)S(1)}, u32[]{:S(2)}, u32[]{:S(2)}) collective-permute-start(bf16[128,128]{1,0:T(8,128)(2,1)} %bitcast.35), channel_id=1, source_target_pairs={{0,2},{1,3},{2,0},{3,1},{4,6},{5,7},{6,4},{7,5},{8,10},{9,11},{10,... | collective-permute-start | bytes 98312 | tf_op jit(solution)/shard_map/ppermute | solution.py:271
  5.3 5.9 %collective-permute-start = (bf16[128,128]{1,0:T(8,128)(2,1)}, bf16[128,128]{1,0:T(8,128)(2,1)S(1)}, u32[]{:S(2)}, u32[]{:S(2)}) collective-permute-start(bf16[128,128]{1,0:T(8,128)(2,1)} %bitcast.36), channel_id=1, source_target_pairs={{0,1},{1,2},{2,3},{3,0},{4,5},{5,6},{6,7},{7,4},{8,9},{9,10},{10,1... | collective-permute-start | bytes 98312 | tf_op jit(solution)/shard_map/ppermute | solution.py:271
  47.1 4.3 %collective-permute-start.3 = (bf16[16,512,128]{2,1,0:T(8,128)(2,1)S(1)}, bf16[16,512,128]{2,1,0:T(8,128)(2,1)}, u32[]{:S(2)}, u32[]{:S(2)}) collective-permute-start(bf16[16,512,128]{2,1,0:T(8,128)(2,1)S(1)} %all_to_all.20.own), channel_id=1, source_target_pairs={{0,4},{4,0},{1,5},{5,1},{2,6},{6,2},{3,7},{7,3},{8,12},{12,8},{9,1... | collective-permute-start | bytes 6291464 | tf_op jit(solution)/shard_map/ppermute | solution.py:42
  58.0 64.3 %collective-permute-start.5 = (bf16[1187,256]{1,0:T(8,128)(2,1)S(1)}, bf16[1187,256]{1,0:T(8,128)(2,1)}, u32[]{:S(2)}, u32[]{:S(2)}) collective-permute-start(bf16[1187,256]{1,0:T(8,128)(2,1)S(1)} %shard_map.68), channel_id=1, source_target_pairs={{0,128},{1,129},{2,130},{3,131},{4,132},{5,133},{6,134},{7,135},{8... | collective-permute-start | bytes 1823240 | tf_op jit(solution)/shard_map/ppermute | solution.py:286
  71.6 50.7 %collective-permute-start.6 = (bf16[1187,256]{1,0:T(8,128)(2,1)S(1)}, bf16[1187,256]{1,0:T(8,128)(2,1)S(1)}, u32[]{:S(2)}, u32[]{:S(2)}) collective-permute-start(bf16[1187,256]{1,0:T(8,128)(2,1)S(1)} %shard_map.69), channel_id=1, source_target_pairs={{0,128},{1,129},{2,130},{3,131},{4,132},{5,133},{6,134},{7,135},{8... | collective-permute-start | bytes 1823240 | tf_op jit(solution)/shard_map/ppermute | solution.py:286
  74.0 1.3 collective-permute-start.4
  76.0 11.2 %all-to-all-start.1 = ((f32[16,3,512]{2,1,0:T(4,128)}), f32[16,3,512]{2,1,0:T(4,128)S(1)}, u32[]{:S(2)}, u32[]{:S(2)}) async-start(f32[16,3,512]{2,1,0:T(4,128)} %shard_map.70), calls=%async_computation.1 | async-start | bytes 262144 | tf_op jit(solution)/shard_map/all_to_all | solution.py:50
  87.8 34.5 %all-to-all-start.2 = ((f32[8,3,512]{2,1,0:T(4,128)}), f32[8,3,512]{2,1,0:T(4,128)S(1)}, u32[]{:S(2)}, u32[]{:S(2)}) async-start(f32[8,3,512]{2,1,0:T(4,128)} %shard_map.71), calls=%async_computation.2 | async-start | bytes 131072 | tf_op jit(solution)/shard_map/all_to_all | solution.py:50
  129.9 8.0 %collective-permute-start.7 = (f32[16,264,128]{2,1,0:T(8,128)S(1)}, f32[16,264,128]{2,1,0:T(8,128)S(1)}, u32[]{:S(2)}, u32[]{:S(2)}) collective-permute-start(f32[16,264,128]{2,1,0:T(8,128)S(1)} %get-tuple-element.57), channel_id=1, source_target_pairs={{128,132},{132,128},{129,133},{133,129},{130,134},{134,130},{131,1... | collective-permute-start | bytes 6488072 | tf_op jit(solution)/shard_map/ppermute | solution.py:46
  137.1 5.2 %collective-permute-start.14 = (f32[16,264,128]{2,1,0:T(8,128)S(1)}, f32[16,264,128]{2,1,0:T(8,128)S(1)}, u32[]{:S(2)}, u32[]{:S(2)}) collective-permute-start(f32[16,264,128]{2,1,0:T(8,128)S(1)} %get-tuple-element.68), channel_id=1, source_target_pairs={{128,132},{132,128},{129,133},{133,129},{130,134},{134,130},{131,1... | collective-permute-start | bytes 6488072 | tf_op jit(solution)/shard_map/ppermute | solution.py:46
  138.6 14.1 %collective-permute-start.8 = (f32[1032,128]{1,0:T(8,128)S(1)}, f32[1032,128]{1,0:T(8,128)S(1)}, u32[]{:S(2)}, u32[]{:S(2)}) collective-permute-start(f32[1032,128]{1,0:T(8,128)S(1)} %get-tuple-element.59), channel_id=1, source_target_pairs={{0,8},{8,16},{16,24},{24,0},{1,9},{9,17},{17,25},{25,1},{2,10},{10... | collective-permute-start | bytes 1585160 | tf_op jit(solution)/shard_map/ppermute | solution.py:253
  139.2 15.4 %collective-permute-start.9 = (f32[1032,128]{1,0:T(8,128)S(1)}, f32[1032,128]{1,0:T(8,128)S(1)}, u32[]{:S(2)}, u32[]{:S(2)}) collective-permute-start(f32[1032,128]{1,0:T(8,128)S(1)} %get-tuple-element.60), channel_id=1, source_target_pairs={{0,16},{8,24},{16,0},{24,8},{1,17},{9,25},{17,1},{25,9},{2,18},{10... | collective-permute-start | bytes 1585160 | tf_op jit(solution)/shard_map/ppermute | solution.py:253
  142.3 17.9 %collective-permute-start.10 = (f32[1032,128]{1,0:T(8,128)S(1)}, f32[1032,128]{1,0:T(8,128)S(1)}, u32[]{:S(2)}, u32[]{:S(2)}) collective-permute-start(f32[1032,128]{1,0:T(8,128)S(1)} %get-tuple-element.61), channel_id=1, source_target_pairs={{0,24},{8,0},{16,8},{24,16},{1,25},{9,1},{17,9},{25,17},{2,26},{10... | collective-permute-start | bytes 1585160 | tf_op jit(solution)/shard_map/ppermute | solution.py:253
  143.1 21.5 %collective-permute-start.15 = (f32[1032,128]{1,0:T(8,128)S(1)}, f32[1032,128]{1,0:T(8,128)S(1)}, u32[]{:S(2)}, u32[]{:S(2)}) collective-permute-start(f32[1032,128]{1,0:T(8,128)S(1)} %get-tuple-element.70), channel_id=1, source_target_pairs={{0,32},{32,64},{64,96},{96,0},{1,33},{33,65},{65,97},{97,1},{2,34}... | collective-permute-start | bytes 1585160 | tf_op jit(solution)/shard_map/ppermute | solution.py:253
  143.6 21.4 %collective-permute-start.16 = (f32[1032,128]{1,0:T(8,128)S(1)}, f32[1032,128]{1,0:T(8,128)S(1)}, u32[]{:S(2)}, u32[]{:S(2)}) collective-permute-start(f32[1032,128]{1,0:T(8,128)S(1)} %get-tuple-element.71), channel_id=1, source_target_pairs={{0,64},{32,96},{64,0},{96,32},{1,65},{33,97},{65,1},{97,33},{2,66}... | collective-permute-start | bytes 1585160 | tf_op jit(solution)/shard_map/ppermute | solution.py:253
  152.7 12.9 %collective-permute-start.17 = (f32[1032,128]{1,0:T(8,128)S(1)}, f32[1032,128]{1,0:T(8,128)S(1)}, u32[]{:S(2)}, u32[]{:S(2)}) collective-permute-start(f32[1032,128]{1,0:T(8,128)S(1)} %get-tuple-element.72), channel_id=1, source_target_pairs={{0,96},{32,0},{64,32},{96,64},{1,97},{33,1},{65,33},{97,65},{2,98}... | collective-permute-start | bytes 1585160 | tf_op jit(solution)/shard_map/ppermute | solution.py:253
  160.3 14.7 %collective-permute-start.11 = (f32[264,128]{1,0:T(8,128)S(1)}, f32[264,128]{1,0:T(8,128)S(1)}, u32[]{:S(2)}, u32[]{:S(2)}) collective-permute-start(f32[264,128]{1,0:T(8,128)S(1)} %get-tuple-element.63), channel_id=1, source_target_pairs={{0,32},{32,64},{64,96},{96,0},{1,33},{33,65},{65,97},{97,1},{2,34}... | collective-permute-start | bytes 405512 | tf_op jit(solution)/shard_map/ppermute | solution.py:253
  161.2 13.7 %collective-permute-start.12 = (f32[264,128]{1,0:T(8,128)S(1)}, f32[264,128]{1,0:T(8,128)S(1)}, u32[]{:S(2)}, u32[]{:S(2)}) collective-permute-start(f32[264,128]{1,0:T(8,128)S(1)} %get-tuple-element.64), channel_id=1, source_target_pairs={{0,64},{32,96},{64,0},{96,32},{1,65},{33,97},{65,1},{97,33},{2,66}... | collective-permute-start | bytes 405512 | tf_op jit(solution)/shard_map/ppermute | solution.py:253
  164.6 10.4 %collective-permute-start.13 = (f32[264,128]{1,0:T(8,128)S(1)}, f32[264,128]{1,0:T(8,128)S(1)}, u32[]{:S(2)}, u32[]{:S(2)}) collective-permute-start(f32[264,128]{1,0:T(8,128)S(1)} %get-tuple-element.65), channel_id=1, source_target_pairs={{0,96},{32,0},{64,32},{96,64},{1,97},{33,1},{65,33},{97,65},{2,98}... | collective-permute-start | bytes 405512 | tf_op jit(solution)/shard_map/ppermute | solution.py:253
  165.8 10.1 %collective-permute-start.18 = (f32[264,128]{1,0:T(8,128)S(1)}, f32[264,128]{1,0:T(8,128)S(1)}, u32[]{:S(2)}, u32[]{:S(2)}) collective-permute-start(f32[264,128]{1,0:T(8,128)S(1)} %get-tuple-element.74), channel_id=1, source_target_pairs={{0,8},{8,16},{16,24},{24,0},{1,9},{9,17},{17,25},{25,1},{2,10},{10... | collective-permute-start | bytes 405512 | tf_op jit(solution)/shard_map/ppermute | solution.py:253
  169.2 8.7 %collective-permute-start.19 = (f32[264,128]{1,0:T(8,128)S(1)}, f32[264,128]{1,0:T(8,128)S(1)}, u32[]{:S(2)}, u32[]{:S(2)}) collective-permute-start(f32[264,128]{1,0:T(8,128)S(1)} %get-tuple-element.75), channel_id=1, source_target_pairs={{0,16},{8,24},{16,0},{24,8},{1,17},{9,25},{17,1},{25,9},{2,18},{10... | collective-permute-start | bytes 405512 | tf_op jit(solution)/shard_map/ppermute | solution.py:253
  174.9 5.0 %collective-permute-start.20 = (f32[264,128]{1,0:T(8,128)S(1)}, f32[264,128]{1,0:T(8,128)S(1)}, u32[]{:S(2)}, u32[]{:S(2)}) collective-permute-start(f32[264,128]{1,0:T(8,128)S(1)} %get-tuple-element.76), channel_id=1, source_target_pairs={{0,24},{8,0},{16,8},{24,16},{1,25},{9,1},{17,9},{25,17},{2,26},{10... | collective-permute-start | bytes 405512 | tf_op jit(solution)/shard_map/ppermute | solution.py:253
  180.8 25.0 %all-to-all-start.3 = ((f32[8,80,128]{2,1,0:T(8,128)}), f32[8,80,128]{2,1,0:T(8,128)S(1)}, u32[]{:S(2)}, u32[]{:S(2)}) async-start(f32[8,80,128]{2,1,0:T(8,128)} %shard_map.79), calls=%async_computation.3 | async-start | bytes 655360 | tf_op jit(solution)/shard_map/all_to_all | solution.py:50
  (3 other events, 42.3 us)

commit v6 on v5

--- a/solution.py
+++ b/solution.py
@@ -214,25 +214,44 @@
     return (parts[0] + parts[2]) + (parts[1] + parts[3])
 
 
-def pair_sum_kernel(x_first, place_ref, keep, got, *outs):
+def pair_sum_kernel(x_first, place_ref, keep, got, stay, right, left, ahead, behind):
     y, x = place_ref[2], place_ref[3]
     rows = keep.shape[1] - EXTRA
-    for first, out in enumerate(outs):
+    extra = keep[0, rows:] + got[0, rows:]
+    for first in range(4):
         for second in range(4):
             kx, ky = (first, second) if x_first else (second, first)
             chip = lax.rem(y + ky, 4) * 4 + lax.rem(x + kx, 4)
-            at = slice(second * rows, (second + 1) * rows)
+            if first == 2:
+                out, slot = (ahead, second) if second < 2 else (behind, second - 2)
+            else:
+                out, slot = (stay, right, None, left)[first], second
+            at = slice(slot * rows, (slot + 1) * rows)
             out[at] = keep[chip, :rows] + got[chip, :rows]
-        out[4 * rows :] = keep[0, rows:] + got[0, rows:]
-
-
-def line_sum_kernel(p0, p1, p2, p3, *outs):
-    parts = (p0, p1, p2, p3)
+    stay[4 * rows :] = extra
+    ahead[2 * rows :] = extra
+
+
+def relay_kernel(stay, right, left, ahead, behind, to_right, to_left):
+    rows = right.shape[0]
+    half = rows // 2
+    to_right[:half] = right[:half] + ahead[:half]
+    to_right[half:rows] = right[half:]
+    to_right[rows : rows + EXTRA] = stay[rows:]
+    to_right[rows + EXTRA :] = ahead[half:]
+    to_left[:half] = left[:half]
+    to_left[half:rows] = left[half:] + behind[...]
+    to_left[rows:] = stay[rows:]
+
+
+def line_sum_kernel(stay, from_left, from_right, *outs):
     rows = outs[0].shape[0] - EXTRA
-    extra = line_total([p[4 * rows :] for p in parts])
+    end = 4 * rows
+    near = from_left[end : end + EXTRA] + from_right[end:]
+    extra = (stay[end:] + from_left[end + EXTRA :]) + near
     for k, out in enumerate(outs):
         at = slice(k * rows, (k + 1) * rows)
-        out[:rows] = line_total([p[at] for p in parts])
+        out[:rows] = stay[at] + (from_left[at] + from_right[at])
         out[rows:] = extra
 
 
@@ -248,11 +267,8 @@
         out[plane, part + EXTRA :] = tails[1]
 
 
-def scattered(parts, axis):
-    def moved(part, step):
-        return lax.ppermute(part, axis, [(i, (i + step) % 4) for i in range(4)])
-
-    return [parts[0]] + [moved(parts[k], k) for k in range(1, 4)]
+def moved(part, axis, step):
+    return lax.ppermute(part, axis, [(i, (i + step) % 4) for i in range(4)])
 
 
 def shards(hidden, head_weight, labels, loss_mask):
@@ -326,20 +342,48 @@
         extra = jnp.zeros((EXTRA, wide), F32).at[:2].set(diverge.reshape(2, wide))
         parts.append(split_grads(place, weights, grads, extra))
     orders = (("x", "y"), ("y", "x"))
-    array_of = lambda rows: [array((rows + EXTRA, wide), F32)] * 4
+    arrays = lambda *heights: [array((height, wide), F32) for height in heights]
+    full, edge = 4 * half, EXTRA
     pieces = [
         vmem_call(
             functools.partial(pair_sum_kernel, c == 0),
-            array_of(4 * half),
+            arrays(full + edge, full, full, full // 2 + edge, full // 2),
             keep,
             swapped_in_student(send),
             place=place,
         )
         for c, (keep, send) in enumerate(parts)
     ]
-    pieces = [scattered(pieces[c], orders[c][0]) for c in range(2)]
-    pieces = [vmem_call(line_sum_kernel, array_of(half), *pieces[c]) for c in range(2)]
-    pieces = [scattered(pieces[c], orders[c][1]) for c in range(2)]
+    relayed = []
+    for c, (stay, right, left, ahead, behind) in enumerate(pieces):
+        axis = orders[c][0]
+        relayed.append(
+            vmem_call(
+                relay_kernel,
+                arrays(full + 2 * edge, full + edge),
+                stay,
+                right,
+                left,
+                moved(ahead, axis, 1),
+                moved(behind, axis, 3),
+            )
+        )
+    lines = []
+    for c, (to_right, to_left) in enumerate(relayed):
+        axis = orders[c][0]
+        lines.append(
+            vmem_call(
+                line_sum_kernel,
+                arrays(*[half + edge] * 4),
+                pieces[c][0],
+                moved(to_right, axis, 1),
+                moved(to_left, axis, 3),
+            )
+        )
+    pieces = [
+        [lines[c][0]] + [moved(lines[c][k], orders[c][1], k) for k in range(1, 4)]
+        for c in range(2)
+    ]
 
     part = half // 4
     last = vmem_call(

time: 208 us -> 200 us (0.962)
  waiting for transfers between devices: 79.8 us -> 72.4 us
  starting transfers between devices: 56.4 us -> 54.2 us
    ppermute x12 -> x14, waiting for transfers between devices: 21 us -> 13.6 us  [moved(): return lax.ppermute(part, axis, [(i, (i + step) % 4) for i in range(4)])]
    all_to_all x3, starting transfers between devices: 21.8 us -> 17.9 us  [exchanged(): return lax.all_to_all(x, axes, 0, 0)]
    ppermute x12 -> x14, starting transfers between devices: 19.2 us -> 21 us  [moved(): return lax.ppermute(part, axis, [(i, (i + step) % 4) for i in range(4)])]
    pallas_call x13 -> x15, Pallas kernels: 29.5 us -> 29.7 us  [vmem_call(): pl.pallas_call(kernel, out_shape=out_shape, in_specs=[in_smem()] * len(sc...]
  transfers between devices with their start and end apart: 24 -> 26, of which waited for: 16 -> 16; matrix products, arithmetic and copies ran while one was open for 1% -> 1% of each run, Pallas kernels for 8% -> 8%
where the time goes in v6:
time: 200 us; the launch traced here: 198 us
  waiting for transfers between devices  72.4 us (36%)
  starting transfers between devices  54.2 us (27%)
  blocking collectives  34.2 us (17%)
  Pallas kernels  29.7 us (15%)
  other arithmetic  4.24 us (2%)
  local copies, waits for them, and re-layouts  2.01 us (1%)
    all_to_all x3, waiting for transfers between devices, exchanged(): return lax.all_to_all(x, axes, 0, 0)  48.2 us
    all_to_all x1, blocking collectives, exchanged(): return lax.all_to_all(x, axes, 0, 0)  34.2 us
    pallas_call x15, Pallas kernels, vmem_call(): pl.pallas_call(kernel, out_shape=out_shape, in_specs=[in_smem()] * len(sc...  29.7 us
    ppermute x14, starting transfers between devices, moved(): return lax.ppermute(part, axis, [(i, (i + step) % 4) for i in range(4)])  21 us
    all_to_all x3, starting transfers between devices, exchanged(): return lax.all_to_all(x, axes, 0, 0)  17.9 us
    ppermute x14, waiting for transfers between devices, moved(): return lax.ppermute(part, axis, [(i, (i + step) % 4) for i in range(4)])  13.6 us
    ppermute x2, starting transfers between devices, shards(): sent.append(lax.ppermute(own_z[c], 'grp', [(0, 1)]))  8.32 us
    ppermute x2, waiting for transfers between devices, swapped(): return lax.ppermute(x, axis, [(0, 1), (1, 0)])  5.43 us
  transfers between devices with their start and end apart: 26, of which 16 were waited for; matrix products, arithmetic and copies ran while one was open for 1% of the time, Pallas kernels for 8%

profile of v6, /device:TPU:2, one launch (start us, length us, event | category | flops | bytes accessed | tf_op | source)
XLA Modules:
  0.0 197.6 jit_solution(6704740938401232343)
XLA Ops:
  0.6 4.7 %collective-permute-start.2 = (bf16[128,128]{1,0:T(8,128)(2,1)}, bf16[128,128]{1,0:T(8,128)(2,1)S(1)}, u32[]{:S(2)}, u32[]{:S(2)}) collective-permute-start(bf16[128,128]{1,0:T(8,128)(2,1)} %bitcast.34), channel_id=1, source_target_pairs={{0,3},{1,0},{2,1},{3,2},{4,7},{5,4},{6,5},{7,6},{8,11},{9,8},{10,9... | collective-permute-start | bytes 98312 | tf_op jit(solution)/shard_map/ppermute | solution.py:287
  7.2 3.1 %collective-permute-done.1.p2 = bf16[128,128]{1,0:T(8,128)(2,1)S(1)} collective-permute-done((bf16[128,128]{1,0:T(8,128)(2,1)}, bf16[128,128]{1,0:T(8,128)(2,1)S(1)}, u32[]{:S(2)}, u32[]{:S(2)}) %collective-permute-start.1) | collective-permute-done | bytes 32800 | tf_op jit(solution)/shard_map/ppermute | solution.py:287
  12.9 34.2 %all_to_all.20.own = bf16[16,512,128]{2,1,0:T(8,128)(2,1)S(1)} all-to-all(bf16[16,512,128]{2,1,0:T(8,128)(2,1)S(1)} %shard_map.67), channel_id=1, replica_groups=mesh['grp'=2,'y'=4,'x'=4,'core'=2,'tok'=4] {'y','x'}, dimensions={0} | all-to-all | bytes 4194304 | tf_op jit(solution)/shard_map/all_to_all | solution.py:50
  47.1 4.3 %collective-permute-done.3.sibling = bf16[16,512,128]{2,1,0:T(8,128)(2,1)} collective-permute-done((bf16[16,512,128]{2,1,0:T(8,128)(2,1)S(1)}, bf16[16,512,128]{2,1,0:T(8,128)(2,1)}, u32[]{:S(2)}, u32[]{:S(2)}) %collective-permute-start.3) | collective-permute-done | bytes 2097184 | tf_op jit(solution)/shard_map/ppermute | solution.py:42
  51.3 6.7 %shard_map.68 = bf16[1187,256]{1,0:T(8,128)(2,1)S(1)} custom-call(s32[4]{0:T(128)S(1)} %pad_add_fusion.place_ref, bf16[1187,4096]{1,0:T(8,128)(2,1)} %bitcast.38, bf16[16,512,128]{2,1,0:T(8,128)(2,1)S(1)} %all_to_all.20.own, bf16[16,512,128]{2,1,0:T(8,128)(2,1)} %collective-permute-done.3.sibling), custom_call_target="tpu_custom_call" | custom-call | tf_op jit(solution)/shard_map/pallas_call | solution.py:29
  58.0 7.0 %collective-permute-start.5 = (bf16[1187,256]{1,0:T(8,128)(2,1)S(1)}, bf16[1187,256]{1,0:T(8,128)(2,1)}, u32[]{:S(2)}, u32[]{:S(2)}) collective-permute-start(bf16[1187,256]{1,0:T(8,128)(2,1)S(1)} %shard_map.68), channel_id=1, source_target_pairs={{0,128},{1,129},{2,130},{3,131},{4,132},{5,133},{6,134},{7,135},{8... | collective-permute-start | bytes 1823240 | tf_op jit(solution)/shard_map/ppermute | solution.py:302
  65.0 6.6 %shard_map.69 = bf16[1187,256]{1,0:T(8,128)(2,1)S(1)} custom-call(s32[4]{0:T(128)S(1)} %pad_add_fusion.place_ref, bf16[1187,4096]{1,0:T(8,128)(2,1)} %bitcast.39, bf16[16,512,128]{2,1,0:T(8,128)(2,1)S(1)} %all_to_all.20.own, bf16[16,512,128]{2,1,0:T(8,128)(2,1)} %collective-permute-done.3.sibling), custom_call_target="tpu_custom_call" | custom-call | tf_op jit(solution)/shard_map/pallas_call | solution.py:29
  76.0 4.4 %all-to-all-start.1 = ((f32[16,3,512]{2,1,0:T(4,128)}), f32[16,3,512]{2,1,0:T(4,128)S(1)}, u32[]{:S(2)}, u32[]{:S(2)}) async-start(f32[16,3,512]{2,1,0:T(4,128)} %shard_map.70), calls=%async_computation.1 | async-start | bytes 262144 | tf_op jit(solution)/shard_map/all_to_all | solution.py:50
  80.5 6.7 %all-to-all-done.1.parts = f32[16,3,512]{2,1,0:T(4,128)S(1)} async-done(((f32[16,3,512]{2,1,0:T(4,128)}), f32[16,3,512]{2,1,0:T(4,128)S(1)}, u32[]{:S(2)}, u32[]{:S(2)}) %all-to-all-start.1) | async-done | bytes 98336 | tf_op jit(solution)/shard_map/all_to_all | solution.py:50
  87.8 3.5 %all-to-all-start.2 = ((f32[8,3,512]{2,1,0:T(4,128)}), f32[8,3,512]{2,1,0:T(4,128)S(1)}, u32[]{:S(2)}, u32[]{:S(2)}) async-start(f32[8,3,512]{2,1,0:T(4,128)} %shard_map.71), calls=%async_computation.2 | async-start | bytes 131072 | tf_op jit(solution)/shard_map/all_to_all | solution.py:50
  91.4 30.9 %all-to-all-done.2.parts = f32[8,3,512]{2,1,0:T(4,128)S(1)} async-done(((f32[8,3,512]{2,1,0:T(4,128)}), f32[8,3,512]{2,1,0:T(4,128)S(1)}, u32[]{:S(2)}, u32[]{:S(2)}) %all-to-all-start.2) | async-done | bytes 49184 | tf_op jit(solution)/shard_map/all_to_all | solution.py:50
  124.2 5.7 %shard_map.73 = (f32[16,264,128]{2,1,0:T(8,128)S(1)}, f32[16,264,128]{2,1,0:T(8,128)S(1)}) custom-call(s32[4]{0:T(128)S(1)} %pad_add_fusion.place_ref, bf16[1187,4096]{1,0:T(8,128)(2,1)} %bitcast.40, bf16[1187,256]{1,0:T(8,128)(2,1)S(1)} %get-tuple-element.96.grads, f32[8,128]{1,0:T(8,128)S(1)} %scatter.6.extra), custom_call_target="tpu_custom_call" | custom-call | tf_op jit(solution)/shard_map/pallas_call | solution.py:29
  131.4 5.7 %shard_map.77 = (f32[16,264,128]{2,1,0:T(8,128)S(1)}, f32[16,264,128]{2,1,0:T(8,128)S(1)}) custom-call(s32[4]{0:T(128)S(1)} %pad_add_fusion.place_ref, bf16[1187,4096]{1,0:T(8,128)(2,1)} %bitcast.41, bf16[1187,256]{1,0:T(8,128)(2,1)S(1)} %get-tuple-element.94.grads, f32[8,128]{1,0:T(8,128)S(1)} %scatter.9.extra), custom_call_target="tpu_custom_call" | custom-call | tf_op jit(solution)/shard_map/pallas_call | solution.py:29
  141.7 3.2 %collective-permute-start.17 = (f32[512,128]{1,0:T(8,128)S(1)}, f32[512,128]{1,0:T(8,128)S(1)}, u32[]{:S(2)}, u32[]{:S(2)}) collective-permute-start(f32[512,128]{1,0:T(8,128)S(1)} %get-tuple-element.82), channel_id=1, source_target_pairs={{0,96},{32,0},{64,32},{96,64},{1,97},{33,1},{65,33},{97,65},{2,98}... | collective-permute-start | bytes 786440 | tf_op jit(solution)/shard_map/ppermute | solution.py:271
  144.9 2.3 %collective-permute-done.9.behind = f32[512,128]{1,0:T(8,128)S(1)} collective-permute-done((f32[512,128]{1,0:T(8,128)S(1)}, f32[512,128]{1,0:T(8,128)S(1)}, u32[]{:S(2)}, u32[]{:S(2)}) %collective-permute-start.9) | collective-permute-done | bytes 262176 | tf_op jit(solution)/shard_map/ppermute | solution.py:271
  148.0 2.5 %collective-permute-start.11 = (f32[1032,128]{1,0:T(8,128)S(1)}, f32[1032,128]{1,0:T(8,128)S(1)}, u32[]{:S(2)}, u32[]{:S(2)}) collective-permute-start(f32[1032,128]{1,0:T(8,128)S(1)} %get-tuple-element.70), channel_id=1, source_target_pairs={{0,24},{8,0},{16,8},{24,16},{1,25},{9,1},{17,9},{25,17},{2,26},{10... | collective-permute-start | bytes 1585160 | tf_op jit(solution)/shard_map/ppermute | solution.py:271
  152.3 3.2 %collective-permute-start.19 = (f32[1032,128]{1,0:T(8,128)S(1)}, f32[1032,128]{1,0:T(8,128)S(1)}, u32[]{:S(2)}, u32[]{:S(2)}) collective-permute-start(f32[1032,128]{1,0:T(8,128)S(1)} %get-tuple-element.84), channel_id=1, source_target_pairs={{0,96},{32,0},{64,32},{96,64},{1,97},{33,1},{65,33},{97,65},{2,98}... | collective-permute-start | bytes 1585160 | tf_op jit(solution)/shard_map/ppermute | solution.py:271
  155.6 4.5 %collective-permute-done.11.from_right = f32[1032,128]{1,0:T(8,128)S(1)} collective-permute-done((f32[1032,128]{1,0:T(8,128)S(1)}, f32[1032,128]{1,0:T(8,128)S(1)}, u32[]{:S(2)}, u32[]{:S(2)}) %collective-permute-start.11) | collective-permute-done | bytes 528416 | tf_op jit(solution)/shard_map/ppermute | solution.py:271
  160.4 2.6 %collective-permute-start.13 = (f32[264,128]{1,0:T(8,128)S(1)}, f32[264,128]{1,0:T(8,128)S(1)}, u32[]{:S(2)}, u32[]{:S(2)}) collective-permute-start(f32[264,128]{1,0:T(8,128)S(1)} %get-tuple-element.73), channel_id=1, source_target_pairs={{0,64},{32,96},{64,0},{96,32},{1,65},{33,97},{65,1},{97,33},{2,66}... | collective-permute-start | bytes 405512 | tf_op jit(solution)/shard_map/ppermute | solution.py:271
  164.6 1.9 collective-permute-start.20
  166.5 2.6 %collective-permute-start.21 = (f32[264,128]{1,0:T(8,128)S(1)}, f32[264,128]{1,0:T(8,128)S(1)}, u32[]{:S(2)}, u32[]{:S(2)}) collective-permute-start(f32[264,128]{1,0:T(8,128)S(1)} %get-tuple-element.87), channel_id=1, source_target_pairs={{0,16},{8,24},{16,0},{24,8},{1,17},{9,25},{17,1},{25,9},{2,18},{10... | collective-permute-start | bytes 405512 | tf_op jit(solution)/shard_map/ppermute | solution.py:271
  170.7 2.4 %collective-permute-done.21.b2 = f32[264,128]{1,0:T(8,128)S(1)} collective-permute-done((f32[264,128]{1,0:T(8,128)S(1)}, f32[264,128]{1,0:T(8,128)S(1)}, u32[]{:S(2)}, u32[]{:S(2)}) %collective-permute-start.21) | collective-permute-done | bytes 135200 | tf_op jit(solution)/shard_map/ppermute | solution.py:271
  175.3 9.9 %all-to-all-start.3 = ((f32[8,80,128]{2,1,0:T(8,128)}), f32[8,80,128]{2,1,0:T(8,128)S(1)}, u32[]{:S(2)}, u32[]{:S(2)}) async-start(f32[8,80,128]{2,1,0:T(8,128)} %shard_map.81), calls=%async_computation.3 | async-start | bytes 655360 | tf_op jit(solution)/shard_map/all_to_all | solution.py:50
  185.8 10.6 %all-to-all-done.3 = f32[8,80,128]{2,1,0:T(8,128)S(1)} async-done(((f32[8,80,128]{2,1,0:T(8,128)}), f32[8,80,128]{2,1,0:T(8,128)S(1)}, u32[]{:S(2)}, u32[]{:S(2)}) %all-to-all-start.3) | async-done | bytes 327712 | tf_op jit(solution)/shard_map/all_to_all | solution.py:50
  (72 shorter events, 27.6 us)
Async XLA Ops:
  0.6 6.6 %collective-permute-start.2 = (bf16[128,128]{1,0:T(8,128)(2,1)}, bf16[128,128]{1,0:T(8,128)(2,1)S(1)}, u32[]{:S(2)}, u32[]{:S(2)}) collective-permute-start(bf16[128,128]{1,0:T(8,128)(2,1)} %bitcast.34), channel_id=1, source_target_pairs={{0,3},{1,0},{2,1},{3,2},{4,7},{5,4},{6,5},{7,6},{8,11},{9,8},{10,9... | collective-permute-start | bytes 98312 | tf_op jit(solution)/shard_map/ppermute | solution.py:287
  5.3 5.0 %collective-permute-start.1 = (bf16[128,128]{1,0:T(8,128)(2,1)}, bf16[128,128]{1,0:T(8,128)(2,1)S(1)}, u32[]{:S(2)}, u32[]{:S(2)}) collective-permute-start(bf16[128,128]{1,0:T(8,128)(2,1)} %bitcast.35), channel_id=1, source_target_pairs={{0,2},{1,3},{2,0},{3,1},{4,6},{5,7},{6,4},{7,5},{8,10},{9,11},{10,... | collective-permute-start | bytes 98312 | tf_op jit(solution)/shard_map/ppermute | solution.py:287
  5.3 5.9 %collective-permute-start = (bf16[128,128]{1,0:T(8,128)(2,1)}, bf16[128,128]{1,0:T(8,128)(2,1)S(1)}, u32[]{:S(2)}, u32[]{:S(2)}) collective-permute-start(bf16[128,128]{1,0:T(8,128)(2,1)} %bitcast.36), channel_id=1, source_target_pairs={{0,1},{1,2},{2,3},{3,0},{4,5},{5,6},{6,7},{7,4},{8,9},{9,10},{10,1... | collective-permute-start | bytes 98312 | tf_op jit(solution)/shard_map/ppermute | solution.py:287
  47.1 4.3 %collective-permute-start.3 = (bf16[16,512,128]{2,1,0:T(8,128)(2,1)S(1)}, bf16[16,512,128]{2,1,0:T(8,128)(2,1)}, u32[]{:S(2)}, u32[]{:S(2)}) collective-permute-start(bf16[16,512,128]{2,1,0:T(8,128)(2,1)S(1)} %all_to_all.20.own), channel_id=1, source_target_pairs={{0,4},{4,0},{1,5},{5,1},{2,6},{6,2},{3,7},{7,3},{8,12},{12,8},{9,1... | collective-permute-start | bytes 6291464 | tf_op jit(solution)/shard_map/ppermute | solution.py:42
  58.0 64.3 %collective-permute-start.5 = (bf16[1187,256]{1,0:T(8,128)(2,1)S(1)}, bf16[1187,256]{1,0:T(8,128)(2,1)}, u32[]{:S(2)}, u32[]{:S(2)}) collective-permute-start(bf16[1187,256]{1,0:T(8,128)(2,1)S(1)} %shard_map.68), channel_id=1, source_target_pairs={{0,128},{1,129},{2,130},{3,131},{4,132},{5,133},{6,134},{7,135},{8... | collective-permute-start | bytes 1823240 | tf_op jit(solution)/shard_map/ppermute | solution.py:302
  71.7 50.7 %collective-permute-start.6 = (bf16[1187,256]{1,0:T(8,128)(2,1)S(1)}, bf16[1187,256]{1,0:T(8,128)(2,1)S(1)}, u32[]{:S(2)}, u32[]{:S(2)}) collective-permute-start(bf16[1187,256]{1,0:T(8,128)(2,1)S(1)} %shard_map.69), channel_id=1, source_target_pairs={{0,128},{1,129},{2,130},{3,131},{4,132},{5,133},{6,134},{7,135},{8... | collective-permute-start | bytes 1823240 | tf_op jit(solution)/shard_map/ppermute | solution.py:302
  76.0 11.2 %all-to-all-start.1 = ((f32[16,3,512]{2,1,0:T(4,128)}), f32[16,3,512]{2,1,0:T(4,128)S(1)}, u32[]{:S(2)}, u32[]{:S(2)}) async-start(f32[16,3,512]{2,1,0:T(4,128)} %shard_map.70), calls=%async_computation.1 | async-start | bytes 262144 | tf_op jit(solution)/shard_map/all_to_all | solution.py:50
  87.8 34.5 %all-to-all-start.2 = ((f32[8,3,512]{2,1,0:T(4,128)}), f32[8,3,512]{2,1,0:T(4,128)S(1)}, u32[]{:S(2)}, u32[]{:S(2)}) async-start(f32[8,3,512]{2,1,0:T(4,128)} %shard_map.71), calls=%async_computation.2 | async-start | bytes 131072 | tf_op jit(solution)/shard_map/all_to_all | solution.py:50
  129.9 8.0 %collective-permute-start.7 = (f32[16,264,128]{2,1,0:T(8,128)S(1)}, f32[16,264,128]{2,1,0:T(8,128)S(1)}, u32[]{:S(2)}, u32[]{:S(2)}) collective-permute-start(f32[16,264,128]{2,1,0:T(8,128)S(1)} %get-tuple-element.63), channel_id=1, source_target_pairs={{128,132},{132,128},{129,133},{133,129},{130,134},{134,130},{131,1... | collective-permute-start | bytes 6488072 | tf_op jit(solution)/shard_map/ppermute | solution.py:46
  138.6 9.1 %collective-permute-start.8 = (f32[520,128]{1,0:T(8,128)S(1)}, f32[520,128]{1,0:T(8,128)S(1)}, u32[]{:S(2)}, u32[]{:S(2)}) collective-permute-start(f32[520,128]{1,0:T(8,128)S(1)} %get-tuple-element.67), channel_id=1, source_target_pairs={{0,8},{8,16},{16,24},{24,0},{1,9},{9,17},{17,25},{25,1},{2,10},{10... | collective-permute-start | bytes 798728 | tf_op jit(solution)/shard_map/ppermute | solution.py:271
  139.2 7.9 %collective-permute-start.9 = (f32[512,128]{1,0:T(8,128)S(1)}, f32[512,128]{1,0:T(8,128)S(1)}, u32[]{:S(2)}, u32[]{:S(2)}) collective-permute-start(f32[512,128]{1,0:T(8,128)S(1)} %get-tuple-element.68), channel_id=1, source_target_pairs={{0,24},{8,0},{16,8},{24,16},{1,25},{9,1},{17,9},{25,17},{2,26},{10... | collective-permute-start | bytes 786440 | tf_op jit(solution)/shard_map/ppermute | solution.py:271
  141.6 10.6 %collective-permute-start.16 = (f32[520,128]{1,0:T(8,128)S(1)}, f32[520,128]{1,0:T(8,128)S(1)}, u32[]{:S(2)}, u32[]{:S(2)}) collective-permute-start(f32[520,128]{1,0:T(8,128)S(1)} %get-tuple-element.81), channel_id=1, source_target_pairs={{0,32},{32,64},{64,96},{96,0},{1,33},{33,65},{65,97},{97,1},{2,34}... | collective-permute-start | bytes 798728 | tf_op jit(solution)/shard_map/ppermute | solution.py:271
  141.7 9.9 %collective-permute-start.17 = (f32[512,128]{1,0:T(8,128)S(1)}, f32[512,128]{1,0:T(8,128)S(1)}, u32[]{:S(2)}, u32[]{:S(2)}) collective-permute-start(f32[512,128]{1,0:T(8,128)S(1)} %get-tuple-element.82), channel_id=1, source_target_pairs={{0,96},{32,0},{64,32},{96,64},{1,97},{33,1},{65,33},{97,65},{2,98}... | collective-permute-start | bytes 786440 | tf_op jit(solution)/shard_map/ppermute | solution.py:271
  147.8 12.2 %collective-permute-start.10 = (f32[1040,128]{1,0:T(8,128)S(1)}, f32[1040,128]{1,0:T(8,128)S(1)}, u32[]{:S(2)}, u32[]{:S(2)}) collective-permute-start(f32[1040,128]{1,0:T(8,128)S(1)} %get-tuple-element.69), channel_id=1, source_target_pairs={{0,8},{8,16},{16,24},{24,0},{1,9},{9,17},{17,25},{25,1},{2,10},{10... | collective-permute-start | bytes 1597448 | tf_op jit(solution)/shard_map/ppermute | solution.py:271
  148.0 12.0 %collective-permute-start.11 = (f32[1032,128]{1,0:T(8,128)S(1)}, f32[1032,128]{1,0:T(8,128)S(1)}, u32[]{:S(2)}, u32[]{:S(2)}) collective-permute-start(f32[1032,128]{1,0:T(8,128)S(1)} %get-tuple-element.70), channel_id=1, source_target_pairs={{0,24},{8,0},{16,8},{24,16},{1,25},{9,1},{17,9},{25,17},{2,26},{10... | collective-permute-start | bytes 1585160 | tf_op jit(solution)/shard_map/ppermute | solution.py:271
  152.2 12.3 %collective-permute-start.18 = (f32[1040,128]{1,0:T(8,128)S(1)}, f32[1040,128]{1,0:T(8,128)S(1)}, u32[]{:S(2)}, u32[]{:S(2)}) collective-permute-start(f32[1040,128]{1,0:T(8,128)S(1)} %get-tuple-element.83), channel_id=1, source_target_pairs={{0,32},{32,64},{64,96},{96,0},{1,33},{33,65},{65,97},{97,1},{2,34}... | collective-permute-start | bytes 1597448 | tf_op jit(solution)/shard_map/ppermute | solution.py:271
  152.3 12.2 %collective-permute-start.19 = (f32[1032,128]{1,0:T(8,128)S(1)}, f32[1032,128]{1,0:T(8,128)S(1)}, u32[]{:S(2)}, u32[]{:S(2)}) collective-permute-start(f32[1032,128]{1,0:T(8,128)S(1)} %get-tuple-element.84), channel_id=1, source_target_pairs={{0,96},{32,0},{64,32},{96,64},{1,97},{33,1},{65,33},{97,65},{2,98}... | collective-permute-start | bytes 1585160 | tf_op jit(solution)/shard_map/ppermute | solution.py:271
  160.2 8.9 %collective-permute-start.12 = (f32[264,128]{1,0:T(8,128)S(1)}, f32[264,128]{1,0:T(8,128)S(1)}, u32[]{:S(2)}, u32[]{:S(2)}) collective-permute-start(f32[264,128]{1,0:T(8,128)S(1)} %get-tuple-element.72), channel_id=1, source_target_pairs={{0,32},{32,64},{64,96},{96,0},{1,33},{33,65},{65,97},{97,1},{2,34}... | collective-permute-start | bytes 405512 | tf_op jit(solution)/shard_map/ppermute | solution.py:271
  160.4 10.2 %collective-permute-start.13 = (f32[264,128]{1,0:T(8,128)S(1)}, f32[264,128]{1,0:T(8,128)S(1)}, u32[]{:S(2)}, u32[]{:S(2)}) collective-permute-start(f32[264,128]{1,0:T(8,128)S(1)} %get-tuple-element.73), channel_id=1, source_target_pairs={{0,64},{32,96},{64,0},{96,32},{1,65},{33,97},{65,1},{97,33},{2,66}... | collective-permute-start | bytes 405512 | tf_op jit(solution)/shard_map/ppermute | solution.py:271
  163.0 7.6 %collective-permute-start.14 = (f32[264,128]{1,0:T(8,128)S(1)}, f32[264,128]{1,0:T(8,128)S(1)}, u32[]{:S(2)}, u32[]{:S(2)}) collective-permute-start(f32[264,128]{1,0:T(8,128)S(1)} %get-tuple-element.74), channel_id=1, source_target_pairs={{0,96},{32,0},{64,32},{96,64},{1,97},{33,1},{65,33},{97,65},{2,98}... | collective-permute-start | bytes 405512 | tf_op jit(solution)/shard_map/ppermute | solution.py:271
  164.6 6.0 %collective-permute-start.20 = (f32[264,128]{1,0:T(8,128)S(1)}, f32[264,128]{1,0:T(8,128)S(1)}, u32[]{:S(2)}, u32[]{:S(2)}) collective-permute-start(f32[264,128]{1,0:T(8,128)S(1)} %get-tuple-element.86), channel_id=1, source_target_pairs={{0,8},{8,16},{16,24},{24,0},{1,9},{9,17},{17,25},{25,1},{2,10},{10... | collective-permute-start | bytes 405512 | tf_op jit(solution)/shard_map/ppermute | solution.py:271
  166.5 6.6 %collective-permute-start.21 = (f32[264,128]{1,0:T(8,128)S(1)}, f32[264,128]{1,0:T(8,128)S(1)}, u32[]{:S(2)}, u32[]{:S(2)}) collective-permute-start(f32[264,128]{1,0:T(8,128)S(1)} %get-tuple-element.87), channel_id=1, source_target_pairs={{0,16},{8,24},{16,0},{24,8},{1,17},{9,25},{17,1},{25,9},{2,18},{10... | collective-permute-start | bytes 405512 | tf_op jit(solution)/shard_map/ppermute | solution.py:271
  169.1 5.4 %collective-permute-start.22 = (f32[264,128]{1,0:T(8,128)S(1)}, f32[264,128]{1,0:T(8,128)S(1)}, u32[]{:S(2)}, u32[]{:S(2)}) collective-permute-start(f32[264,128]{1,0:T(8,128)S(1)} %get-tuple-element.88), channel_id=1, source_target_pairs={{0,24},{8,0},{16,8},{24,16},{1,25},{9,1},{17,9},{25,17},{2,26},{10... | collective-permute-start | bytes 405512 | tf_op jit(solution)/shard_map/ppermute | solution.py:271
  175.3 21.1 %all-to-all-start.3 = ((f32[8,80,128]{2,1,0:T(8,128)}), f32[8,80,128]{2,1,0:T(8,128)S(1)}, u32[]{:S(2)}, u32[]{:S(2)}) async-start(f32[8,80,128]{2,1,0:T(8,128)} %shard_map.81), calls=%async_computation.3 | async-start | bytes 655360 | tf_op jit(solution)/shard_map/all_to_all | solution.py:50
  (5 other events, 47.2 us)

commit v7 on v6

--- a/solution.py
+++ b/solution.py
@@ -40,10 +40,6 @@
 
 def swapped(x, axis):
     return lax.ppermute(x, axis, [(0, 1), (1, 0)])
-
-
-def swapped_in_student(x):
-    return lax.ppermute(x, ("grp", "core"), [(2, 3), (3, 2)])
 
 
 def exchanged(x, axes):
@@ -349,7 +345,7 @@
             functools.partial(pair_sum_kernel, c == 0),
             arrays(full + edge, full, full, full // 2 + edge, full // 2),
             keep,
-            swapped_in_student(send),
+            swapped(send, "core"),
             place=place,
         )
         for c, (keep, send) in enumerate(parts)

time: 200 us -> 197 us (0.985)
  starting transfers between devices: 54.2 us -> 44.7 us
  waiting for transfers between devices: 72.4 us -> 79.4 us
    all_to_all x3, starting transfers between devices: 17.9 us -> 11.4 us  [exchanged(): return lax.all_to_all(x, axes, 0, 0)]
    ppermute x14, waiting for transfers between devices: 13.6 us -> 19.7 us  [moved(): return lax.ppermute(part, axis, [(i, (i + step) % 4) for i in range(4)])]
    ppermute x14, starting transfers between devices: 21 us -> 18.8 us  [moved(): return lax.ppermute(part, axis, [(i, (i + step) % 4) for i in range(4)])]
    ppermute x2 -> x4, waiting for transfers between devices: 5.43 us -> 6.43 us  [swapped(): return lax.ppermute(x, axis, [(0, 1), (1, 0)])]
  transfers between devices with their start and end apart: 26 -> 26, of which waited for: 16 -> 17; matrix products, arithmetic and copies ran while one was open for 1% -> 1% of each run, Pallas kernels for 8% -> 8%
where the time goes in v7:
time: 197 us; the launch traced here: 195 us
  waiting for transfers between devices  79.4 us (40%)
  starting transfers between devices  44.7 us (23%)
  blocking collectives  34.2 us (17%)
  Pallas kernels  29.7 us (15%)
  other arithmetic  4.24 us (2%)
  local copies, waits for them, and re-layouts  2.01 us (1%)
    all_to_all x3, waiting for transfers between devices, exchanged(): return lax.all_to_all(x, axes, 0, 0)  48.1 us
    all_to_all x1, blocking collectives, exchanged(): return lax.all_to_all(x, axes, 0, 0)  34.2 us
    pallas_call x15, Pallas kernels, vmem_call(): pl.pallas_call(kernel, out_shape=out_shape, in_specs=[in_smem()] * len(sc...  29.7 us
    ppermute x14, waiting for transfers between devices, moved(): return lax.ppermute(part, axis, [(i, (i + step) % 4) for i in range(4)])  19.7 us
    ppermute x14, starting transfers between devices, moved(): return lax.ppermute(part, axis, [(i, (i + step) % 4) for i in range(4)])  18.8 us
    all_to_all x3, starting transfers between devices, exchanged(): return lax.all_to_all(x, axes, 0, 0)  11.4 us
    ppermute x2, starting transfers between devices, shards(): sent.append(lax.ppermute(own_z[c], 'grp', [(0, 1)]))  8.32 us
    ppermute x4, waiting for transfers between devices, swapped(): return lax.ppermute(x, axis, [(0, 1), (1, 0)])  6.43 us
  transfers between devices with their start and end apart: 26, of which 17 were waited for; matrix products, arithmetic and copies ran while one was open for 1% of the time, Pallas kernels for 8%

profile of v7, /device:TPU:2, one launch (start us, length us, event | category | flops | bytes accessed | tf_op | source)
XLA Modules:
  0.0 195.1 jit_solution(8517227963983014154)
XLA Ops:
  0.6 4.7 %collective-permute-start.2 = (bf16[128,128]{1,0:T(8,128)(2,1)}, bf16[128,128]{1,0:T(8,128)(2,1)S(1)}, u32[]{:S(2)}, u32[]{:S(2)}) collective-permute-start(bf16[128,128]{1,0:T(8,128)(2,1)} %bitcast.34), channel_id=1, source_target_pairs={{0,3},{1,0},{2,1},{3,2},{4,7},{5,4},{6,5},{7,6},{8,11},{9,8},{10,9... | collective-permute-start | bytes 98312 | tf_op jit(solution)/shard_map/ppermute | solution.py:283
  7.2 3.1 %collective-permute-done.1.p2 = bf16[128,128]{1,0:T(8,128)(2,1)S(1)} collective-permute-done((bf16[128,128]{1,0:T(8,128)(2,1)}, bf16[128,128]{1,0:T(8,128)(2,1)S(1)}, u32[]{:S(2)}, u32[]{:S(2)}) %collective-permute-start.1) | collective-permute-done | bytes 32800 | tf_op jit(solution)/shard_map/ppermute | solution.py:283
  12.9 34.2 %all_to_all.20.own = bf16[16,512,128]{2,1,0:T(8,128)(2,1)S(1)} all-to-all(bf16[16,512,128]{2,1,0:T(8,128)(2,1)S(1)} %shard_map.67), channel_id=1, replica_groups=mesh['grp'=2,'y'=4,'x'=4,'core'=2,'tok'=4] {'y','x'}, dimensions={0} | all-to-all | bytes 4194304 | tf_op jit(solution)/shard_map/all_to_all | solution.py:46
  47.1 4.3 %collective-permute-done.3.sibling = bf16[16,512,128]{2,1,0:T(8,128)(2,1)} collective-permute-done((bf16[16,512,128]{2,1,0:T(8,128)(2,1)S(1)}, bf16[16,512,128]{2,1,0:T(8,128)(2,1)}, u32[]{:S(2)}, u32[]{:S(2)}) %collective-permute-start.3) | collective-permute-done | bytes 2097184 | tf_op jit(solution)/shard_map/ppermute | solution.py:42
  51.3 6.7 %shard_map.68 = bf16[1187,256]{1,0:T(8,128)(2,1)S(1)} custom-call(s32[4]{0:T(128)S(1)} %pad_add_fusion.place_ref, bf16[1187,4096]{1,0:T(8,128)(2,1)} %bitcast.38, bf16[16,512,128]{2,1,0:T(8,128)(2,1)S(1)} %all_to_all.20.own, bf16[16,512,128]{2,1,0:T(8,128)(2,1)} %collective-permute-done.3.sibling), custom_call_target="tpu_custom_call" | custom-call | tf_op jit(solution)/shard_map/pallas_call | solution.py:29
  58.0 7.0 %collective-permute-start.5 = (bf16[1187,256]{1,0:T(8,128)(2,1)S(1)}, bf16[1187,256]{1,0:T(8,128)(2,1)}, u32[]{:S(2)}, u32[]{:S(2)}) collective-permute-start(bf16[1187,256]{1,0:T(8,128)(2,1)S(1)} %shard_map.68), channel_id=1, source_target_pairs={{0,128},{1,129},{2,130},{3,131},{4,132},{5,133},{6,134},{7,135},{8... | collective-permute-start | bytes 1823240 | tf_op jit(solution)/shard_map/ppermute | solution.py:298
  65.0 6.6 %shard_map.69 = bf16[1187,256]{1,0:T(8,128)(2,1)S(1)} custom-call(s32[4]{0:T(128)S(1)} %pad_add_fusion.place_ref, bf16[1187,4096]{1,0:T(8,128)(2,1)} %bitcast.39, bf16[16,512,128]{2,1,0:T(8,128)(2,1)S(1)} %all_to_all.20.own, bf16[16,512,128]{2,1,0:T(8,128)(2,1)} %collective-permute-done.3.sibling), custom_call_target="tpu_custom_call" | custom-call | tf_op jit(solution)/shard_map/pallas_call | solution.py:29
  76.0 4.4 %all-to-all-start.1 = ((f32[16,3,512]{2,1,0:T(4,128)}), f32[16,3,512]{2,1,0:T(4,128)S(1)}, u32[]{:S(2)}, u32[]{:S(2)}) async-start(f32[16,3,512]{2,1,0:T(4,128)} %shard_map.70), calls=%async_computation.1 | async-start | bytes 262144 | tf_op jit(solution)/shard_map/all_to_all | solution.py:46
  80.5 6.7 %all-to-all-done.1.parts = f32[16,3,512]{2,1,0:T(4,128)S(1)} async-done(((f32[16,3,512]{2,1,0:T(4,128)}), f32[16,3,512]{2,1,0:T(4,128)S(1)}, u32[]{:S(2)}, u32[]{:S(2)}) %all-to-all-start.1) | async-done | bytes 98336 | tf_op jit(solution)/shard_map/all_to_all | solution.py:46
  87.8 3.5 %all-to-all-start.2 = ((f32[8,3,512]{2,1,0:T(4,128)}), f32[8,3,512]{2,1,0:T(4,128)S(1)}, u32[]{:S(2)}, u32[]{:S(2)}) async-start(f32[8,3,512]{2,1,0:T(4,128)} %shard_map.71), calls=%async_computation.2 | async-start | bytes 131072 | tf_op jit(solution)/shard_map/all_to_all | solution.py:46
  91.4 30.9 %all-to-all-done.2.parts = f32[8,3,512]{2,1,0:T(4,128)S(1)} async-done(((f32[8,3,512]{2,1,0:T(4,128)}), f32[8,3,512]{2,1,0:T(4,128)S(1)}, u32[]{:S(2)}, u32[]{:S(2)}) %all-to-all-start.2) | async-done | bytes 49184 | tf_op jit(solution)/shard_map/all_to_all | solution.py:46
  122.4 1.8 fusion.17
  124.2 5.7 %shard_map.73 = (f32[16,264,128]{2,1,0:T(8,128)S(1)}, f32[16,264,128]{2,1,0:T(8,128)S(1)}) custom-call(s32[4]{0:T(128)S(1)} %pad_add_fusion.place_ref, bf16[1187,4096]{1,0:T(8,128)(2,1)} %bitcast.40, bf16[1187,256]{1,0:T(8,128)(2,1)S(1)} %get-tuple-element.96.grads, f32[8,128]{1,0:T(8,128)S(1)} %scatter.6.extra), custom_call_target="tpu_custom_call" | custom-call | tf_op jit(solution)/shard_map/pallas_call | solution.py:29
  130.7 5.7 %shard_map.77 = (f32[16,264,128]{2,1,0:T(8,128)S(1)}, f32[16,264,128]{2,1,0:T(8,128)S(1)}) custom-call(s32[4]{0:T(128)S(1)} %pad_add_fusion.place_ref, bf16[1187,4096]{1,0:T(8,128)(2,1)} %bitcast.41, bf16[1187,256]{1,0:T(8,128)(2,1)S(1)} %get-tuple-element.94.grads, f32[8,128]{1,0:T(8,128)S(1)} %scatter.9.extra), custom_call_target="tpu_custom_call" | custom-call | tf_op jit(solution)/shard_map/pallas_call | solution.py:29
  141.7 3.2 %collective-permute-start.17 = (f32[512,128]{1,0:T(8,128)S(1)}, f32[512,128]{1,0:T(8,128)S(1)}, u32[]{:S(2)}, u32[]{:S(2)}) collective-permute-start(f32[512,128]{1,0:T(8,128)S(1)} %get-tuple-element.82), channel_id=1, source_target_pairs={{0,96},{32,0},{64,32},{96,64},{1,97},{33,1},{65,33},{97,65},{2,98}... | collective-permute-start | bytes 786440 | tf_op jit(solution)/shard_map/ppermute | solution.py:267
  146.3 1.9 collective-permute-start.10
  151.8 3.2 %collective-permute-start.19 = (f32[1032,128]{1,0:T(8,128)S(1)}, f32[1032,128]{1,0:T(8,128)S(1)}, u32[]{:S(2)}, u32[]{:S(2)}) collective-permute-start(f32[1032,128]{1,0:T(8,128)S(1)} %get-tuple-element.84), channel_id=1, source_target_pairs={{0,96},{32,0},{64,32},{96,64},{1,97},{33,1},{65,33},{97,65},{2,98}... | collective-permute-start | bytes 1585160 | tf_op jit(solution)/shard_map/ppermute | solution.py:267
  155.0 7.0 %collective-permute-done.11.from_right = f32[1032,128]{1,0:T(8,128)S(1)} collective-permute-done((f32[1032,128]{1,0:T(8,128)S(1)}, f32[1032,128]{1,0:T(8,128)S(1)}, u32[]{:S(2)}, u32[]{:S(2)}) %collective-permute-start.11) | collective-permute-done | bytes 528416 | tf_op jit(solution)/shard_map/ppermute | solution.py:267
  162.2 2.3 %collective-permute-start.13 = (f32[264,128]{1,0:T(8,128)S(1)}, f32[264,128]{1,0:T(8,128)S(1)}, u32[]{:S(2)}, u32[]{:S(2)}) collective-permute-start(f32[264,128]{1,0:T(8,128)S(1)} %get-tuple-element.73), channel_id=1, source_target_pairs={{0,64},{32,96},{64,0},{96,32},{1,65},{33,97},{65,1},{97,33},{2,66}... | collective-permute-start | bytes 405512 | tf_op jit(solution)/shard_map/ppermute | solution.py:267
  165.9 4.1 %collective-permute-done.19.from_right = f32[1032,128]{1,0:T(8,128)S(1)} collective-permute-done((f32[1032,128]{1,0:T(8,128)S(1)}, f32[1032,128]{1,0:T(8,128)S(1)}, u32[]{:S(2)}, u32[]{:S(2)}) %collective-permute-start.19) | collective-permute-done | bytes 528416 | tf_op jit(solution)/shard_map/ppermute | solution.py:267
  170.3 3.3 %collective-permute-start.21 = (f32[264,128]{1,0:T(8,128)S(1)}, f32[264,128]{1,0:T(8,128)S(1)}, u32[]{:S(2)}, u32[]{:S(2)}) collective-permute-start(f32[264,128]{1,0:T(8,128)S(1)} %get-tuple-element.87), channel_id=1, source_target_pairs={{0,16},{8,24},{16,0},{24,8},{1,17},{9,25},{17,1},{25,9},{2,18},{10... | collective-permute-start | bytes 405512 | tf_op jit(solution)/shard_map/ppermute | solution.py:267
  176.9 1.7 collective-permute-done.22.b3
  179.4 3.4 %all-to-all-start.3 = ((f32[8,80,128]{2,1,0:T(8,128)}), f32[8,80,128]{2,1,0:T(8,128)S(1)}, u32[]{:S(2)}, u32[]{:S(2)}) async-start(f32[8,80,128]{2,1,0:T(8,128)} %shard_map.81), calls=%async_computation.3 | async-start | bytes 655360 | tf_op jit(solution)/shard_map/all_to_all | solution.py:46
  183.4 10.5 %all-to-all-done.3 = f32[8,80,128]{2,1,0:T(8,128)S(1)} async-done(((f32[8,80,128]{2,1,0:T(8,128)}), f32[8,80,128]{2,1,0:T(8,128)S(1)}, u32[]{:S(2)}, u32[]{:S(2)}) %all-to-all-start.3) | async-done | bytes 327712 | tf_op jit(solution)/shard_map/all_to_all | solution.py:46
  (72 shorter events, 28.2 us)
Async XLA Ops:
  0.6 6.6 %collective-permute-start.2 = (bf16[128,128]{1,0:T(8,128)(2,1)}, bf16[128,128]{1,0:T(8,128)(2,1)S(1)}, u32[]{:S(2)}, u32[]{:S(2)}) collective-permute-start(bf16[128,128]{1,0:T(8,128)(2,1)} %bitcast.34), channel_id=1, source_target_pairs={{0,3},{1,0},{2,1},{3,2},{4,7},{5,4},{6,5},{7,6},{8,11},{9,8},{10,9... | collective-permute-start | bytes 98312 | tf_op jit(solution)/shard_map/ppermute | solution.py:283
  5.3 5.0 %collective-permute-start.1 = (bf16[128,128]{1,0:T(8,128)(2,1)}, bf16[128,128]{1,0:T(8,128)(2,1)S(1)}, u32[]{:S(2)}, u32[]{:S(2)}) collective-permute-start(bf16[128,128]{1,0:T(8,128)(2,1)} %bitcast.35), channel_id=1, source_target_pairs={{0,2},{1,3},{2,0},{3,1},{4,6},{5,7},{6,4},{7,5},{8,10},{9,11},{10,... | collective-permute-start | bytes 98312 | tf_op jit(solution)/shard_map/ppermute | solution.py:283
  5.3 5.9 %collective-permute-start = (bf16[128,128]{1,0:T(8,128)(2,1)}, bf16[128,128]{1,0:T(8,128)(2,1)S(1)}, u32[]{:S(2)}, u32[]{:S(2)}) collective-permute-start(bf16[128,128]{1,0:T(8,128)(2,1)} %bitcast.36), channel_id=1, source_target_pairs={{0,1},{1,2},{2,3},{3,0},{4,5},{5,6},{6,7},{7,4},{8,9},{9,10},{10,1... | collective-permute-start | bytes 98312 | tf_op jit(solution)/shard_map/ppermute | solution.py:283
  58.0 64.3 %collective-permute-start.5 = (bf16[1187,256]{1,0:T(8,128)(2,1)S(1)}, bf16[1187,256]{1,0:T(8,128)(2,1)}, u32[]{:S(2)}, u32[]{:S(2)}) collective-permute-start(bf16[1187,256]{1,0:T(8,128)(2,1)S(1)} %shard_map.68), channel_id=1, source_target_pairs={{0,128},{1,129},{2,130},{3,131},{4,132},{5,133},{6,134},{7,135},{8... | collective-permute-start | bytes 1823240 | tf_op jit(solution)/shard_map/ppermute | solution.py:298
  71.7 50.7 %collective-permute-start.6 = (bf16[1187,256]{1,0:T(8,128)(2,1)S(1)}, bf16[1187,256]{1,0:T(8,128)(2,1)S(1)}, u32[]{:S(2)}, u32[]{:S(2)}) collective-permute-start(bf16[1187,256]{1,0:T(8,128)(2,1)S(1)} %shard_map.69), channel_id=1, source_target_pairs={{0,128},{1,129},{2,130},{3,131},{4,132},{5,133},{6,134},{7,135},{8... | collective-permute-start | bytes 1823240 | tf_op jit(solution)/shard_map/ppermute | solution.py:298
  76.0 11.2 %all-to-all-start.1 = ((f32[16,3,512]{2,1,0:T(4,128)}), f32[16,3,512]{2,1,0:T(4,128)S(1)}, u32[]{:S(2)}, u32[]{:S(2)}) async-start(f32[16,3,512]{2,1,0:T(4,128)} %shard_map.70), calls=%async_computation.1 | async-start | bytes 262144 | tf_op jit(solution)/shard_map/all_to_all | solution.py:46
  87.8 34.5 %all-to-all-start.2 = ((f32[8,3,512]{2,1,0:T(4,128)}), f32[8,3,512]{2,1,0:T(4,128)S(1)}, u32[]{:S(2)}, u32[]{:S(2)}) async-start(f32[8,3,512]{2,1,0:T(4,128)} %shard_map.71), calls=%async_computation.2 | async-start | bytes 131072 | tf_op jit(solution)/shard_map/all_to_all | solution.py:46
  129.9 7.1 %collective-permute-start.7 = (f32[16,264,128]{2,1,0:T(8,128)S(1)}, f32[16,264,128]{2,1,0:T(8,128)S(1)}, u32[]{:S(2)}, u32[]{:S(2)}) collective-permute-start(f32[16,264,128]{2,1,0:T(8,128)S(1)} %get-tuple-element.63), channel_id=1, source_target_pairs={{0,4},{4,0},{1,5},{5,1},{2,6},{6,2},{3,7},{7,3},{8,12},{12,8},{9,1... | collective-permute-start | bytes 6488072 | tf_op jit(solution)/shard_map/ppermute | solution.py:42
  136.3 4.5 %collective-permute-start.15 = (f32[16,264,128]{2,1,0:T(8,128)S(1)}, f32[16,264,128]{2,1,0:T(8,128)S(1)}, u32[]{:S(2)}, u32[]{:S(2)}) collective-permute-start(f32[16,264,128]{2,1,0:T(8,128)S(1)} %get-tuple-element.77), channel_id=1, source_target_pairs={{0,4},{4,0},{1,5},{5,1},{2,6},{6,2},{3,7},{7,3},{8,12},{12,8},{9,1... | collective-permute-start | bytes 6488072 | tf_op jit(solution)/shard_map/ppermute | solution.py:42
  137.7 8.5 %collective-permute-start.8 = (f32[520,128]{1,0:T(8,128)S(1)}, f32[520,128]{1,0:T(8,128)S(1)}, u32[]{:S(2)}, u32[]{:S(2)}) collective-permute-start(f32[520,128]{1,0:T(8,128)S(1)} %get-tuple-element.67), channel_id=1, source_target_pairs={{0,8},{8,16},{16,24},{24,0},{1,9},{9,17},{17,25},{25,1},{2,10},{10... | collective-permute-start | bytes 798728 | tf_op jit(solution)/shard_map/ppermute | solution.py:267
  138.3 8.0 %collective-permute-start.9 = (f32[512,128]{1,0:T(8,128)S(1)}, f32[512,128]{1,0:T(8,128)S(1)}, u32[]{:S(2)}, u32[]{:S(2)}) collective-permute-start(f32[512,128]{1,0:T(8,128)S(1)} %get-tuple-element.68), channel_id=1, source_target_pairs={{0,24},{8,0},{16,8},{24,16},{1,25},{9,1},{17,9},{25,17},{2,26},{10... | collective-permute-start | bytes 786440 | tf_op jit(solution)/shard_map/ppermute | solution.py:267
  141.6 10.0 %collective-permute-start.16 = (f32[520,128]{1,0:T(8,128)S(1)}, f32[520,128]{1,0:T(8,128)S(1)}, u32[]{:S(2)}, u32[]{:S(2)}) collective-permute-start(f32[520,128]{1,0:T(8,128)S(1)} %get-tuple-element.81), channel_id=1, source_target_pairs={{0,32},{32,64},{64,96},{96,0},{1,33},{33,65},{65,97},{97,1},{2,34}... | collective-permute-start | bytes 798728 | tf_op jit(solution)/shard_map/ppermute | solution.py:267
  141.7 9.0 %collective-permute-start.17 = (f32[512,128]{1,0:T(8,128)S(1)}, f32[512,128]{1,0:T(8,128)S(1)}, u32[]{:S(2)}, u32[]{:S(2)}) collective-permute-start(f32[512,128]{1,0:T(8,128)S(1)} %get-tuple-element.82), channel_id=1, source_target_pairs={{0,96},{32,0},{64,32},{96,64},{1,97},{33,1},{65,33},{97,65},{2,98}... | collective-permute-start | bytes 786440 | tf_op jit(solution)/shard_map/ppermute | solution.py:267
  146.3 15.6 %collective-permute-start.10 = (f32[1040,128]{1,0:T(8,128)S(1)}, f32[1040,128]{1,0:T(8,128)S(1)}, u32[]{:S(2)}, u32[]{:S(2)}) collective-permute-start(f32[1040,128]{1,0:T(8,128)S(1)} %get-tuple-element.69), channel_id=1, source_target_pairs={{0,8},{8,16},{16,24},{24,0},{1,9},{9,17},{17,25},{25,1},{2,10},{10... | collective-permute-start | bytes 1597448 | tf_op jit(solution)/shard_map/ppermute | solution.py:267
  148.3 13.7 %collective-permute-start.11 = (f32[1032,128]{1,0:T(8,128)S(1)}, f32[1032,128]{1,0:T(8,128)S(1)}, u32[]{:S(2)}, u32[]{:S(2)}) collective-permute-start(f32[1032,128]{1,0:T(8,128)S(1)} %get-tuple-element.70), channel_id=1, source_target_pairs={{0,24},{8,0},{16,8},{24,16},{1,25},{9,1},{17,9},{25,17},{2,26},{10... | collective-permute-start | bytes 1585160 | tf_op jit(solution)/shard_map/ppermute | solution.py:267
  151.7 18.4 %collective-permute-start.18 = (f32[1040,128]{1,0:T(8,128)S(1)}, f32[1040,128]{1,0:T(8,128)S(1)}, u32[]{:S(2)}, u32[]{:S(2)}) collective-permute-start(f32[1040,128]{1,0:T(8,128)S(1)} %get-tuple-element.83), channel_id=1, source_target_pairs={{0,32},{32,64},{64,96},{96,0},{1,33},{33,65},{65,97},{97,1},{2,34}... | collective-permute-start | bytes 1597448 | tf_op jit(solution)/shard_map/ppermute | solution.py:267
  151.8 18.3 %collective-permute-start.19 = (f32[1032,128]{1,0:T(8,128)S(1)}, f32[1032,128]{1,0:T(8,128)S(1)}, u32[]{:S(2)}, u32[]{:S(2)}) collective-permute-start(f32[1032,128]{1,0:T(8,128)S(1)} %get-tuple-element.84), channel_id=1, source_target_pairs={{0,96},{32,0},{64,32},{96,64},{1,97},{33,1},{65,33},{97,65},{2,98}... | collective-permute-start | bytes 1585160 | tf_op jit(solution)/shard_map/ppermute | solution.py:267
  162.1 11.5 %collective-permute-start.12 = (f32[264,128]{1,0:T(8,128)S(1)}, f32[264,128]{1,0:T(8,128)S(1)}, u32[]{:S(2)}, u32[]{:S(2)}) collective-permute-start(f32[264,128]{1,0:T(8,128)S(1)} %get-tuple-element.72), channel_id=1, source_target_pairs={{0,32},{32,64},{64,96},{96,0},{1,33},{33,65},{65,97},{97,1},{2,34}... | collective-permute-start | bytes 405512 | tf_op jit(solution)/shard_map/ppermute | solution.py:267
  162.2 11.4 %collective-permute-start.13 = (f32[264,128]{1,0:T(8,128)S(1)}, f32[264,128]{1,0:T(8,128)S(1)}, u32[]{:S(2)}, u32[]{:S(2)}) collective-permute-start(f32[264,128]{1,0:T(8,128)S(1)} %get-tuple-element.73), channel_id=1, source_target_pairs={{0,64},{32,96},{64,0},{96,32},{1,65},{33,97},{65,1},{97,33},{2,66}... | collective-permute-start | bytes 405512 | tf_op jit(solution)/shard_map/ppermute | solution.py:267
  164.5 9.1 %collective-permute-start.14 = (f32[264,128]{1,0:T(8,128)S(1)}, f32[264,128]{1,0:T(8,128)S(1)}, u32[]{:S(2)}, u32[]{:S(2)}) collective-permute-start(f32[264,128]{1,0:T(8,128)S(1)} %get-tuple-element.74), channel_id=1, source_target_pairs={{0,96},{32,0},{64,32},{96,64},{1,97},{33,1},{65,33},{97,65},{2,98}... | collective-permute-start | bytes 405512 | tf_op jit(solution)/shard_map/ppermute | solution.py:267
  170.2 5.1 %collective-permute-start.20 = (f32[264,128]{1,0:T(8,128)S(1)}, f32[264,128]{1,0:T(8,128)S(1)}, u32[]{:S(2)}, u32[]{:S(2)}) collective-permute-start(f32[264,128]{1,0:T(8,128)S(1)} %get-tuple-element.86), channel_id=1, source_target_pairs={{0,8},{8,16},{16,24},{24,0},{1,9},{9,17},{17,25},{25,1},{2,10},{10... | collective-permute-start | bytes 405512 | tf_op jit(solution)/shard_map/ppermute | solution.py:267
  170.3 6.6 %collective-permute-start.21 = (f32[264,128]{1,0:T(8,128)S(1)}, f32[264,128]{1,0:T(8,128)S(1)}, u32[]{:S(2)}, u32[]{:S(2)}) collective-permute-start(f32[264,128]{1,0:T(8,128)S(1)} %get-tuple-element.87), channel_id=1, source_target_pairs={{0,16},{8,24},{16,0},{24,8},{1,17},{9,25},{17,1},{25,9},{2,18},{10... | collective-permute-start | bytes 405512 | tf_op jit(solution)/shard_map/ppermute | solution.py:267
  173.6 5.0 %collective-permute-start.22 = (f32[264,128]{1,0:T(8,128)S(1)}, f32[264,128]{1,0:T(8,128)S(1)}, u32[]{:S(2)}, u32[]{:S(2)}) collective-permute-start(f32[264,128]{1,0:T(8,128)S(1)} %get-tuple-element.88), channel_id=1, source_target_pairs={{0,24},{8,0},{16,8},{24,16},{1,25},{9,1},{17,9},{25,17},{2,26},{10... | collective-permute-start | bytes 405512 | tf_op jit(solution)/shard_map/ppermute | solution.py:267
  179.4 14.5 %all-to-all-start.3 = ((f32[8,80,128]{2,1,0:T(8,128)}), f32[8,80,128]{2,1,0:T(8,128)S(1)}, u32[]{:S(2)}, u32[]{:S(2)}) async-start(f32[8,80,128]{2,1,0:T(8,128)} %shard_map.81), calls=%async_computation.3 | async-start | bytes 655360 | tf_op jit(solution)/shard_map/all_to_all | solution.py:46
  (5 other events, 47.8 us)

commit v8 on v7

--- a/solution.py
+++ b/solution.py
@@ -163,12 +163,16 @@
     out[2:3] = label
 
 
-def grads_kernel(place_ref, weights, grads, extra, keep, send, turned, held, sems):
+def grads_kernel(
+    place_ref, weights, lower, upper, low_extra, high_extra, *refs
+):
+    keeps, sends, (turned, held, sems) = refs[:2], refs[2:4], refs[4:]
     core = place_ref[0]
-    tokens = grads.shape[1]
-    chips, _, wide = keep.shape
+    tokens = lower.shape[1]
+    chips, _, wide = keeps[0].shape
     copies = strips_of(weights, held, sems)
-    turned[...] = grads[...].T
+    turned[:tokens] = lower[...].T
+    turned[tokens:] = upper[...].T
     per_strip = chips // STRIPS
     for chip in range(chips):
         strip, at = chip // per_strip, (chip % per_strip) * 2 * wide
@@ -177,33 +181,36 @@
         full = jnp.dot(
             turned[...], held[strip, :, at : at + 2 * wide], preferred_element_type=F32
         )
-        low = full[:, :wide]
-        high = full[:, wide:]
-        keep[chip, :tokens] = jnp.where(core == 0, low, high)
-        send[chip, :tokens] = jnp.where(core == 0, high, low)
-        keep[chip, tokens:] = extra[...]
-        send[chip, tokens:] = extra[...]
-
-
-def split_grads(place, weights, grads, extra):
-    words, tokens = grads.shape
+        mine = jnp.where(core == 0, full[:, :wide], full[:, wide:])
+        theirs = jnp.where(core == 0, full[:, wide:], full[:, :wide])
+        for half, extra in enumerate((low_extra, high_extra)):
+            rows = slice(half * tokens, (half + 1) * tokens)
+            keeps[half][chip, :tokens] = mine[rows]
+            sends[half][chip, :tokens] = theirs[rows]
+            keeps[half][chip, tokens:] = extra[...]
+            sends[half][chip, tokens:] = extra[...]
+
+
+def split_grads(place, weights, grads, extras):
+    words, tokens = grads[0].shape
     feats = weights.shape[1]
-    wide = extra.shape[1]
+    wide = extras[0].shape[1]
     part = jax.ShapeDtypeStruct((feats // (2 * wide), tokens + EXTRA, wide), F32)
-    return vmem_call(
+    out = vmem_call(
         grads_kernel,
-        [part] * 2,
-        grads,
-        extra,
+        [part] * 4,
+        *grads,
+        *extras,
         place=place,
         weights=weights,
         scratch=[
-            pltpu.VMEM((tokens, words), BF16),
+            pltpu.VMEM((2 * tokens, words), BF16),
             pltpu.VMEM((STRIPS, words, feats // STRIPS), BF16),
             pltpu.SemaphoreType.DMA((STRIPS,)),
         ],
-        mib=22,
-    )
+        mib=28,
+    )
+    return [(out[0], out[2]), (out[1], out[3])]
 
 
 def line_total(parts):
@@ -261,6 +268,14 @@
         out[plane, :part] = line_total([p[at] for p in halves[plane // 4]])
         out[plane, part : part + EXTRA] = tails[0]
         out[plane, part + EXTRA :] = tails[1]
+
+
+def finish_kernel(parts, rows_out, diverged):
+    mine = total([parts[i] for i in range(4, 8)])
+    part = rows_out.shape[0]
+    rows_out[...] = mine[:part].astype(BF16)
+    diverged[:2] = mine[part : part + 2]
+    diverged[2:] = mine[part + EXTRA : part + EXTRA + 2]
 
 
 def moved(part, axis, step):
@@ -336,7 +351,8 @@
             (2.0 * student_prob - teacher_prob - hits[c].astype(F32)) * mask[span]
         ).astype(BF16)
         extra = jnp.zeros((EXTRA, wide), F32).at[:2].set(diverge.reshape(2, wide))
-        parts.append(split_grads(place, weights, grads, extra))
+        parts.append((grads, extra))
+    parts = split_grads(place, weights, *zip(*parts))
     orders = (("x", "y"), ("y", "x"))
     arrays = lambda *heights: [array((height, wide), F32) for height in heights]
     full, edge = 4 * half, EXTRA
@@ -388,9 +404,11 @@
         *pieces[0],
         *pieces[1],
     )
-    mine = total(list(exchanged(last, PLANES))[4:])
-    input_grads = mine[:part].astype(BF16)
-    diverged = jnp.concatenate([mine[part : part + 2], mine[part + EXTRA : part + EXTRA + 2]])
+    input_grads, diverged = vmem_call(
+        finish_kernel,
+        [array((part, wide), BF16), array((4 * rows // wide, wide), F32)],
+        exchanged(last, PLANES),
+    )
     token_loss = mask * (diverged.reshape(-1) + student_norm - label_logit)
     return (input_grads, token_loss, jnp.stack([teacher_norm, student_norm]))
 

time: 197 us -> 196 us (level)
  Pallas kernels: 29.7 us -> 27.6 us
    ppermute x14, waiting for transfers between devices: 19.7 us -> 16.6 us  [moved(): return lax.ppermute(part, axis, [(i, (i + step) % 4) for i in range(4)])]
    ppermute x4, waiting for transfers between devices: 6.43 us -> 9.39 us  [swapped(): return lax.ppermute(x, axis, [(0, 1), (1, 0)])]
    pallas_call x15, Pallas kernels: 29.7 us -> 27.6 us  [vmem_call(): pl.pallas_call(kernel, out_shape=out_shape, in_specs=[in_smem()] * len(sc...]
  transfers between devices with their start and end apart: 26 -> 26, of which waited for: 17 -> 19; matrix products, arithmetic and copies ran while one was open for 1% -> 1% of each run, Pallas kernels for 8% -> 5%
where the time goes in v8:
time: 196 us; the launch traced here: 194 us
  waiting for transfers between devices  79.3 us (40%)
  starting transfers between devices  46 us (23%)
  blocking collectives  34.2 us (17%)
  Pallas kernels  27.6 us (14%)
  other arithmetic  4.58 us (2%)
    all_to_all x3, waiting for transfers between devices, exchanged(): return lax.all_to_all(x, axes, 0, 0)  48.1 us
    all_to_all x1, blocking collectives, exchanged(): return lax.all_to_all(x, axes, 0, 0)  34.2 us
    pallas_call x15, Pallas kernels, vmem_call(): pl.pallas_call(kernel, out_shape=out_shape, in_specs=[in_smem()] * len(sc...  27.6 us
    ppermute x14, starting transfers between devices, moved(): return lax.ppermute(part, axis, [(i, (i + step) % 4) for i in range(4)])  20.3 us
    ppermute x14, waiting for transfers between devices, moved(): return lax.ppermute(part, axis, [(i, (i + step) % 4) for i in range(4)])  16.6 us
    all_to_all x3, starting transfers between devices, exchanged(): return lax.all_to_all(x, axes, 0, 0)  11.4 us
    ppermute x4, waiting for transfers between devices, swapped(): return lax.ppermute(x, axis, [(0, 1), (1, 0)])  9.39 us
    ppermute x2, starting transfers between devices, shards(): sent.append(lax.ppermute(own_z[c], 'grp', [(0, 1)]))  8.31 us
  transfers between devices with their start and end apart: 26, of which 19 were waited for; matrix products, arithmetic and copies ran while one was open for 1% of the time, Pallas kernels for 5%

profile of v8, /device:TPU:2, one launch (start us, length us, event | category | flops | bytes accessed | tf_op | source)
XLA Modules:
  0.0 194.0 jit_solution(1355525532091500489)
XLA Ops:
  0.6 4.7 %collective-permute-start.2 = (bf16[128,128]{1,0:T(8,128)(2,1)}, bf16[128,128]{1,0:T(8,128)(2,1)S(1)}, u32[]{:S(2)}, u32[]{:S(2)}) collective-permute-start(bf16[128,128]{1,0:T(8,128)(2,1)} %bitcast.26), channel_id=1, source_target_pairs={{0,3},{1,0},{2,1},{3,2},{4,7},{5,4},{6,5},{7,6},{8,11},{9,8},{10,9... | collective-permute-start | bytes 98312 | tf_op jit(solution)/shard_map/ppermute | solution.py:298
  7.2 3.1 %collective-permute-done.1.p2 = bf16[128,128]{1,0:T(8,128)(2,1)S(1)} collective-permute-done((bf16[128,128]{1,0:T(8,128)(2,1)}, bf16[128,128]{1,0:T(8,128)(2,1)S(1)}, u32[]{:S(2)}, u32[]{:S(2)}) %collective-permute-start.1) | collective-permute-done | bytes 32800 | tf_op jit(solution)/shard_map/ppermute | solution.py:298
  12.9 34.2 %all_to_all.20.own = bf16[16,512,128]{2,1,0:T(8,128)(2,1)S(1)} all-to-all(bf16[16,512,128]{2,1,0:T(8,128)(2,1)S(1)} %shard_map.67), channel_id=1, replica_groups=mesh['grp'=2,'y'=4,'x'=4,'core'=2,'tok'=4] {'y','x'}, dimensions={0} | all-to-all | bytes 4194304 | tf_op jit(solution)/shard_map/all_to_all | solution.py:46
  47.1 4.3 %collective-permute-done.3.sibling = bf16[16,512,128]{2,1,0:T(8,128)(2,1)} collective-permute-done((bf16[16,512,128]{2,1,0:T(8,128)(2,1)S(1)}, bf16[16,512,128]{2,1,0:T(8,128)(2,1)}, u32[]{:S(2)}, u32[]{:S(2)}) %collective-permute-start.3) | collective-permute-done | bytes 2097184 | tf_op jit(solution)/shard_map/ppermute | solution.py:42
  51.3 6.7 %shard_map.68 = bf16[1187,256]{1,0:T(8,128)(2,1)S(1)} custom-call(s32[4]{0:T(128)S(1)} %pad_add_fusion.place_ref, bf16[1187,4096]{1,0:T(8,128)(2,1)} %bitcast.30, bf16[16,512,128]{2,1,0:T(8,128)(2,1)S(1)} %all_to_all.20.own, bf16[16,512,128]{2,1,0:T(8,128)(2,1)} %collective-permute-done.3.sibling), custom_call_target="tpu_custom_call" | custom-call | tf_op jit(solution)/shard_map/pallas_call | solution.py:29
  58.0 7.0 %collective-permute-start.5 = (bf16[1187,256]{1,0:T(8,128)(2,1)S(1)}, bf16[1187,256]{1,0:T(8,128)(2,1)}, u32[]{:S(2)}, u32[]{:S(2)}) collective-permute-start(bf16[1187,256]{1,0:T(8,128)(2,1)S(1)} %shard_map.68), channel_id=1, source_target_pairs={{0,128},{1,129},{2,130},{3,131},{4,132},{5,133},{6,134},{7,135},{8... | collective-permute-start | bytes 1823240 | tf_op jit(solution)/shard_map/ppermute | solution.py:313
  65.0 6.6 %shard_map.69 = bf16[1187,256]{1,0:T(8,128)(2,1)S(1)} custom-call(s32[4]{0:T(128)S(1)} %pad_add_fusion.place_ref, bf16[1187,4096]{1,0:T(8,128)(2,1)} %bitcast.31, bf16[16,512,128]{2,1,0:T(8,128)(2,1)S(1)} %all_to_all.20.own, bf16[16,512,128]{2,1,0:T(8,128)(2,1)} %collective-permute-done.3.sibling), custom_call_target="tpu_custom_call" | custom-call | tf_op jit(solution)/shard_map/pallas_call | solution.py:29
  76.0 4.4 %all-to-all-start.1 = ((f32[16,3,512]{2,1,0:T(4,128)}), f32[16,3,512]{2,1,0:T(4,128)S(1)}, u32[]{:S(2)}, u32[]{:S(2)}) async-start(f32[16,3,512]{2,1,0:T(4,128)} %shard_map.70), calls=%async_computation.1 | async-start | bytes 262144 | tf_op jit(solution)/shard_map/all_to_all | solution.py:46
  80.5 6.7 %all-to-all-done.1.parts = f32[16,3,512]{2,1,0:T(4,128)S(1)} async-done(((f32[16,3,512]{2,1,0:T(4,128)}), f32[16,3,512]{2,1,0:T(4,128)S(1)}, u32[]{:S(2)}, u32[]{:S(2)}) %all-to-all-start.1) | async-done | bytes 98336 | tf_op jit(solution)/shard_map/all_to_all | solution.py:46
  87.8 3.5 %all-to-all-start.2 = ((f32[8,3,512]{2,1,0:T(4,128)}), f32[8,3,512]{2,1,0:T(4,128)S(1)}, u32[]{:S(2)}, u32[]{:S(2)}) async-start(f32[8,3,512]{2,1,0:T(4,128)} %shard_map.71), calls=%async_computation.2 | async-start | bytes 131072 | tf_op jit(solution)/shard_map/all_to_all | solution.py:46
  91.4 30.9 %all-to-all-done.2.parts = f32[8,3,512]{2,1,0:T(4,128)S(1)} async-done(((f32[8,3,512]{2,1,0:T(4,128)}), f32[8,3,512]{2,1,0:T(4,128)S(1)}, u32[]{:S(2)}, u32[]{:S(2)}) %all-to-all-start.2) | async-done | bytes 49184 | tf_op jit(solution)/shard_map/all_to_all | solution.py:46
  122.4 2.9 %fusion.10 = (f32[256]{0:T(256)S(1)}, bf16[1187,256]{1,0:T(8,128)(2,1)S(1)}, bf16[1187,256]{1,0:T(8,128)(2,1)S(1)}, f32[256]{0:T(256)S(1)}) fusion(bf16[1187,256]{1,0:T(8,128)(2,1)S(1)} %shard_map.69, bf16[1187,256]{1,0:T(8,128)(2,1)S(1)} %collective-permute-done.6, f32[256]{0:T(256)S(1)} %bitcast.44, f32[256]{0:T(256)S(1)} %bitcast.43, ...), kind=kLoop, calls=%fused_computation.18 | loop fusion | flops 8507904 | bytes 3661452 | tf_op jit(solution)/shard_map/reduce_sum | solution.py:349
  125.3 8.7 %shard_map.73 = (f32[16,264,128]{2,1,0:T(8,128)S(1)}, f32[16,264,128]{2,1,0:T(8,128)S(1)}, f32[16,264,128]{2,1,0:T(8,128)S(1)}, f32[16,264,128]{2,1,0:T(8,128)S(1)}) custom-call(s32[4]{0:T(128)S(1)} %pad_add_fusion.place_ref, bf16[1187,4096]{1,0:T(8,128)(2,1)} %bitcast.32, bf16[1187,256]{1,0:T(8,128)(2,1)S(1)} %get-tuple-element.113.lower, ...), custom_call_target="tpu_custom_call" | custom-call | tf_op jit(solution)/shard_map/pallas_call | solution.py:29
  134.6 3.7 %collective-permute-done.7.got = f32[16,264,128]{2,1,0:T(8,128)S(1)} collective-permute-done((f32[16,264,128]{2,1,0:T(8,128)S(1)}, f32[16,264,128]{2,1,0:T(8,128)S(1)}, u32[]{:S(2)}, u32[]{:S(2)}) %collective-permute-start.7) | collective-permute-done | bytes 2162720 | tf_op jit(solution)/shard_map/ppermute | solution.py:42
  142.3 3.2 %collective-permute-start.17 = (f32[512,128]{1,0:T(8,128)S(1)}, f32[512,128]{1,0:T(8,128)S(1)}, u32[]{:S(2)}, u32[]{:S(2)}) collective-permute-start(f32[512,128]{1,0:T(8,128)S(1)} %get-tuple-element.84), channel_id=1, source_target_pairs={{0,96},{32,0},{64,32},{96,64},{1,97},{33,1},{65,33},{97,65},{2,98}... | collective-permute-start | bytes 786440 | tf_op jit(solution)/shard_map/ppermute | solution.py:282
  145.5 2.2 %collective-permute-done.9.behind = f32[512,128]{1,0:T(8,128)S(1)} collective-permute-done((f32[512,128]{1,0:T(8,128)S(1)}, f32[512,128]{1,0:T(8,128)S(1)}, u32[]{:S(2)}, u32[]{:S(2)}) %collective-permute-start.9) | collective-permute-done | bytes 262176 | tf_op jit(solution)/shard_map/ppermute | solution.py:282
  147.8 1.9 collective-permute-start.10
  152.4 3.2 %collective-permute-start.19 = (f32[1032,128]{1,0:T(8,128)S(1)}, f32[1032,128]{1,0:T(8,128)S(1)}, u32[]{:S(2)}, u32[]{:S(2)}) collective-permute-start(f32[1032,128]{1,0:T(8,128)S(1)} %get-tuple-element.86), channel_id=1, source_target_pairs={{0,96},{32,0},{64,32},{96,64},{1,97},{33,1},{65,33},{97,65},{2,98}... | collective-permute-start | bytes 1585160 | tf_op jit(solution)/shard_map/ppermute | solution.py:282
  155.6 8.0 %collective-permute-done.11.from_right = f32[1032,128]{1,0:T(8,128)S(1)} collective-permute-done((f32[1032,128]{1,0:T(8,128)S(1)}, f32[1032,128]{1,0:T(8,128)S(1)}, u32[]{:S(2)}, u32[]{:S(2)}) %collective-permute-start.11) | collective-permute-done | bytes 528416 | tf_op jit(solution)/shard_map/ppermute | solution.py:282
  163.8 2.3 %collective-permute-start.13 = (f32[264,128]{1,0:T(8,128)S(1)}, f32[264,128]{1,0:T(8,128)S(1)}, u32[]{:S(2)}, u32[]{:S(2)}) collective-permute-start(f32[264,128]{1,0:T(8,128)S(1)} %get-tuple-element.76), channel_id=1, source_target_pairs={{0,64},{32,96},{64,0},{96,32},{1,65},{33,97},{65,1},{97,33},{2,66}... | collective-permute-start | bytes 405512 | tf_op jit(solution)/shard_map/ppermute | solution.py:282
  171.4 2.0 %collective-permute-start.22 = (f32[264,128]{1,0:T(8,128)S(1)}, f32[264,128]{1,0:T(8,128)S(1)}, u32[]{:S(2)}, u32[]{:S(2)}) collective-permute-start(f32[264,128]{1,0:T(8,128)S(1)} %get-tuple-element.90), channel_id=1, source_target_pairs={{0,24},{8,0},{16,8},{24,16},{1,25},{9,1},{17,9},{25,17},{2,26},{10... | collective-permute-start | bytes 405512 | tf_op jit(solution)/shard_map/ppermute | solution.py:282
  173.9 2.1 %collective-permute-done.21.b2 = f32[264,128]{1,0:T(8,128)S(1)} collective-permute-done((f32[264,128]{1,0:T(8,128)S(1)}, f32[264,128]{1,0:T(8,128)S(1)}, u32[]{:S(2)}, u32[]{:S(2)}) %collective-permute-start.21) | collective-permute-done | bytes 135200 | tf_op jit(solution)/shard_map/ppermute | solution.py:282
  178.2 3.4 %all-to-all-start.3 = ((f32[8,80,128]{2,1,0:T(8,128)}), f32[8,80,128]{2,1,0:T(8,128)S(1)}, u32[]{:S(2)}, u32[]{:S(2)}) async-start(f32[8,80,128]{2,1,0:T(8,128)} %shard_map.80), calls=%async_computation.3 | async-start | bytes 655360 | tf_op jit(solution)/shard_map/all_to_all | solution.py:46
  182.3 10.5 %all-to-all-done.3.parts = f32[8,80,128]{2,1,0:T(8,128)S(1)} async-done(((f32[8,80,128]{2,1,0:T(8,128)}), f32[8,80,128]{2,1,0:T(8,128)S(1)}, u32[]{:S(2)}, u32[]{:S(2)}) %all-to-all-start.3) | async-done | bytes 327712 | tf_op jit(solution)/shard_map/all_to_all | solution.py:46
  (68 shorter events, 26.7 us)
Async XLA Ops:
  0.6 6.6 %collective-permute-start.2 = (bf16[128,128]{1,0:T(8,128)(2,1)}, bf16[128,128]{1,0:T(8,128)(2,1)S(1)}, u32[]{:S(2)}, u32[]{:S(2)}) collective-permute-start(bf16[128,128]{1,0:T(8,128)(2,1)} %bitcast.26), channel_id=1, source_target_pairs={{0,3},{1,0},{2,1},{3,2},{4,7},{5,4},{6,5},{7,6},{8,11},{9,8},{10,9... | collective-permute-start | bytes 98312 | tf_op jit(solution)/shard_map/ppermute | solution.py:298
  5.3 5.0 %collective-permute-start.1 = (bf16[128,128]{1,0:T(8,128)(2,1)}, bf16[128,128]{1,0:T(8,128)(2,1)S(1)}, u32[]{:S(2)}, u32[]{:S(2)}) collective-permute-start(bf16[128,128]{1,0:T(8,128)(2,1)} %bitcast.27), channel_id=1, source_target_pairs={{0,2},{1,3},{2,0},{3,1},{4,6},{5,7},{6,4},{7,5},{8,10},{9,11},{10,... | collective-permute-start | bytes 98312 | tf_op jit(solution)/shard_map/ppermute | solution.py:298
  5.3 5.9 %collective-permute-start = (bf16[128,128]{1,0:T(8,128)(2,1)}, bf16[128,128]{1,0:T(8,128)(2,1)S(1)}, u32[]{:S(2)}, u32[]{:S(2)}) collective-permute-start(bf16[128,128]{1,0:T(8,128)(2,1)} %bitcast.28), channel_id=1, source_target_pairs={{0,1},{1,2},{2,3},{3,0},{4,5},{5,6},{6,7},{7,4},{8,9},{9,10},{10,1... | collective-permute-start | bytes 98312 | tf_op jit(solution)/shard_map/ppermute | solution.py:298
  58.0 64.3 %collective-permute-start.5 = (bf16[1187,256]{1,0:T(8,128)(2,1)S(1)}, bf16[1187,256]{1,0:T(8,128)(2,1)}, u32[]{:S(2)}, u32[]{:S(2)}) collective-permute-start(bf16[1187,256]{1,0:T(8,128)(2,1)S(1)} %shard_map.68), channel_id=1, source_target_pairs={{0,128},{1,129},{2,130},{3,131},{4,132},{5,133},{6,134},{7,135},{8... | collective-permute-start | bytes 1823240 | tf_op jit(solution)/shard_map/ppermute | solution.py:313
  71.6 50.7 %collective-permute-start.6 = (bf16[1187,256]{1,0:T(8,128)(2,1)S(1)}, bf16[1187,256]{1,0:T(8,128)(2,1)S(1)}, u32[]{:S(2)}, u32[]{:S(2)}) collective-permute-start(bf16[1187,256]{1,0:T(8,128)(2,1)S(1)} %shard_map.69), channel_id=1, source_target_pairs={{0,128},{1,129},{2,130},{3,131},{4,132},{5,133},{6,134},{7,135},{8... | collective-permute-start | bytes 1823240 | tf_op jit(solution)/shard_map/ppermute | solution.py:313
  76.0 11.2 %all-to-all-start.1 = ((f32[16,3,512]{2,1,0:T(4,128)}), f32[16,3,512]{2,1,0:T(4,128)S(1)}, u32[]{:S(2)}, u32[]{:S(2)}) async-start(f32[16,3,512]{2,1,0:T(4,128)} %shard_map.70), calls=%async_computation.1 | async-start | bytes 262144 | tf_op jit(solution)/shard_map/all_to_all | solution.py:46
  87.8 34.5 %all-to-all-start.2 = ((f32[8,3,512]{2,1,0:T(4,128)}), f32[8,3,512]{2,1,0:T(4,128)S(1)}, u32[]{:S(2)}, u32[]{:S(2)}) async-start(f32[8,3,512]{2,1,0:T(4,128)} %shard_map.71), calls=%async_computation.2 | async-start | bytes 131072 | tf_op jit(solution)/shard_map/all_to_all | solution.py:46
  134.0 4.3 %collective-permute-start.7 = (f32[16,264,128]{2,1,0:T(8,128)S(1)}, f32[16,264,128]{2,1,0:T(8,128)S(1)}, u32[]{:S(2)}, u32[]{:S(2)}) collective-permute-start(f32[16,264,128]{2,1,0:T(8,128)S(1)} %get-tuple-element.66), channel_id=1, source_target_pairs={{0,4},{4,0},{1,5},{5,1},{2,6},{6,2},{3,7},{7,3},{8,12},{12,8},{9,1... | collective-permute-start | bytes 6488072 | tf_op jit(solution)/shard_map/ppermute | solution.py:42
  134.1 7.3 %collective-permute-start.15 = (f32[16,264,128]{2,1,0:T(8,128)S(1)}, f32[16,264,128]{2,1,0:T(8,128)S(1)}, u32[]{:S(2)}, u32[]{:S(2)}) collective-permute-start(f32[16,264,128]{2,1,0:T(8,128)S(1)} %get-tuple-element.79), channel_id=1, source_target_pairs={{0,4},{4,0},{1,5},{5,1},{2,6},{6,2},{3,7},{7,3},{8,12},{12,8},{9,1... | collective-permute-start | bytes 6488072 | tf_op jit(solution)/shard_map/ppermute | solution.py:42
  139.1 8.7 %collective-permute-start.8 = (f32[520,128]{1,0:T(8,128)S(1)}, f32[520,128]{1,0:T(8,128)S(1)}, u32[]{:S(2)}, u32[]{:S(2)}) collective-permute-start(f32[520,128]{1,0:T(8,128)S(1)} %get-tuple-element.70), channel_id=1, source_target_pairs={{0,8},{8,16},{16,24},{24,0},{1,9},{9,17},{17,25},{25,1},{2,10},{10... | collective-permute-start | bytes 798728 | tf_op jit(solution)/shard_map/ppermute | solution.py:282
  139.7 8.1 %collective-permute-start.9 = (f32[512,128]{1,0:T(8,128)S(1)}, f32[512,128]{1,0:T(8,128)S(1)}, u32[]{:S(2)}, u32[]{:S(2)}) collective-permute-start(f32[512,128]{1,0:T(8,128)S(1)} %get-tuple-element.71), channel_id=1, source_target_pairs={{0,24},{8,0},{16,8},{24,16},{1,25},{9,1},{17,9},{25,17},{2,26},{10... | collective-permute-start | bytes 786440 | tf_op jit(solution)/shard_map/ppermute | solution.py:282
  142.2 9.7 %collective-permute-start.16 = (f32[520,128]{1,0:T(8,128)S(1)}, f32[520,128]{1,0:T(8,128)S(1)}, u32[]{:S(2)}, u32[]{:S(2)}) collective-permute-start(f32[520,128]{1,0:T(8,128)S(1)} %get-tuple-element.83), channel_id=1, source_target_pairs={{0,32},{32,64},{64,96},{96,0},{1,33},{33,65},{65,97},{97,1},{2,34}... | collective-permute-start | bytes 798728 | tf_op jit(solution)/shard_map/ppermute | solution.py:282
  142.3 8.8 %collective-permute-start.17 = (f32[512,128]{1,0:T(8,128)S(1)}, f32[512,128]{1,0:T(8,128)S(1)}, u32[]{:S(2)}, u32[]{:S(2)}) collective-permute-start(f32[512,128]{1,0:T(8,128)S(1)} %get-tuple-element.84), channel_id=1, source_target_pairs={{0,96},{32,0},{64,32},{96,64},{1,97},{33,1},{65,33},{97,65},{2,98}... | collective-permute-start | bytes 786440 | tf_op jit(solution)/shard_map/ppermute | solution.py:282
  147.8 15.8 %collective-permute-start.10 = (f32[1040,128]{1,0:T(8,128)S(1)}, f32[1040,128]{1,0:T(8,128)S(1)}, u32[]{:S(2)}, u32[]{:S(2)}) collective-permute-start(f32[1040,128]{1,0:T(8,128)S(1)} %get-tuple-element.72), channel_id=1, source_target_pairs={{0,8},{8,16},{16,24},{24,0},{1,9},{9,17},{17,25},{25,1},{2,10},{10... | collective-permute-start | bytes 1597448 | tf_op jit(solution)/shard_map/ppermute | solution.py:282
  149.7 13.8 %collective-permute-start.11 = (f32[1032,128]{1,0:T(8,128)S(1)}, f32[1032,128]{1,0:T(8,128)S(1)}, u32[]{:S(2)}, u32[]{:S(2)}) collective-permute-start(f32[1032,128]{1,0:T(8,128)S(1)} %get-tuple-element.73), channel_id=1, source_target_pairs={{0,24},{8,0},{16,8},{24,16},{1,25},{9,1},{17,9},{25,17},{2,26},{10... | collective-permute-start | bytes 1585160 | tf_op jit(solution)/shard_map/ppermute | solution.py:282
  152.0 16.3 %collective-permute-start.18 = (f32[1040,128]{1,0:T(8,128)S(1)}, f32[1040,128]{1,0:T(8,128)S(1)}, u32[]{:S(2)}, u32[]{:S(2)}) collective-permute-start(f32[1040,128]{1,0:T(8,128)S(1)} %get-tuple-element.85), channel_id=1, source_target_pairs={{0,32},{32,64},{64,96},{96,0},{1,33},{33,65},{65,97},{97,1},{2,34}... | collective-permute-start | bytes 1597448 | tf_op jit(solution)/shard_map/ppermute | solution.py:282
  152.4 16.0 %collective-permute-start.19 = (f32[1032,128]{1,0:T(8,128)S(1)}, f32[1032,128]{1,0:T(8,128)S(1)}, u32[]{:S(2)}, u32[]{:S(2)}) collective-permute-start(f32[1032,128]{1,0:T(8,128)S(1)} %get-tuple-element.86), channel_id=1, source_target_pairs={{0,96},{32,0},{64,32},{96,64},{1,97},{33,1},{65,33},{97,65},{2,98}... | collective-permute-start | bytes 1585160 | tf_op jit(solution)/shard_map/ppermute | solution.py:282
  163.7 7.7 %collective-permute-start.12 = (f32[264,128]{1,0:T(8,128)S(1)}, f32[264,128]{1,0:T(8,128)S(1)}, u32[]{:S(2)}, u32[]{:S(2)}) collective-permute-start(f32[264,128]{1,0:T(8,128)S(1)} %get-tuple-element.75), channel_id=1, source_target_pairs={{0,32},{32,64},{64,96},{96,0},{1,33},{33,65},{65,97},{97,1},{2,34}... | collective-permute-start | bytes 405512 | tf_op jit(solution)/shard_map/ppermute | solution.py:282
  163.8 9.6 %collective-permute-start.13 = (f32[264,128]{1,0:T(8,128)S(1)}, f32[264,128]{1,0:T(8,128)S(1)}, u32[]{:S(2)}, u32[]{:S(2)}) collective-permute-start(f32[264,128]{1,0:T(8,128)S(1)} %get-tuple-element.76), channel_id=1, source_target_pairs={{0,64},{32,96},{64,0},{96,32},{1,65},{33,97},{65,1},{97,33},{2,66}... | collective-permute-start | bytes 405512 | tf_op jit(solution)/shard_map/ppermute | solution.py:282
  166.1 7.3 %collective-permute-start.14 = (f32[264,128]{1,0:T(8,128)S(1)}, f32[264,128]{1,0:T(8,128)S(1)}, u32[]{:S(2)}, u32[]{:S(2)}) collective-permute-start(f32[264,128]{1,0:T(8,128)S(1)} %get-tuple-element.77), channel_id=1, source_target_pairs={{0,96},{32,0},{64,32},{96,64},{1,97},{33,1},{65,33},{97,65},{2,98}... | collective-permute-start | bytes 405512 | tf_op jit(solution)/shard_map/ppermute | solution.py:282
  168.5 5.4 %collective-permute-start.20 = (f32[264,128]{1,0:T(8,128)S(1)}, f32[264,128]{1,0:T(8,128)S(1)}, u32[]{:S(2)}, u32[]{:S(2)}) collective-permute-start(f32[264,128]{1,0:T(8,128)S(1)} %get-tuple-element.88), channel_id=1, source_target_pairs={{0,8},{8,16},{16,24},{24,0},{1,9},{9,17},{17,25},{25,1},{2,10},{10... | collective-permute-start | bytes 405512 | tf_op jit(solution)/shard_map/ppermute | solution.py:282
  169.5 6.6 %collective-permute-start.21 = (f32[264,128]{1,0:T(8,128)S(1)}, f32[264,128]{1,0:T(8,128)S(1)}, u32[]{:S(2)}, u32[]{:S(2)}) collective-permute-start(f32[264,128]{1,0:T(8,128)S(1)} %get-tuple-element.89), channel_id=1, source_target_pairs={{0,16},{8,24},{16,0},{24,8},{1,17},{9,25},{17,1},{25,9},{2,18},{10... | collective-permute-start | bytes 405512 | tf_op jit(solution)/shard_map/ppermute | solution.py:282
  171.4 6.0 %collective-permute-start.22 = (f32[264,128]{1,0:T(8,128)S(1)}, f32[264,128]{1,0:T(8,128)S(1)}, u32[]{:S(2)}, u32[]{:S(2)}) collective-permute-start(f32[264,128]{1,0:T(8,128)S(1)} %get-tuple-element.90), channel_id=1, source_target_pairs={{0,24},{8,0},{16,8},{24,16},{1,25},{9,1},{17,9},{25,17},{2,26},{10... | collective-permute-start | bytes 405512 | tf_op jit(solution)/shard_map/ppermute | solution.py:282
  178.2 14.5 %all-to-all-start.3 = ((f32[8,80,128]{2,1,0:T(8,128)}), f32[8,80,128]{2,1,0:T(8,128)S(1)}, u32[]{:S(2)}, u32[]{:S(2)}) async-start(f32[8,80,128]{2,1,0:T(8,128)} %shard_map.80), calls=%async_computation.3 | async-start | bytes 655360 | tf_op jit(solution)/shard_map/all_to_all | solution.py:46
  (5 other events, 47.8 us)
